TPU v7x, 256 devices: a whole 4x4x8 slice. The times are simulated.
256 devices in a mesh: sub: 128 (over y, z, x), mode: 2 (over core).
Axes of the slice: x: 4, y: 4, z: 8, core: 2. Of those that a mesh axis runs over, the one named last changes fastest.
Arguments:
- coupling: bfloat16 [8192, 64, 128], P('sub'), may hold values from -0.5 to 0.5
- coupling_pairs: int32 [8192, 2], P('sub'), may hold values from 0 to 3, as said below
- modes: bfloat16 [8192, 256, 256], P('sub', None, 'mode'), may hold values from -6 to 6
- mode_weights: bfloat16 [8192, 256], P('sub', 'mode'), may hold values from 0 to 1, as said below
- parent_of: int32 [8192, 1], P('sub'), may hold values from 0 to 127; in each aligned block of 64 rows (0 to 63, 64 to 127, ...) at most 2 rows name the same one
- row_block: int32 [8192], P('sub'), may hold values from 0 to 7
- parent_modes: bfloat16 [128, 512, 256], P('sub'), may hold values from -1 to 1
- parent_eigs: float32 [128, 256], P('sub'), may hold values from 0.02 to 0.5
Outputs:
- strengths: float32 [8192, 256], P('sub', 'mode')
Inputs may be any that keep to these rules, and one draw needn't show every extreme that they name: `coupling_pairs`: within each child the 2 block indices are distinct. `parent_of`: the 64 children of one index of sub name any one parent at most 2 times; some parent is named exactly 2 times by some index's children. `mode_weights`: Positive.
All inputs are finite; a program needn't handle non-finite values.
Results may differ from a plain program's by a relative error of at most 0.0015.
Values may be sent and summed in bfloat16 or wider, within the bound.
No kernel may reach another device: no remote copies, remote signals or barrier semaphores. Data moves between devices by JAX's collectives and lax.ppermute only.
A program may use at most 128 MiB of HBM per device.

v0:
```python
import jax
import jax.numpy as jnp
from jax import lax
from jax.sharding import PartitionSpec as P

M = 256
MP = 256
BLK = 64
CH_DEV = 64


def pick_blocks(modes, coupling_pairs):
    child_count, interface_rows, mode_cols = modes.shape
    blocks = modes.reshape(child_count, interface_rows // BLK, BLK, mode_cols)
    selector = (
        coupling_pairs[:, :, None]
        == jnp.arange(interface_rows // BLK, dtype=jnp.int32)[None, None, :]
    ).astype(jnp.bfloat16)
    picked = jnp.einsum(
        "skb,sbim->skim", selector, blocks, preferred_element_type=jnp.float32
    ).astype(jnp.bfloat16)
    return picked.reshape(child_count, coupling_pairs.shape[1] * BLK, mode_cols)


def weighted_records(coupling_rows, picked, weights):
    record = jnp.einsum("sij,sjm->sim", coupling_rows, picked, preferred_element_type=jnp.float32)
    return (record * weights[:, None, :].astype(jnp.float32)).astype(jnp.bfloat16)


def to_slots(values, slot_index, slot_count):
    empty = jnp.zeros((slot_count,) + values.shape[1:], values.dtype)
    return empty.at[slot_index].set(values)


def per_device(
    coupling, coupling_pairs, modes, mode_weights, parent_of, row_block, parent_modes, parent_eigs
):
    sub_count = lax.axis_size("sub")
    child_count = coupling.shape[0]
    mode_cols = modes.shape[2]
    capacity = max(2, 2 * child_count // sub_count)
    slot_count = sub_count * capacity
    owner = parent_of[:, 0]
    order_ids = jnp.arange(child_count, dtype=jnp.int32)
    earlier = (owner[:, None] == owner[None, :]) & (order_ids[None, :] < order_ids[:, None])
    position = jnp.sum(earlier.astype(jnp.int32), axis=1)
    slot_index = owner * capacity + position
    picked = pick_blocks(modes, coupling_pairs)
    row_send = to_slots(row_block, slot_index, slot_count).reshape(sub_count, capacity)
    record = weighted_records(coupling, picked, mode_weights)
    record_send = to_slots(record, slot_index, slot_count).reshape(
        sub_count, capacity, BLK, mode_cols
    )
    record_recv, row_recv = (
        lax.all_to_all(record_send, "sub", split_axis=0, concat_axis=0, tiled=True),
        lax.all_to_all(row_send, "sub", split_axis=0, concat_axis=0, tiled=True),
    )
    records = record_recv.reshape(slot_count, BLK, mode_cols)
    row_index = row_recv.reshape(slot_count)
    sep_blocks = parent_modes.shape[1] // BLK
    parent_blocks = parent_modes[0].reshape(sep_blocks, BLK, MP)
    group_size = min(64, slot_count)
    group_count = slot_count // group_size
    record_groups = records.reshape(group_count, group_size, BLK, mode_cols)
    row_groups = row_index.reshape(group_count, group_size)

    def project(gram_sum, members):
        record_part, row_part = members
        selector = (row_part[:, None] == jnp.arange(sep_blocks, dtype=jnp.int32)[None, :]).astype(
            jnp.bfloat16
        )
        parent_rows = jnp.einsum(
            "sb,bik->sik", selector, parent_blocks, preferred_element_type=jnp.float32
        ).astype(jnp.bfloat16)
        projected = jnp.einsum(
            "sik,sim->skm", parent_rows, record_part, preferred_element_type=jnp.float32
        ).astype(jnp.bfloat16)
        term = jnp.einsum("skm,slm->kl", projected, projected, preferred_element_type=jnp.float32)
        return (gram_sum + term, projected)

    gram_sum, projected_all = lax.scan(
        project, jnp.zeros((MP, MP), jnp.float32), (record_groups, row_groups)
    )
    gram_sum = lax.psum(gram_sum, "mode")
    pencil = jnp.diag(parent_eigs[0]) + gram_sum / (CH_DEV * M)
    factor = jnp.linalg.cholesky(pencil)
    identity = jnp.eye(MP, dtype=pencil.dtype)
    inverse = lax.linalg.triangular_solve(factor, identity, left_side=True, lower=True).astype(
        jnp.bfloat16
    )

    def strength(projected):
        rotated = jnp.einsum("kl,slm->skm", inverse, projected, preferred_element_type=jnp.float32)
        return jnp.sum(rotated * rotated, axis=1) / MP

    slot_values = lax.map(strength, projected_all).reshape(sub_count, capacity, mode_cols)
    returned = lax.all_to_all(slot_values, "sub", split_axis=0, concat_axis=0, tiled=True)
    return returned.reshape(slot_count, mode_cols)[slot_index]


def solution(mesh):
    in_specs = (
        P("sub", None, None),
        P("sub", None),
        P("sub", None, "mode"),
        P("sub", "mode"),
        P("sub", None),
        P("sub"),
        P("sub", None, None),
        P("sub", None),
    )
    out_specs = P("sub", "mode")
    return jax.shard_map(
        per_device, mesh=mesh, in_specs=in_specs, out_specs=out_specs, check_vma=False
    )
```

profile of v0, /device:TPU:1, one launch (start us, length us, event | category | flops | bytes accessed | tf_op | source)
XLA Modules:
  0.0 348.5 jit_solution(17957443767118149357)
XLA Ops:
  6.5 0.9 convert_reduce_fusion
  7.5 0.7 fusion.31
  8.1 0.9 scatter_custom_fusion
  9.1 0.8 all_to_all.12
  9.8 16.3 %all-to-all-start = ((s32[128,1,2]{2,1,0:T(1,128)}), s32[128,1,2]{2,1,0:T(1,128)S(1)}, u32[]{:S(2)}, u32[]{:S(2)}) async-start(s32[128,1,2]{2,1,0:T(1,128)} %bitcast.6), calls=%async_computation | async-start | bytes 131072 | tf_op jit(solution)/shard_map/all_to_all | solution.py:56
  26.2 0.8 copy.57
  26.9 5.6 %fusion.15 = bf16[64,2,64,128]{3,1,2,0:T(2,128)(2,1)S(1)} fusion(bf16[64,4,64,128]{3,2,1,0:T(8,128)(2,1)} %bitcast.112, s32[64,2]{1,0:T(8,128)S(1)} %copy.57), kind=kOutput, calls=%fused_computation.27 | convolution fusion | flops 9437696 | bytes 6291968 | tf_op jit(solution)/shard_map/skb,sbim->skim/dot_general | solution.py:19
  33.3 0.7 fusion.18
  33.9 3.0 broadcast_in_dim.55
  37.0 8.1 %scatter_fusion = bf16[256,64,128]{2,1,0:T(8,128)(2,1)} fusion(bf16[256,64,128]{2,1,0:T(8,128)(2,1)} %broadcast_in_dim.55, s32[64]{0:T(128)S(1)} %fusion.31, bf16[64,64,128]{2,1,0:T(8,128)(2,1)S(1)} %fusion.18), kind=kCustom, calls=%fused_computation.2 | custom fusion | bytes 3145984 | tf_op jit(solution)/shard_map/scatter | solution.py:32
  45.1 13.9 %all-to-all-start.1 = ((bf16[128,2,64,128]{3,2,1,0:T(8,128)(2,1)}), bf16[128,2,64,128]{3,2,1,0:T(8,128)(2,1)}, u32[]{:S(2)}, u32[]{:S(2)}) async-start(bf16[128,2,64,128]{3,2,1,0:T(8,128)(2,1)} %bitcast.106), calls=%async_computation.1 | async-start | bytes 8388608 | tf_op jit(solution)/shard_map/all_to_all | solution.py:55
  59.9 0.7 reduce.16
  60.8 90.8 %all-to-all-done.1 = bf16[128,2,64,128]{3,2,1,0:T(8,128)(2,1)} async-done(((bf16[128,2,64,128]{3,2,1,0:T(8,128)(2,1)}), bf16[128,2,64,128]{3,2,1,0:T(8,128)(2,1)}, u32[]{:S(2)}, u32[]{:S(2)}) %all-to-all-start.1) | async-done | bytes 4194336 | tf_op jit(solution)/shard_map/all_to_all | solution.py:55
  151.5 50.3 %while.26 = (s32[]{:T(128)}, f32[256,256]{1,0:T(8,128)S(1)}, bf16[4,64,256,128]{3,2,1,0:T(8,128)(2,1)}, s32[4,64]{1,0:T(4,128)S(1)}, bf16[8,64,256]{2,0,1:T(8,12...) while((s32[]{:T(128)}, f32[256,256]{1,0:T(8,128)S(1)}, ...), condition=%wide.region_4.5_spmd.clone, body=%wide.region_3.4_spmd.clone.sunk | while | flops 1362231808 | bytes 18614116 | solution.py:81
  151.6 0.8 convolution_convert_fusion.4
  152.3 6.9 %bitcast_dynamic-update-slice_fusion.8 = (bf16[4,64,256,128]{3,2,1,0:T(8,128)(2,1)}, bf16[64,256,128]{2,1,0:T(8,128)(2,1)}) fusion(bf16[4,64,256,128]{3,2,1,0:T(8,128)(2,1)} %get-tuple-element.287, s32[]{:T(128)} %get-tuple-element.285, bf16[4,64,64,128]{3,2,1,0:T(8,128)(2,1)} %get-tuple-element.298, ...), kind=kOutput, calls=%fused_computation.11.clone.1 | convolution fusion | flops 270532608 | bytes 11535360 | tf_op jit(solution)/shard_map/while/body/eval_jaxpr/sik,sim->skm/dot_general | solution.py:75
  159.2 4.8 %fusion.62 = f32[256,256]{1,0:T(8,128)S(1)} fusion(bf16[64,256,128]{2,1,0:T(8,128)(2,1)} %get-tuple-element.275, f32[256,256]{1,0:T(8,128)S(1)} %get-tuple-element.286, pred[]{:T(512)S(6)} %compare.26), kind=kOutput, calls=%fused_computation.16.clone.1 | convolution fusion | flops 1073872896 | bytes 4718593 | tf_op jit(solution)/shard_map/while/body/eval_jaxpr/skm,slm->kl/dot_general | solution.py:78
  164.1 0.8 convolution_convert_fusion.4
  164.8 7.1 %bitcast_dynamic-update-slice_fusion.8 = (bf16[4,64,256,128]{3,2,1,0:T(8,128)(2,1)}, bf16[64,256,128]{2,1,0:T(8,128)(2,1)}) fusion(bf16[4,64,256,128]{3,2,1,0:T(8,128)(2,1)} %get-tuple-element.287, s32[]{:T(128)} %get-tuple-element.285, bf16[4,64,64,128]{3,2,1,0:T(8,128)(2,1)} %get-tuple-element.298, ...), kind=kOutput, calls=%fused_computation.11.clone.1 | convolution fusion | flops 270532608 | bytes 11535360 | tf_op jit(solution)/shard_map/while/body/eval_jaxpr/sik,sim->skm/dot_general | solution.py:75
  171.9 4.8 %fusion.62 = f32[256,256]{1,0:T(8,128)S(1)} fusion(bf16[64,256,128]{2,1,0:T(8,128)(2,1)} %get-tuple-element.275, f32[256,256]{1,0:T(8,128)S(1)} %get-tuple-element.286, pred[]{:T(512)S(6)} %compare.26), kind=kOutput, calls=%fused_computation.16.clone.1 | convolution fusion | flops 1073872896 | bytes 4718593 | tf_op jit(solution)/shard_map/while/body/eval_jaxpr/skm,slm->kl/dot_general | solution.py:78
  176.7 0.8 convolution_convert_fusion.4
  177.5 7.0 %bitcast_dynamic-update-slice_fusion.8 = (bf16[4,64,256,128]{3,2,1,0:T(8,128)(2,1)}, bf16[64,256,128]{2,1,0:T(8,128)(2,1)}) fusion(bf16[4,64,256,128]{3,2,1,0:T(8,128)(2,1)} %get-tuple-element.287, s32[]{:T(128)} %get-tuple-element.285, bf16[4,64,64,128]{3,2,1,0:T(8,128)(2,1)} %get-tuple-element.298, ...), kind=kOutput, calls=%fused_computation.11.clone.1 | convolution fusion | flops 270532608 | bytes 11535360 | tf_op jit(solution)/shard_map/while/body/eval_jaxpr/sik,sim->skm/dot_general | solution.py:75
  184.5 4.8 %fusion.62 = f32[256,256]{1,0:T(8,128)S(1)} fusion(bf16[64,256,128]{2,1,0:T(8,128)(2,1)} %get-tuple-element.275, f32[256,256]{1,0:T(8,128)S(1)} %get-tuple-element.286, pred[]{:T(512)S(6)} %compare.26), kind=kOutput, calls=%fused_computation.16.clone.1 | convolution fusion | flops 1073872896 | bytes 4718593 | tf_op jit(solution)/shard_map/while/body/eval_jaxpr/skm,slm->kl/dot_general | solution.py:78
  189.3 0.7 convolution_convert_fusion.4
  190.1 7.0 %bitcast_dynamic-update-slice_fusion.8 = (bf16[4,64,256,128]{3,2,1,0:T(8,128)(2,1)}, bf16[64,256,128]{2,1,0:T(8,128)(2,1)}) fusion(bf16[4,64,256,128]{3,2,1,0:T(8,128)(2,1)} %get-tuple-element.287, s32[]{:T(128)} %get-tuple-element.285, bf16[4,64,64,128]{3,2,1,0:T(8,128)(2,1)} %get-tuple-element.298, ...), kind=kOutput, calls=%fused_computation.11.clone.1 | convolution fusion | flops 270532608 | bytes 11535360 | tf_op jit(solution)/shard_map/while/body/eval_jaxpr/sik,sim->skm/dot_general | solution.py:75
  197.0 4.8 %fusion.62 = f32[256,256]{1,0:T(8,128)S(1)} fusion(bf16[64,256,128]{2,1,0:T(8,128)(2,1)} %get-tuple-element.275, f32[256,256]{1,0:T(8,128)S(1)} %get-tuple-element.286, pred[]{:T(512)S(6)} %compare.26), kind=kOutput, calls=%fused_computation.16.clone.1 | convolution fusion | flops 1073872896 | bytes 4718593 | tf_op jit(solution)/shard_map/while/body/eval_jaxpr/skm,slm->kl/dot_general | solution.py:78
  201.8 0.8 copy.61
  202.8 28.9 %all-reduce.3.cloned.1.call-done = f32[256,256]{0,1:T(8,128)} async-done(((f32[256,256]{0,1:T(8,128)}), f32[256,256]{0,1:T(8,128)}) %all-reduce.3.cloned.1.call-update) | async-done | bytes 262160 | tf_op jit(solution)/shard_map/psum | solution.py:84
  231.7 1.0 multiply_add_fusion
  232.8 1.0 fusion.19
  233.8 11.7 %cholesky.49 = f32[128,128]{1,0:T(8,128)S(1)} custom-call(f32[128,128]{1,0:T(8,128)S(1)} %cholesky.115), custom_call_target="Cholesky" | custom-call | tf_op jit(solution)/shard_map/jit(cholesky)/cholesky | solution.py:86
  245.6 9.8 %custom-call.14 = f32[1,128,128]{1,2,0:T(8,128)S(1)} custom-call(f32[1,128,128]{2,1,0:T(8,128)S(1)} %get-tuple-element.177), custom_call_target="InvertDiagBlocksLowerTriangular" | custom-call | tf_op jit(solution)/shard_map/jit(cholesky)/cholesky | solution.py:86
  255.9 11.7 %cholesky.103 = f32[128,128]{1,0:T(8,128)S(1)} custom-call(f32[128,128]{1,0:T(8,128)S(1)} %convolution_subtract_fusion.1), custom_call_target="Cholesky" | custom-call | tf_op jit(solution)/shard_map/jit(cholesky)/cholesky | solution.py:86
  267.9 0.7 compare_reduce_fusion
  270.1 4.1 %while.25 = (s32[]{:T(128)}, f32[256,256]{0,1:T(8,128)S(1)}, s32[2,2]{1,0:T(2,128)S(1)}, f32[2,128,128]{2,1,0:T(8,128)S(1)}, s32[]{:T(128)}) while((s32[]{:T(128)}, f32[256,256]{0,1:T(8,128)S(1)}, s32[2,2]{1,0:T(2,128)S(1)}, f32[2,128,128]{2,1,0:T(8,128)S(1)}, s32[]{:T(128)}) %tuple.70), condition=%wide.while_cond, body=%wide.while_body.sunk | while | flops 2 | bytes 393321 | solution.py:88
  270.7 1.3 dynamic-slice.7
  272.8 1.3 dynamic-slice.7
  274.2 19.9 %custom-call.15 = f32[2,128,128]{1,2,0:T(8,128)S(1)} custom-call(f32[2,128,128]{2,1,0:T(8,128)S(1)} %get-tuple-element.70), custom_call_target="InvertDiagBlocksLowerTriangular" | custom-call | tf_op jit(solution)/shard_map/triangular_solve | solution.py:88
  295.1 20.9 %while.24 = (s32[]{:T(128)}, f32[4,64,128]{2,1,0:T(8,128)}, bf16[4,64,256,128]{3,2,1,0:T(8,128)(2,1)}, bf16[256,256]{1,0:T(8,128)(2,1)S(1)}, s32[]{:T(128)}) while((s32[]{:T(128)}, f32[4,64,128]{2,1,0:T(8,128)}, bf16[4,64,256,128]{3,2,1,0:T(8,128)(2,1)}, bf16[256,256]{1,0:T(8,128)(2,1)S(1)}, s32[]{:T(128)}) %tuple.73), condition=%wide.region_12.13_spmd, body=%wide.region_10.12_spmd.sunk | while | flops 1077936128 | bytes 4424765 | solution.py:96
  295.1 4.6 %multiply_reduce_fusion.2 = f32[64,128]{1,0:T(8,128)S(1)} fusion(bf16[4,64,256,128]{3,2,1,0:T(8,128)(2,1)} %get-tuple-element.328, s32[]{:T(128)} %get-tuple-element.321, bf16[256,256]{1,0:T(8,128)(2,1)S(1)} %get-tuple-element.329), kind=kOutput, calls=%fused_computation.3.clone.1 | convolution fusion | flops 1077927936 | bytes 4358656 | tf_op jit(solution)/shard_map/while/body/eval_jaxpr/kl,slm->skm/dot_general | solution.py:93
  300.4 4.6 %multiply_reduce_fusion.2 = f32[64,128]{1,0:T(8,128)S(1)} fusion(bf16[4,64,256,128]{3,2,1,0:T(8,128)(2,1)} %get-tuple-element.328, s32[]{:T(128)} %get-tuple-element.321, bf16[256,256]{1,0:T(8,128)(2,1)S(1)} %get-tuple-element.329), kind=kOutput, calls=%fused_computation.3.clone.1 | convolution fusion | flops 1077927936 | bytes 4358656 | tf_op jit(solution)/shard_map/while/body/eval_jaxpr/kl,slm->skm/dot_general | solution.py:93
  305.0 0.6 bitcast_dynamic-update-slice_fusion.6
  305.6 4.6 %multiply_reduce_fusion.2 = f32[64,128]{1,0:T(8,128)S(1)} fusion(bf16[4,64,256,128]{3,2,1,0:T(8,128)(2,1)} %get-tuple-element.328, s32[]{:T(128)} %get-tuple-element.321, bf16[256,256]{1,0:T(8,128)(2,1)S(1)} %get-tuple-element.329), kind=kOutput, calls=%fused_computation.3.clone.1 | convolution fusion | flops 1077927936 | bytes 4358656 | tf_op jit(solution)/shard_map/while/body/eval_jaxpr/kl,slm->skm/dot_general | solution.py:93
  310.8 4.6 %multiply_reduce_fusion.2 = f32[64,128]{1,0:T(8,128)S(1)} fusion(bf16[4,64,256,128]{3,2,1,0:T(8,128)(2,1)} %get-tuple-element.328, s32[]{:T(128)} %get-tuple-element.321, bf16[256,256]{1,0:T(8,128)(2,1)S(1)} %get-tuple-element.329), kind=kOutput, calls=%fused_computation.3.clone.1 | convolution fusion | flops 1077927936 | bytes 4358656 | tf_op jit(solution)/shard_map/while/body/eval_jaxpr/kl,slm->skm/dot_general | solution.py:93
  315.5 0.6 bitcast_dynamic-update-slice_fusion.6
  316.1 13.6 %all-to-all-start.2 = ((f32[128,2,128]{2,1,0:T(2,128)}), f32[128,2,128]{2,1,0:T(2,128)S(1)}, u32[]{:S(2)}, u32[]{:S(2)}) async-start(f32[128,2,128]{2,1,0:T(2,128)} %bitcast.21), calls=%async_computation.2 | async-start | bytes 262144 | tf_op jit(solution)/shard_map/all_to_all | solution.py:97
  329.7 10.8 %all-to-all-done.2 = f32[128,2,128]{2,1,0:T(2,128)S(1)} async-done(((f32[128,2,128]{2,1,0:T(2,128)}), f32[128,2,128]{2,1,0:T(2,128)S(1)}, u32[]{:S(2)}, u32[]{:S(2)}) %all-to-all-start.2) | async-done | bytes 131104 | tf_op jit(solution)/shard_map/all_to_all | solution.py:97
  340.4 1.2 gather_fusion
  (55 shorter events, 6.5 us)
Async XLA Ops:
  6.5 26.7 %copy-start = (bf16[64,64,128]{2,1,0:T(8,128)(2,1)S(1)}, bf16[64,64,128]{2,1,0:T(8,128)(2,1)}, u32[]{:S(2)}) copy-start(bf16[64,64,128]{2,1,0:T(8,128)(2,1)} %param.12) | copy-start | bytes 3145732
  9.8 35.3 %all-to-all-start = ((s32[128,1,2]{2,1,0:T(1,128)}), s32[128,1,2]{2,1,0:T(1,128)S(1)}, u32[]{:S(2)}, u32[]{:S(2)}) async-start(s32[128,1,2]{2,1,0:T(1,128)} %bitcast.6), calls=%async_computation | async-start | bytes 131072 | tf_op jit(solution)/shard_map/all_to_all | solution.py:56
  32.5 0.7 copy-start.2
  45.1 14.1 %copy-start.1 = (bf16[1,512,256]{2,1,0:T(8,128)(2,1)S(1)}, bf16[1,512,256]{2,1,0:T(8,128)(2,1)}, u32[]{:S(2)}) copy-start(bf16[1,512,256]{2,1,0:T(8,128)(2,1)} %param.18) | copy-start | bytes 786436
  45.1 106.4 %all-to-all-start.1 = ((bf16[128,2,64,128]{3,2,1,0:T(8,128)(2,1)}), bf16[128,2,64,128]{3,2,1,0:T(8,128)(2,1)}, u32[]{:S(2)}, u32[]{:S(2)}) async-start(bf16[128,2,64,128]{3,2,1,0:T(8,128)(2,1)} %bitcast.106), calls=%async_computation.1 | async-start | bytes 8388608 | tf_op jit(solution)/shard_map/all_to_all | solution.py:55
  59.0 172.7 %all-reduce.3.cloned.1.call-start = ((), (), s32[]{:S(2)}) async-start(), calls=%async_computation.3 | async-start | bytes 524288 | tf_op jit(solution)/shard_map/psum | solution.py:84
  151.5 80.2 %copy-start.3 = (f32[1,256]{1,0:T(1,128)S(1)}, f32[1,256]{1,0:T(1,128)}, u32[]{:S(2)}) copy-start(f32[1,256]{1,0:T(1,128)} %param.19) | copy-start | bytes 3076
  316.1 24.4 %all-to-all-start.2 = ((f32[128,2,128]{2,1,0:T(2,128)}), f32[128,2,128]{2,1,0:T(2,128)S(1)}, u32[]{:S(2)}, u32[]{:S(2)}) async-start(f32[128,2,128]{2,1,0:T(2,128)} %bitcast.21), calls=%async_computation.2 | async-start | bytes 262144 | tf_op jit(solution)/shard_map/all_to_all | solution.py:97
Sparse Core Ops, SparseCore 0:
  202.8 28.8 all-reduce.2
where the time goes:
time: 350 us; the launch traced here: 348 us
  waiting for transfers between devices  131 us (37%)
  matrix products  76.3 us (22%)
  other arithmetic  60.8 us (17%)
  starting transfers between devices  44 us (13%)
  local copies, waits for them, and re-layouts  21.7 us (6%)
  between operations  14.9 us (4%)
    all_to_all x1, waiting for transfers between devices, per_device(): lax.all_to_all(record_send, 'sub', split_axis=0, concat_axis=0, tiled=True)  90.8 us
    another operation x6, other arithmetic, per_device(): factor = jnp.linalg.cholesky(pencil)  34 us
    psum x1, waiting for transfers between devices, per_device(): gram_sum = lax.psum(gram_sum, 'mode')  28.9 us
    dot_general x4, matrix products, project(): jnp.einsum('sik,sim->skm', parent_rows, record_part, preferred_element_ty...  28 us
    another operation x4, other arithmetic, per_device(): lax.linalg.triangular_solve(factor, identity, left_side=True, lower=True)  19.9 us
    dot_general x4, matrix products, project(): jnp.einsum('skm,slm->kl', projected, projected, preferred_element_type=jn...  19.2 us
    dot_general x4, matrix products, strength(): jnp.einsum('kl,slm->skm', inverse, projected, preferred_element_type=jnp....  18.5 us
    all_to_all x1, starting transfers between devices, per_device(): lax.all_to_all(row_send, 'sub', split_axis=0, concat_axis=0, tiled=True)  16.3 us
  transfers between devices with their start and end apart: 4, of which 3 were waited for; matrix products, arithmetic and copies ran while one was open for 6% of the time, Pallas kernels for 0%

commit v1 on v0

v1 whole, which is shorter than its diff:
```python
import jax
import jax.numpy as jnp
from jax import lax
from jax.experimental import pallas as pl
from jax.experimental.pallas import tpu as pltpu
from jax.sharding import Mesh, PartitionSpec as P

MP = 256
BLK = 64
HALF = 32
SB = 8
CHILDREN_DEV = 64
CB = 16
STEPS = CHILDREN_DEV // CB
NY, NZ, NX = 4, 8, 4
NG = NY * NX
SLOTS = 2 * NZ
ROWS = 9 * SLOTS
ZROWS = 80
PB = 32
BF = jnp.bfloat16
F32 = jnp.float32
VMEM = pl.BlockSpec(memory_space=pltpu.VMEM)
SMEM = pl.BlockSpec(memory_space=pltpu.SMEM)


def params(mib, **more):
    return pltpu.CompilerParams(vmem_limit_bytes=mib * 1024 * 1024, **more)


def dot(a, b):
    return jnp.dot(a, b, preferred_element_type=F32)


def dot_nt(a, b):
    return lax.dot_general(a, b, (((1,), (1,)), ((), ())), preferred_element_type=F32)


def dot_tn(a, b):
    return lax.dot_general(a, b, (((0,), (0,)), ((), ())), preferred_element_type=F32)


def four(x):
    return jnp.concatenate([x, x, x, x], axis=0)


def tile_index():
    row = lax.broadcasted_iota(jnp.int32, (HALF, 128), 0)
    lane = lax.broadcasted_iota(jnp.int32, (HALF, 128), 1)
    return row, lane % HALF, (lane // HALF) == (row // 8)


def pack(x):
    lane = lax.broadcasted_iota(jnp.int32, (8, 128), 1)
    low = jnp.where(lane < 32, x[0:8], x[8:16])
    high = jnp.where(lane < 96, x[16:24], x[24:32])
    return jnp.where(lane < 64, low, high)


def moments_kernel(core_ref, pairs_ref, coupling_ref, modes_ref, weights_ref, record_ref, own_ref, other_ref):
    step = pl.program_id(0)
    row, col, _ = tile_index()
    lower = row >= col
    diagonal = row == col
    first = core_ref[0] == 0
    for j in range(CB):
        c = step * CB + j
        top = modes_ref[j, pl.ds(pl.multiple_of(pairs_ref[c, 0] * BLK, BLK), BLK), :]
        bottom = modes_ref[j, pl.ds(pl.multiple_of(pairs_ref[c, 1] * BLK, BLK), BLK), :]
        picked = jnp.concatenate([top, bottom], axis=0)
        record = dot(coupling_ref[j], picked)
        record = (record * weights_ref[j : j + 1, :].astype(F32)).astype(BF)
        record_ref[j] = record
        u = dot_nt(record, four(record[:HALF]))
        v = dot_nt(record[HALF:], four(record[HALF:]))
        cross = pack(u[HALF:])
        triangle = pack(jnp.where(lower, u[:HALF], v))
        diag = jnp.sum(jnp.where(diagonal, v, 0.0), axis=0, keepdims=True)
        own_ref[0, j * 8 : j * 8 + 8, :] = jnp.where(first, cross, triangle)
        other_ref[0, j * 8 : j * 8 + 8, :] = jnp.where(first, triangle, cross)
        own_ref[0, CB * 8 + j : CB * 8 + j + 1, :] = diag
        other_ref[0, CB * 8 + j : CB * 8 + j + 1, :] = diag


def moments(core, pairs, coupling, modes, weights):
    block = CB * 8 + CB
    return pl.pallas_call(
        moments_kernel,
        grid=(STEPS,),
        in_specs=[
            SMEM,
            SMEM,
            pl.BlockSpec((CB, BLK, 128), lambda i: (i, 0, 0)),
            pl.BlockSpec((CB, 256, 128), lambda i: (i, 0, 0)),
            pl.BlockSpec((CB, 128), lambda i: (i, 0)),
        ],
        out_specs=[
            pl.BlockSpec((CB, BLK, 128), lambda i: (i, 0, 0)),
            pl.BlockSpec((1, block, 128), lambda i: (i, 0, 0)),
            pl.BlockSpec((1, block, 128), lambda i: (i, 0, 0)),
        ],
        out_shape=[
            jax.ShapeDtypeStruct((CHILDREN_DEV, BLK, 128), BF),
            jax.ShapeDtypeStruct((STEPS, block, 128), F32),
            jax.ShapeDtypeStruct((STEPS, block, 128), F32),
        ],
        compiler_params=params(32),
        name="child_moments",
    )(core, pairs, coupling, modes, weights)


def slot_of(parent_ref, count_ref, c):
    p = parent_ref[c]
    k = count_ref[p]
    count_ref[p] = k + 1
    group = (p // (NZ * NX)) * NX + p % NX
    slot = ((p // NX) % NZ) * 2 + k
    return group, slot


def clear_counts(count_ref):
    for p in range(NG * NZ):
        count_ref[p] = 0


def dispatch_kernel(parent_ref, block_ref, own_ref, recv_ref, out_ref, buf_ref, count_ref):
    clear_counts(count_ref)
    lane = lax.broadcasted_iota(jnp.int32, (1, 128), 1)
    lane16 = lax.broadcasted_iota(jnp.int32, (SLOTS, 128), 1)
    empty = jnp.where(lane16 < 64, -1000.0, 0.0)
    for g in range(NG):
        buf_ref[g, 0 : 8 * SLOTS, :] = jnp.zeros((8 * SLOTS, 128), F32)
        buf_ref[g, 8 * SLOTS : ROWS, :] = empty
    for c in range(CHILDREN_DEV):
        group, slot = slot_of(parent_ref, count_ref, c)
        s, j = c // CB, c % CB
        buf_ref[group, pl.ds(slot, 8, stride=SLOTS), :] = (
            own_ref[s, j * 8 : j * 8 + 8, :] + recv_ref[s, j * 8 : j * 8 + 8, :]
        )
        r = CB * 8 + j
        diag = own_ref[s, r : r + 1, :] + recv_ref[s, r : r + 1, :]
        block = block_ref[c].astype(F32)
        buf_ref[group, pl.ds(8 * SLOTS + slot, 1), :] = jnp.where(lane < 64, block, diag)
    for g in range(NG):
        out_ref[g] = buf_ref[g].astype(BF)


def dispatch(parent, block, own, recv):
    return pl.pallas_call(
        dispatch_kernel,
        in_specs=[SMEM, SMEM, VMEM, VMEM],
        out_specs=VMEM,
        out_shape=jax.ShapeDtypeStruct((NG, ROWS, 128), BF),
        scratch_shapes=[pltpu.VMEM((NG, ROWS, 128), F32), pltpu.SMEM((NG * NZ,), jnp.int32)],
        compiler_params=params(32),
        name="dispatch",
    )(parent, block, own, recv)


def bin_kernel(recv_ref, out_ref, onehot_ref):
    count = NG * SLOTS
    meta = recv_ref[:, 8 * SLOTS : ROWS, :].astype(F32).reshape(count, 128)
    slot = lax.broadcasted_iota(jnp.int32, (count, 128), 0) % SLOTS
    lane = lax.broadcasted_iota(jnp.int32, (count, 128), 1)
    target = meta + (SB * (slot // 2)).astype(F32)
    onehot = jnp.where((lane < 64) & (target == lane.astype(F32)), 1.0, 0.0).astype(BF)
    onehot_ref[...] = onehot
    values = jnp.concatenate(
        [recv_ref[:, i * SLOTS : (i + 1) * SLOTS, :].reshape(count, 128) for i in range(9)], axis=1
    )
    bins = dot_tn(onehot, values)
    zero = jnp.zeros((8, 128), F32)
    for z in range(NZ):
        rows = [bins[8 * z : 8 * z + 8, 128 * i : 128 * (i + 1)] for i in range(9)] + [zero]
        out_ref[z] = jnp.concatenate(rows, axis=0).astype(BF)


def bin_slots(recv):
    return pl.pallas_call(
        bin_kernel,
        in_specs=[VMEM],
        out_specs=[VMEM, VMEM],
        out_shape=[
            jax.ShapeDtypeStruct((NZ, ZROWS, 128), BF),
            jax.ShapeDtypeStruct((NG * SLOTS, 128), BF),
        ],
        compiler_params=params(32),
        name="bin_slots",
    )(recv)


def sum_kernel(recv_ref, out_ref):
    total = recv_ref[0].astype(F32)
    for z in range(1, NZ):
        total = total + recv_ref[z].astype(F32)
    out_ref[...] = total


def sum_bins(recv):
    return pl.pallas_call(
        sum_kernel,
        in_specs=[VMEM],
        out_specs=VMEM,
        out_shape=jax.ShapeDtypeStruct((ZROWS, 128), F32),
        name="sum_bins",
    )(recv)


def invert(a_ref):
    lane = lax.broadcasted_iota(jnp.int32, (PB, MP), 1)
    row = lax.broadcasted_iota(jnp.int32, (PB, MP), 0)
    lane_all = lax.broadcasted_iota(jnp.int32, (MP, MP), 1)
    for b in range(MP // PB):
        r = b * PB
        panel = a_ref[r : r + PB, :]
        for j in range(PB):
            k = r + j
            col = panel[:, k : k + 1]
            inv = 1.0 / panel[j : j + 1, k : k + 1]
            pivot = jnp.where(lane[:1] == k, 1.0, panel[j : j + 1, :])
            scaled = pivot * inv
            panel = jnp.where(row == j, scaled, jnp.where(lane == k, 0.0, panel) - col * scaled)
        cols = a_ref[:, r : r + PB]
        update = jnp.dot(cols, panel, preferred_element_type=F32, precision=lax.Precision.HIGHEST)
        a_ref[...] = jnp.where((lane_all // PB) == b, 0.0, a_ref[...]) - update
        a_ref[r : r + PB, :] = panel


def split(x):
    high = x.astype(BF)
    return high, (x - high.astype(F32)).astype(BF)


def pencil_kernel(core_ref, own_ref, other_ref, q_ref, eigs_ref, out_ref, a_ref, y_ref, pack_ref):
    row, col, same = tile_index()
    first = core_ref[0] == 0
    lane8 = lax.broadcasted_iota(jnp.int32, (8, 128), 1)
    diags = jnp.where(first, other_ref[64:72, :], own_ref[64:72, :])
    diags = jnp.where(lane8 < 64, pltpu.roll(diags, 64, 1), diags)
    zero = jnp.zeros((HALF, 128), F32)
    for b in range(SB):
        own = own_ref[pl.ds(b, 8, stride=8), :]
        other = other_ref[pl.ds(b, 8, stride=8), :]
        cross = jnp.where(same, four(jnp.where(first, own, other)), 0.0)
        triangle = jnp.where(same, four(jnp.where(first, other, own)), 0.0)
        n11 = jnp.where(row > col, triangle, jnp.where(row == col, 0.5 * triangle, 0.0))
        half = jnp.where(same & (row == col), 0.5 * diags[b : b + 1, :], 0.0)
        n22 = jnp.where(row < col, triangle, half)
        lhs = jnp.concatenate(
            [jnp.concatenate([n11, zero], axis=1), jnp.concatenate([cross, n22], axis=1)], axis=0
        ).astype(BF)
        q1 = q_ref[b * BLK : b * BLK + HALF, :]
        q2 = q_ref[b * BLK + HALF : (b + 1) * BLK, :]
        y_ref[b * BLK : (b + 1) * BLK, :] = dot(lhs, jnp.concatenate([four(q1), four(q2)], axis=0)).astype(BF)
    x = dot_tn(q_ref[...], y_ref[...])
    r = lax.broadcasted_iota(jnp.int32, (MP, MP), 0)
    c = lax.broadcasted_iota(jnp.int32, (MP, MP), 1)
    a_ref[...] = (x + x.T) * (1.0 / 16384.0) + jnp.where(r == c, eigs_ref[...], 0.0)
    invert(a_ref)
    high, low = split(a_ref[...] * (1.0 / MP))
    q = q_ref[...]
    y_high, y_low = split(dot(q, high) + dot(q, low))
    for b in range(SB):
        s = b * BLK
        qb = q_ref[s : s + BLK, :]
        u = dot_nt(qb, four(y_high[s : s + HALF])) + dot_nt(qb, four(y_low[s : s + HALF]))
        v = dot_nt(qb[HALF:], four(y_high[s + HALF : s + BLK])) + dot_nt(
            qb[HALF:], four(y_low[s + HALF : s + BLK])
        )
        cross = pack(2.0 * u[HALF:])
        triangle = pack(
            jnp.where(row > col, 2.0 * u[:HALF], jnp.where(row == col, u[:HALF], 2.0 * v))
        )
        pack_ref[pl.ds(b, 8, stride=8), :] = jnp.where(first, cross, triangle)
        pack_ref[64 + b : 65 + b, :] = jnp.sum(jnp.where(row == col, v, 0.0), axis=0, keepdims=True)
    pack_ref[72:80, :] = jnp.zeros((8, 128), F32)
    result = pack_ref[...].astype(BF)
    for z in range(NZ):
        out_ref[z] = result


def pencil_blocks(core, own, other, q, eigs):
    return pl.pallas_call(
        pencil_kernel,
        in_specs=[SMEM, VMEM, VMEM, VMEM, VMEM],
        out_specs=VMEM,
        out_shape=jax.ShapeDtypeStruct((NZ, ZROWS, 128), BF),
        scratch_shapes=[
            pltpu.VMEM((MP, MP), F32),
            pltpu.VMEM((SB * BLK, MP), BF),
            pltpu.VMEM((ZROWS, 128), F32),
        ],
        compiler_params=params(32),
        name="pencil_blocks",
    )(core, own, other, q, eigs)


def select_kernel(bins_ref, onehot_ref, out_ref):
    onehot = onehot_ref[:, 0:64]
    bins = [bins_ref[z].astype(F32) for z in range(NZ)]
    for i in range(9):
        values = jnp.concatenate([x[8 * i : 8 * i + 8] for x in bins], axis=0).astype(BF)
        picked = dot(onehot, values).astype(BF)
        out_ref[:, i * SLOTS : (i + 1) * SLOTS, :] = picked.reshape(NG, SLOTS, 128)


def select_bins(bins, onehot):
    return pl.pallas_call(
        select_kernel,
        in_specs=[VMEM, VMEM],
        out_specs=VMEM,
        out_shape=jax.ShapeDtypeStruct((NG, ROWS, 128), BF),
        compiler_params=params(32),
        name="select_bins",
    )(bins, onehot)


def collect_kernel(parent_ref, recv_ref, out_ref, buf_ref, count_ref):
    clear_counts(count_ref)
    for g in range(NG):
        buf_ref[g] = recv_ref[g].astype(F32)
    for c in range(CHILDREN_DEV):
        group, slot = slot_of(parent_ref, count_ref, c)
        s, j = c // CB, c % CB
        out_ref[s, j * 8 : j * 8 + 8, :] = buf_ref[group, pl.ds(slot, 8, stride=SLOTS), :]
        r = CB * 8 + j
        out_ref[s, r : r + 1, :] = buf_ref[group, pl.ds(8 * SLOTS + slot, 1), :]


def collect(parent, recv):
    return pl.pallas_call(
        collect_kernel,
        in_specs=[SMEM, VMEM],
        out_specs=VMEM,
        out_shape=jax.ShapeDtypeStruct((STEPS, CB * 9, 128), F32),
        scratch_shapes=[pltpu.VMEM((NG, ROWS, 128), F32), pltpu.SMEM((NG * NZ,), jnp.int32)],
        compiler_params=params(32),
        name="collect",
    )(parent, recv)


def strength_kernel(core_ref, own_ref, other_ref, record_ref, out_ref):
    row, col, same = tile_index()
    first = core_ref[0] == 0
    lower = same & (row >= col)
    upper = same & (row < col)
    diagonal = same & (row == col)
    zero = jnp.zeros((HALF, 128), F32)
    for j in range(CB):
        own = own_ref[0, j * 8 : j * 8 + 8, :]
        other = other_ref[0, j * 8 : j * 8 + 8, :]
        r = CB * 8 + j
        diag = jnp.where(first, other_ref[0, r : r + 1, :], own_ref[0, r : r + 1, :])
        cross = jnp.where(same, four(jnp.where(first, own, other)), 0.0)
        triangle = four(jnp.where(first, other, own))
        m11 = jnp.where(lower, triangle, 0.0)
        m22 = jnp.where(upper, triangle, jnp.where(diagonal, diag, 0.0))
        lhs = jnp.concatenate(
            [jnp.concatenate([m11, zero], axis=1), jnp.concatenate([cross, m22], axis=1)], axis=0
        ).astype(BF)
        record = record_ref[j]
        rhs = jnp.concatenate([four(record[:HALF]), four(record[HALF:])], axis=0)
        rotated = dot(lhs, rhs)
        out_ref[j : j + 1, :] = jnp.sum(rotated * record.astype(F32), axis=0, keepdims=True)


def strengths(core, own, other, record):
    block = CB * 9
    return pl.pallas_call(
        strength_kernel,
        grid=(STEPS,),
        in_specs=[
            SMEM,
            pl.BlockSpec((1, block, 128), lambda i: (i, 0, 0)),
            pl.BlockSpec((1, block, 128), lambda i: (i, 0, 0)),
            pl.BlockSpec((CB, BLK, 128), lambda i: (i, 0, 0)),
        ],
        out_specs=pl.BlockSpec((CB, 128), lambda i: (i, 0)),
        out_shape=jax.ShapeDtypeStruct((CHILDREN_DEV, 128), F32),
        compiler_params=params(32),
        name="strengths",
    )(core, own, other, record)


def swap(x):
    return lax.ppermute(x, "mode", [(0, 1), (1, 0)])


def exchange(x, axes):
    return lax.all_to_all(x, axes, split_axis=0, concat_axis=0, tiled=True)


def per_device(coupling, pairs, modes, weights, parent_of, row_block, parent_modes, parent_eigs):
    core = lax.axis_index("mode").astype(jnp.int32).reshape(1)
    parent = parent_of.reshape(CHILDREN_DEV)
    record, own, other = moments(core, pairs, coupling, modes, weights)
    sent = dispatch(parent, row_block, own, swap(other))
    binned, onehot = bin_slots(exchange(sent, ("y", "x")))
    total = sum_bins(exchange(binned, "z"))
    blocks = pencil_blocks(core, total, swap(total), parent_modes[0], parent_eigs)
    picked = select_bins(exchange(blocks, "z"), onehot)
    mine = collect(parent, exchange(picked, ("y", "x")))
    return strengths(core, mine, swap(mine), record)


def solution(mesh):
    grid = Mesh(mesh.devices.reshape(NY, NZ, NX, 2), ("y", "z", "x", "mode"))
    sub = ("y", "z", "x")
    in_specs = (
        P(sub, None, None),
        P(sub, None),
        P(sub, None, "mode"),
        P(sub, "mode"),
        P(sub, None),
        P(sub),
        P(sub, None, None),
        P(sub, None),
    )
    return jax.shard_map(
        per_device, mesh=grid, in_specs=in_specs, out_specs=P(sub, "mode"), check_vma=False
    )
```

time: 350 us -> 123 us (0.35)
  waiting for transfers between devices: 131 us -> 3.5 us
  matrix products: 76.3 us -> 0 us
  other arithmetic: 60.8 us -> 0 us
  blocking collectives: 0 us -> 57.7 us
  Pallas kernels: 0 us -> 46.5 us
  starting transfers between devices: 44 us -> 9.27 us
  local copies, waits for them, and re-layouts: 21.7 us -> 5.72 us
  between operations: 14.9 us -> 0.06 us
    all_to_all x3 -> x0, waiting for transfers between devices: 102 us -> none  [the longest x1 90.8 us: per_device(): lax.all_to_all(record_send, 'sub', split_axis=0, concat_axis=0, tiled=True)]
    dot_general x18 -> x0, matrix products: 74.9 us -> none  [the longest x4 28 us: project(): jnp.einsum('sik,sim->skm', parent_rows, record_part, preferred_element_ty...]
    all_to_all x0 -> x4, blocking collectives: none -> 57.7 us  [exchange(): return lax.all_to_all(x, axes, split_axis=0, concat_axis=0, tiled=True)]
    another operation x10 -> x0, other arithmetic: 54 us -> none  [the longest x6 34 us: per_device(): factor = jnp.linalg.cholesky(pencil)]
    pallas_call x0 -> x8, Pallas kernels: none -> 46.5 us  [the longest x1 26.8 us: pencil_blocks(): pl.pallas_call(pencil_kernel, in_specs=[SMEM, VMEM, VMEM, VMEM, VMEM], ou...]
    all_to_all x3 -> x0, starting transfers between devices: 43.8 us -> none  [the longest x1 16.3 us: per_device(): lax.all_to_all(row_send, 'sub', split_axis=0, concat_axis=0, tiled=True)]
    psum x1 -> x0, waiting for transfers between devices: 28.9 us -> none  [per_device(): gram_sum = lax.psum(gram_sum, 'mode')]
    ppermute x0 -> x3, starting transfers between devices: none -> 9.27 us  [swap(): return lax.ppermute(x, 'mode', [(0, 1), (1, 0)])]
  transfers between devices with their start and end apart: 4 -> 3, of which waited for: 3 -> 3; matrix products, arithmetic and copies ran while one was open for 6% -> 0% of each run, Pallas kernels for 0% -> 0%
where the time goes in v1:
time: 123 us
  blocking collectives  57.7 us (47%)
  Pallas kernels  46.5 us (38%)
  starting transfers between devices  9.27 us (8%)
  local copies, waits for them, and re-layouts  5.72 us (5%)
  waiting for transfers between devices  3.5 us (3%)
    all_to_all x4, blocking collectives, exchange(): return lax.all_to_all(x, axes, split_axis=0, concat_axis=0, tiled=True)  57.7 us
    pallas_call x1, Pallas kernels, pencil_blocks(): pl.pallas_call(pencil_kernel, in_specs=[SMEM, VMEM, VMEM, VMEM, VMEM], ou...  26.8 us
    pallas_call x1, Pallas kernels, moments(): pl.pallas_call(moments_kernel, grid=(STEPS,), in_specs=[SMEM, SMEM, pl.Bl...  12.4 us
    ppermute x3, starting transfers between devices, swap(): return lax.ppermute(x, 'mode', [(0, 1), (1, 0)])  9.27 us
    unnamed x17, local copies, waits for them, and re-layouts  5.72 us
    ppermute x3, waiting for transfers between devices, swap(): return lax.ppermute(x, 'mode', [(0, 1), (1, 0)])  3.5 us
  transfers between devices with their start and end apart: 3, of which 3 were waited for; matrix products, arithmetic and copies ran while one was open for 0% of the time, Pallas kernels for 0%

profile of v1, /device:TPU:1, one launch (start us, length us, event | category | flops | bytes accessed | tf_op | source)
XLA Modules:
  0.0 122.7 jit_solution(3451029362882479915)
XLA Ops:
  0.0 0.0 copy-start.7
  0.0 0.0 copy-start.5
  0.0 0.8 copy.9.pairs_ref
  0.8 0.0 copy-start
  0.8 2.2 %copy-done = bf16[64,256,128]{2,1,0:T(8,128)(2,1)S(1)} copy-done((bf16[64,256,128]{2,1,0:T(8,128)(2,1)S(1)}, bf16[64,256,128]{2,1,0:T(8,128)(2,1)}, u32[]{:S(2)}) %copy-start) | copy-done | bytes 4194328
  3.0 0.0 copy-start.1
  3.0 1.2 copy-done.1
  4.2 0.0 copy-start.4
  4.2 0.7 copy-done.4
  4.9 0.0 copy-start.2
  4.9 0.0 copy-start.6
  4.9 12.4 %child_moments.1 = (bf16[64,64,128]{2,1,0:T(8,128)(2,1)S(1)}, f32[4,144,128]{2,1,0:T(8,128)S(1)}, f32[4,144,128]{2,1,0:T(8,128)S(1)}) custom-call(s32[1]{0:T(128)} %bitcast.core_ref, s32[64,2]{1,0:T(8,128)S(1)} %copy.9.pairs_ref, bf16[64,64,128]{2,1,0:T(8,128)(2,1)S(1)} %copy-done.1, bf16[64,256,128]{2,1,0:T(8,128)(2,1)S(1)} %copy-done, ...), custom_call_target="tpu_custom_call" | custom-call | tf_op jit(solution)/shard_map/child_moments/pallas_call | solution.py:87
  17.3 3.3 %collective-permute-start = (f32[4,144,128]{2,1,0:T(8,128)S(1)}, f32[4,144,128]{2,1,0:T(8,128)S(1)}, u32[]{:S(2)}, u32[]{:S(2)}) collective-permute-start(f32[4,144,128]{2,1,0:T(8,128)S(1)} %get-tuple-element.11), channel_id=1, source_target_pairs={{0,1},{1,0},{2,3},{3,2},{4,5},{5,4},{6,7},{7,6},{8,9},{9,8},{10,11... | collective-permute-start | bytes 884744 | tf_op jit(solution)/shard_map/ppermute | solution.py:386
  20.6 1.2 collective-permute-done.recv_ref
  21.8 0.0 copy-done.7
  21.8 0.0 copy-done.5
  21.8 1.5 %dispatch.1 = bf16[16,144,128]{2,1,0:T(8,128)(2,1)S(1)} custom-call(s32[64]{0:T(128)S(1)} %bitcast.4, s32[64]{0:T(128)S(1)} %copy-done.7, f32[4,144,128]{2,1,0:T(8,128)S(1)} %get-tuple-element.10.own_ref, f32[4,144,128]{2,1,0:T(8,128)S(1)} %collective-permute-done.recv_ref), custom_call_target="tpu_custom_call" | custom-call | tf_op jit(solution)/shard_map/dispatch/pallas_call | solution.py:149
  23.4 16.2 %all_to_all.20.recv_ref = bf16[16,144,128]{2,1,0:T(8,128)(2,1)S(1)} all-to-all(bf16[16,144,128]{2,1,0:T(8,128)(2,1)S(1)} %dispatch.1), channel_id=1, replica_groups=mesh['y'=4,'z'=8,'x'=4,'mode'=2] {'y','x'}, dimensions={0} | all-to-all | bytes 1179648 | tf_op jit(solution)/shard_map/all_to_all | solution.py:390
  39.6 0.3 bin_slots.1
  40.0 16.5 %all_to_all.21.recv_ref = bf16[8,80,128]{2,1,0:T(8,128)(2,1)} all-to-all(bf16[8,80,128]{2,1,0:T(8,128)(2,1)S(1)} %get-tuple-element.12), channel_id=1, replica_groups=mesh['y'=4,'z'=8,'x'=4,'mode'=2] {'z'}, dimensions={0} | all-to-all | bytes 327680 | tf_op jit(solution)/shard_map/all_to_all | solution.py:390
  56.4 1.5 %sum_bins.1.own_ref = f32[80,128]{1,0:T(8,128)} custom-call(bf16[8,80,128]{2,1,0:T(8,128)(2,1)} %all_to_all.21.recv_ref), custom_call_target="tpu_custom_call" | custom-call | tf_op jit(solution)/shard_map/sum_bins/pallas_call | solution.py:200
  58.0 3.1 %collective-permute-start.1 = (f32[80,128]{1,0:T(8,128)}, f32[80,128]{1,0:T(8,128)S(1)}, u32[]{:S(2)}, u32[]{:S(2)}) collective-permute-start(f32[80,128]{1,0:T(8,128)} %sum_bins.1.own_ref), channel_id=1, source_target_pairs={{0,1},{1,0},{2,3},{3,2},{4,5},{5,4},{6,7},{7,6},{8,9},{9,8},{10,11... | collective-permute-start | bytes 122888 | tf_op jit(solution)/shard_map/ppermute | solution.py:386
  61.1 1.1 collective-permute-done.1.other_ref
  62.2 0.0 copy-done.2
  62.2 0.0 copy-done.6
  62.2 0.0 copy-start.3
  62.2 0.8 copy-done.3
  63.0 26.8 %pencil_blocks.1 = bf16[8,80,128]{2,1,0:T(8,128)(2,1)S(1)} custom-call(s32[1]{0:T(128)} %bitcast.core_ref, f32[80,128]{1,0:T(8,128)S(1)} %copy-done.3, f32[80,128]{1,0:T(8,128)S(1)} %collective-permute-done.1.other_ref, bf16[512,256]{1,0:T(8,128)(2,1)S(1)} %bitcast.3, f32[1,256]{1,0:T(1,128)S(1)} %copy-done.6), custom_call_target="tpu_custom_call" | custom-call | tf_op jit(solution)/shard_map/pencil_blocks/pallas_call | solution.py:283
  89.8 11.6 %all_to_all.22.bins_ref = bf16[8,80,128]{2,1,0:T(8,128)(2,1)S(1)} all-to-all(bf16[8,80,128]{2,1,0:T(8,128)(2,1)S(1)} %pencil_blocks.1), channel_id=1, replica_groups=mesh['y'=4,'z'=8,'x'=4,'mode'=2] {'z'}, dimensions={0} | all-to-all | bytes 327680 | tf_op jit(solution)/shard_map/all_to_all | solution.py:390
  101.4 0.3 select_bins.1
  101.7 13.4 %all_to_all.23.recv_ref = bf16[16,144,128]{2,1,0:T(8,128)(2,1)S(1)} all-to-all(bf16[16,144,128]{2,1,0:T(8,128)(2,1)S(1)} %select_bins.1), channel_id=1, replica_groups=mesh['y'=4,'z'=8,'x'=4,'mode'=2] {'y','x'}, dimensions={0} | all-to-all | bytes 1179648 | tf_op jit(solution)/shard_map/all_to_all | solution.py:390
  115.1 1.5 %collect.1.own_ref = f32[4,144,128]{2,1,0:T(8,128)S(1)} custom-call(s32[64]{0:T(128)S(1)} %bitcast.5, bf16[16,144,128]{2,1,0:T(8,128)(2,1)S(1)} %all_to_all.23.recv_ref), custom_call_target="tpu_custom_call" | custom-call | tf_op jit(solution)/shard_map/collect/pallas_call | solution.py:331
  116.5 2.8 %collective-permute-start.2 = (f32[4,144,128]{2,1,0:T(8,128)S(1)}, f32[4,144,128]{2,1,0:T(8,128)S(1)}, u32[]{:S(2)}, u32[]{:S(2)}) collective-permute-start(f32[4,144,128]{2,1,0:T(8,128)S(1)} %collect.1.own_ref), channel_id=1, source_target_pairs={{0,1},{1,0},{2,3},{3,2},{4,5},{5,4},{6,7},{7,6},{8,9},{9,8},{10,11... | collective-permute-start | bytes 884744 | tf_op jit(solution)/shard_map/ppermute | solution.py:386
  119.4 1.2 collective-permute-done.2.other_ref
  120.6 2.1 %strengths.1 = f32[64,128]{1,0:T(8,128)} custom-call(s32[1]{0:T(128)} %bitcast.core_ref, f32[4,144,128]{2,1,0:T(8,128)S(1)} %collect.1.own_ref, f32[4,144,128]{2,1,0:T(8,128)S(1)} %collective-permute-done.2.other_ref, bf16[64,64,128]{2,1,0:T(8,128)(2,1)S(1)} %get-tuple-element.14.record_ref), custom_call_target="tpu_custom_call" | custom-call | tf_op jit(solution)/shard_map/strengths/pallas_call | solution.py:369
Async XLA Ops:
  0.0 21.8 %copy-start.7 = (s32[64]{0:T(128)S(1)}, s32[64]{0:T(128)}, u32[]{:S(2)}) copy-start(s32[64]{0:T(128)} %block_ref.1) | copy-start | bytes 772
  0.0 21.8 %copy-start.5 = (s32[64,1]{0,1:T(1,128)S(1)}, s32[64,1]{0,1:T(1,128)}, u32[]{:S(2)}) copy-start(s32[64,1]{0,1:T(1,128)} %param.12) | copy-start | bytes 772
  0.8 2.2 %copy-start = (bf16[64,256,128]{2,1,0:T(8,128)(2,1)S(1)}, bf16[64,256,128]{2,1,0:T(8,128)(2,1)}, u32[]{:S(2)}) copy-start(bf16[64,256,128]{2,1,0:T(8,128)(2,1)} %modes_ref.1) | copy-start | bytes 12582916
  3.0 1.2 copy-start.1
  4.2 0.7 copy-start.4
  4.9 57.3 %copy-start.2 = (bf16[1,512,256]{2,1,0:T(8,128)(2,1)S(1)}, bf16[1,512,256]{2,1,0:T(8,128)(2,1)}, u32[]{:S(2)}) copy-start(bf16[1,512,256]{2,1,0:T(8,128)(2,1)} %param.14) | copy-start | bytes 786436
  4.9 57.3 %copy-start.6 = (f32[1,256]{1,0:T(1,128)S(1)}, f32[1,256]{1,0:T(1,128)}, u32[]{:S(2)}) copy-start(f32[1,256]{1,0:T(1,128)} %eigs_ref.1) | copy-start | bytes 3076
  17.3 4.5 %collective-permute-start = (f32[4,144,128]{2,1,0:T(8,128)S(1)}, f32[4,144,128]{2,1,0:T(8,128)S(1)}, u32[]{:S(2)}, u32[]{:S(2)}) collective-permute-start(f32[4,144,128]{2,1,0:T(8,128)S(1)} %get-tuple-element.11), channel_id=1, source_target_pairs={{0,1},{1,0},{2,3},{3,2},{4,5},{5,4},{6,7},{7,6},{8,9},{9,8},{10,11... | collective-permute-start | bytes 884744 | tf_op jit(solution)/shard_map/ppermute | solution.py:386
  58.0 4.2 %collective-permute-start.1 = (f32[80,128]{1,0:T(8,128)}, f32[80,128]{1,0:T(8,128)S(1)}, u32[]{:S(2)}, u32[]{:S(2)}) collective-permute-start(f32[80,128]{1,0:T(8,128)} %sum_bins.1.own_ref), channel_id=1, source_target_pairs={{0,1},{1,0},{2,3},{3,2},{4,5},{5,4},{6,7},{7,6},{8,9},{9,8},{10,11... | collective-permute-start | bytes 122888 | tf_op jit(solution)/shard_map/ppermute | solution.py:386
  62.2 0.8 copy-start.3
  116.5 4.0 %collective-permute-start.2 = (f32[4,144,128]{2,1,0:T(8,128)S(1)}, f32[4,144,128]{2,1,0:T(8,128)S(1)}, u32[]{:S(2)}, u32[]{:S(2)}) collective-permute-start(f32[4,144,128]{2,1,0:T(8,128)S(1)} %collect.1.own_ref), channel_id=1, source_target_pairs={{0,1},{1,0},{2,3},{3,2},{4,5},{5,4},{6,7},{7,6},{8,9},{9,8},{10,11... | collective-permute-start | bytes 884744 | tf_op jit(solution)/shard_map/ppermute | solution.py:386

commit v2 on v1

v2 whole, which is shorter than its diff:
```python
import jax
import jax.numpy as jnp
from jax import lax
from jax.experimental import pallas as pl
from jax.experimental.pallas import tpu as pltpu
from jax.sharding import Mesh, PartitionSpec as P

MP = 256
BLK = 64
HALF = 32
SB = 8
CHILDREN_DEV = 64
CB = 16
STEPS = CHILDREN_DEV // CB
NY, NZ, NX = 4, 8, 4
NG = NY * NX
SLOTS = 2 * NZ
ROWS = 9 * SLOTS
ZROWS = 80
PB = 32
BF = jnp.bfloat16
F32 = jnp.float32
VMEM = pl.BlockSpec(memory_space=pltpu.VMEM)
SMEM = pl.BlockSpec(memory_space=pltpu.SMEM)


def params(mib, **more):
    return pltpu.CompilerParams(vmem_limit_bytes=mib * 1024 * 1024, **more)


def dot(a, b):
    return jnp.dot(a, b, preferred_element_type=F32)


def dot_nt(a, b):
    return lax.dot_general(a, b, (((1,), (1,)), ((), ())), preferred_element_type=F32)


def dot_tn(a, b):
    return lax.dot_general(a, b, (((0,), (0,)), ((), ())), preferred_element_type=F32)


def four(x):
    return jnp.concatenate([x, x, x, x], axis=0)


def tile_index():
    row = lax.broadcasted_iota(jnp.int32, (HALF, 128), 0)
    lane = lax.broadcasted_iota(jnp.int32, (HALF, 128), 1)
    return row, lane % HALF, (lane // HALF) == (row // 8)


def pack(x):
    lane = lax.broadcasted_iota(jnp.int32, (8, 128), 1)
    low = jnp.where(lane < 32, x[0:8], x[8:16])
    high = jnp.where(lane < 96, x[16:24], x[24:32])
    return jnp.where(lane < 64, low, high)


def side_by_side(x):
    return jnp.concatenate([x[0:8], x[8:16], x[16:24], x[24:32]], axis=1)


def moments_kernel(
    core_ref, pairs_ref, parent_ref, block_ref, coupling_ref, modes_ref, weights_ref,
    record_ref, own_ref, other_ref, onehot_ref, count_ref,
):
    step = pl.program_id(0)
    row = lax.broadcasted_iota(jnp.int32, (HALF, HALF), 0)
    col = lax.broadcasted_iota(jnp.int32, (HALF, HALF), 1)
    lower = row >= col
    diagonal = lax.broadcasted_iota(jnp.int32, (HALF, BLK), 1) == (
        lax.broadcasted_iota(jnp.int32, (HALF, BLK), 0) + HALF
    )
    slots = lax.broadcasted_iota(jnp.int32, (1, NG * SLOTS), 1)
    first = core_ref[0] == 0

    @pl.when(step == 0)
    def _():
        for p in range(NG * NZ):
            count_ref[p] = 0

    for pair in range(CB // 2):
        records = []
        for j in (2 * pair, 2 * pair + 1):
            c = step * CB + j
            top = modes_ref[j, pl.ds(pl.multiple_of(pairs_ref[0, c] * BLK, BLK), BLK), :]
            bottom = modes_ref[j, pl.ds(pl.multiple_of(pairs_ref[1, c] * BLK, BLK), BLK), :]
            record = dot(coupling_ref[j], jnp.concatenate([top, bottom], axis=0))
            record = (record * weights_ref[j : j + 1, :].astype(F32)).astype(BF)
            record_ref[j] = record
            records.append(record)
        both = jnp.concatenate(records, axis=0)
        products = dot_nt(both, both)
        for i in range(2):
            c = step * CB + 2 * pair + i
            s = products[i * BLK : (i + 1) * BLK, i * BLK : (i + 1) * BLK]
            cross = side_by_side(s[HALF:, :HALF])
            triangle = side_by_side(jnp.where(lower, s[:HALF, :HALF], s[HALF:, HALF:]))
            own_ref[pl.ds(c, 8, stride=CHILDREN_DEV), :] = jnp.where(first, cross, triangle)
            other_ref[pl.ds(c, 8, stride=CHILDREN_DEV), :] = jnp.where(first, triangle, cross)
            diag = jnp.sum(jnp.where(diagonal, s[HALF:], 0.0), axis=0, keepdims=True)
            zero = jnp.zeros((1, BLK), F32)
            named = zero + (block_ref[c] + 1).astype(F32)
            own_ref[pl.ds(8 * CHILDREN_DEV + c, 1), :] = jnp.concatenate([diag, named], axis=1)
            other_ref[pl.ds(8 * CHILDREN_DEV + c, 1), :] = jnp.concatenate([diag, zero], axis=1)
            p = parent_ref[c]
            k = count_ref[p]
            count_ref[p] = k + 1
            group = (p // (NZ * NX)) * NX + p % NX
            slot = group * SLOTS + ((p // NX) % NZ) * 2 + k
            onehot_ref[pl.ds(c, 1), :] = jnp.where(slots == slot, 1.0, 0.0)


def moments(core, pairs, parent, block, coupling, modes, weights):
    whole = (9 * CHILDREN_DEV, 128)
    onehot = (CHILDREN_DEV, NG * SLOTS)
    return pl.pallas_call(
        moments_kernel,
        grid=(STEPS,),
        in_specs=[
            SMEM,
            SMEM,
            SMEM,
            SMEM,
            pl.BlockSpec((CB, BLK, 128), lambda i: (i, 0, 0)),
            pl.BlockSpec((CB, 256, 128), lambda i: (i, 0, 0)),
            pl.BlockSpec((CB, 128), lambda i: (i, 0)),
        ],
        out_specs=[
            pl.BlockSpec((CB, BLK, 128), lambda i: (i, 0, 0)),
            pl.BlockSpec(whole, lambda i: (0, 0)),
            pl.BlockSpec(whole, lambda i: (0, 0)),
            pl.BlockSpec(onehot, lambda i: (0, 0)),
        ],
        out_shape=[
            jax.ShapeDtypeStruct((CHILDREN_DEV, BLK, 128), BF),
            jax.ShapeDtypeStruct(whole, F32),
            jax.ShapeDtypeStruct(whole, F32),
            jax.ShapeDtypeStruct(onehot, F32),
        ],
        scratch_shapes=[pltpu.SMEM((NG * NZ,), jnp.int32)],
        compiler_params=params(60),
        name="child_moments",
    )(core, pairs, parent, block, coupling, modes, weights)


def dispatch_kernel(onehot_ref, own_ref, recv_ref, out_ref):
    place = onehot_ref[...].T.astype(BF)
    for i in range(9):
        rows = slice(i * CHILDREN_DEV, (i + 1) * CHILDREN_DEV)
        values = (own_ref[rows, :] + recv_ref[rows, :]).astype(BF)
        out_ref[:, i * SLOTS : (i + 1) * SLOTS, :] = dot(place, values).astype(BF).reshape(NG, SLOTS, 128)


def dispatch(onehot, own, recv):
    return pl.pallas_call(
        dispatch_kernel,
        in_specs=[VMEM, VMEM, VMEM],
        out_specs=VMEM,
        out_shape=jax.ShapeDtypeStruct((NG, ROWS, 128), BF),
        compiler_params=params(16),
        name="dispatch",
    )(onehot, own, recv)


def bin_kernel(recv_ref, out_ref, onehot_ref):
    count = NG * SLOTS
    meta = recv_ref[:, 8 * SLOTS : ROWS, :].astype(F32).reshape(count, 128)
    slot = lax.broadcasted_iota(jnp.int32, (count, 128), 0) % SLOTS
    lane = lax.broadcasted_iota(jnp.int32, (count, 128), 1)
    meta = pltpu.roll(meta, 64, 1)
    target = meta + (SB * (slot // 2) - 1).astype(F32)
    hit = (lane < 64) & (meta > 0.5) & (target == lane.astype(F32))
    onehot = jnp.where(hit, 1.0, 0.0).astype(BF)
    onehot_ref[...] = onehot
    values = jnp.concatenate(
        [recv_ref[:, i * SLOTS : (i + 1) * SLOTS, :].reshape(count, 128) for i in range(9)], axis=1
    )
    bins = dot_tn(onehot, values)
    zero = jnp.zeros((8, 128), F32)
    for z in range(NZ):
        rows = [bins[8 * z : 8 * z + 8, 128 * i : 128 * (i + 1)] for i in range(9)] + [zero]
        out_ref[z] = jnp.concatenate(rows, axis=0).astype(BF)


def bin_slots(recv):
    return pl.pallas_call(
        bin_kernel,
        in_specs=[VMEM],
        out_specs=[VMEM, VMEM],
        out_shape=[
            jax.ShapeDtypeStruct((NZ, ZROWS, 128), BF),
            jax.ShapeDtypeStruct((NG * SLOTS, 128), BF),
        ],
        compiler_params=params(16),
        name="bin_slots",
    )(recv)


def invert(a_ref):
    lane = lax.broadcasted_iota(jnp.int32, (PB, MP), 1)
    row = lax.broadcasted_iota(jnp.int32, (PB, MP), 0)
    lane_all = lax.broadcasted_iota(jnp.int32, (MP, MP), 1)
    line = lane[:1]

    def wide(x):
        return jnp.concatenate([x, x], axis=1)

    for b in range(MP // PB):
        r = b * PB
        panel = a_ref[r : r + PB, :]
        for j in range(0, PB, 4):
            k = r + j
            inside = (line >= k) & (line < k + 4)
            c = [jnp.broadcast_to(panel[:, k + i : k + i + 1], (PB, 128)) for i in range(4)]
            p = [
                jnp.where(line == k + i, 1.0, jnp.where(inside, 0.0, panel[j + i : j + i + 1]))
                for i in range(4)
            ]
            a00, a01, a11 = c[0][j : j + 1], c[1][j : j + 1], c[1][j + 1 : j + 2]
            a02, a12, a22 = c[2][j : j + 1], c[2][j + 1 : j + 2], c[2][j + 2 : j + 3]
            a03, a13, a23 = c[3][j : j + 1], c[3][j + 1 : j + 2], c[3][j + 2 : j + 3]
            a33 = c[3][j + 3 : j + 4]
            scale = 1.0 / (a00 * a11 - a01 * a01)
            p00, p01, p11 = a11 * scale, -a01 * scale, a00 * scale
            t00, t10 = p00 * a02 + p01 * a12, p01 * a02 + p11 * a12
            t01, t11 = p00 * a03 + p01 * a13, p01 * a03 + p11 * a13
            s00 = a22 - (a02 * t00 + a12 * t10)
            s01 = a23 - (a02 * t01 + a12 * t11)
            s11 = a33 - (a03 * t01 + a13 * t11)
            scale = 1.0 / (s00 * s11 - s01 * s01)
            q00, q01, q11 = s11 * scale, -s01 * scale, s00 * scale
            t00, t10, t01, t11 = wide(t00), wide(t10), wide(t01), wide(t11)
            p00, p01, p11 = wide(p00), wide(p01), wide(p11)
            q00, q01, q11 = wide(q00), wide(q01), wide(q11)
            u2 = p[2] - (t00 * p[0] + t10 * p[1])
            u3 = p[3] - (t01 * p[0] + t11 * p[1])
            x2, x3 = q00 * u2 + q01 * u3, q01 * u2 + q11 * u3
            x0 = (p00 * p[0] + p01 * p[1]) - (t00 * x2 + t01 * x3)
            x1 = (p01 * p[0] + p11 * p[1]) - (t10 * x2 + t11 * x3)
            c = [wide(v) for v in c]
            rest = jnp.where((lane >= k) & (lane < k + 4), 0.0, panel) - (
                (c[0] * x0 + c[1] * x1) + (c[2] * x2 + c[3] * x3)
            )
            low = jnp.where(row == j, x0, jnp.where(row == j + 1, x1, rest))
            panel = jnp.where(row == j + 2, x2, jnp.where(row == j + 3, x3, low))
        ch, cm, cl = split3(a_ref[:, r : r + PB])
        ph, pm, pw = split3(panel)
        update = dot(
            jnp.concatenate([ch, ch, cm, ch, cm, cl], axis=1),
            jnp.concatenate([ph, pm, ph, pw, pm, ph], axis=0),
        )
        a_ref[...] = jnp.where((lane_all // PB) == b, 0.0, a_ref[...]) - update
        a_ref[r : r + PB, :] = panel


def split3(x):
    high = x.astype(BF)
    rest = x - high.astype(F32)
    mid = rest.astype(BF)
    return high, mid, (rest - mid.astype(F32)).astype(BF)


def split(x):
    high = x.astype(BF)
    return high, (x - high.astype(F32)).astype(BF)


def pencil_kernel(
    core_ref, mine_ref, theirs_ref, q_ref, eigs_ref, out_ref, a_ref, y_ref, pack_ref, own_ref, other_ref
):
    for source, target in ((mine_ref, own_ref), (theirs_ref, other_ref)):
        parts = [source[z].astype(F32) for z in range(NZ)]
        while len(parts) > 1:
            parts = [x + y for x, y in zip(parts[::2], parts[1::2])]
        target[...] = parts[0]
    row, col, same = tile_index()
    first = core_ref[0] == 0
    lane8 = lax.broadcasted_iota(jnp.int32, (8, 128), 1)
    diags = jnp.where(first, other_ref[64:72, :], own_ref[64:72, :])
    diags = jnp.where((lane8 >= 32) & (lane8 < 64), diags, 0.0)
    diags = diags + pltpu.roll(diags, 32, 1)
    diags = diags + pltpu.roll(diags, 64, 1)
    zero = jnp.zeros((HALF, 128), F32)
    for b in range(SB):
        own = own_ref[pl.ds(b, 8, stride=8), :]
        other = other_ref[pl.ds(b, 8, stride=8), :]
        cross = jnp.where(same, four(jnp.where(first, own, other)), 0.0)
        triangle = jnp.where(same, four(jnp.where(first, other, own)), 0.0)
        n11 = jnp.where(row > col, triangle, jnp.where(row == col, 0.5 * triangle, 0.0))
        half = jnp.where(same & (row == col), 0.5 * diags[b : b + 1, :], 0.0)
        n22 = jnp.where(row < col, triangle, half)
        lhs = jnp.concatenate(
            [jnp.concatenate([n11, zero], axis=1), jnp.concatenate([cross, n22], axis=1)], axis=0
        ).astype(BF)
        q1 = q_ref[b * BLK : b * BLK + HALF, :]
        q2 = q_ref[b * BLK + HALF : (b + 1) * BLK, :]
        y_ref[b * BLK : (b + 1) * BLK, :] = dot(lhs, jnp.concatenate([four(q1), four(q2)], axis=0)).astype(BF)
    x = dot_tn(q_ref[...], y_ref[...])
    r = lax.broadcasted_iota(jnp.int32, (MP, MP), 0)
    c = lax.broadcasted_iota(jnp.int32, (MP, MP), 1)
    a_ref[...] = (x + x.T) * (1.0 / 16384.0) + jnp.where(r == c, eigs_ref[...], 0.0)
    invert(a_ref)
    high, low = split(a_ref[...] * (1.0 / MP))
    q = q_ref[...]
    y_high, y_low = split(dot(q, high) + dot(q, low))
    for b in range(SB):
        s = b * BLK
        qb = q_ref[s : s + BLK, :]
        u = dot_nt(qb, four(y_high[s : s + HALF])) + dot_nt(qb, four(y_low[s : s + HALF]))
        v = dot_nt(qb[HALF:], four(y_high[s + HALF : s + BLK])) + dot_nt(
            qb[HALF:], four(y_low[s + HALF : s + BLK])
        )
        cross = pack(2.0 * u[HALF:])
        triangle = pack(
            jnp.where(row > col, 2.0 * u[:HALF], jnp.where(row == col, u[:HALF], 2.0 * v))
        )
        pack_ref[pl.ds(b, 8, stride=8), :] = jnp.where(first, cross, triangle)
        pack_ref[64 + b : 65 + b, :] = jnp.sum(jnp.where(row == col, v, 0.0), axis=0, keepdims=True)
    pack_ref[72:80, :] = jnp.zeros((8, 128), F32)
    result = pack_ref[...].astype(BF)
    for z in range(NZ):
        out_ref[z] = result


def pencil_blocks(core, own, other, q, eigs):
    return pl.pallas_call(
        pencil_kernel,
        in_specs=[SMEM, VMEM, VMEM, VMEM, VMEM],
        out_specs=VMEM,
        out_shape=jax.ShapeDtypeStruct((NZ, ZROWS, 128), BF),
        scratch_shapes=[
            pltpu.VMEM((MP, MP), F32),
            pltpu.VMEM((SB * BLK, MP), BF),
            pltpu.VMEM((ZROWS, 128), F32),
            pltpu.VMEM((ZROWS, 128), F32),
            pltpu.VMEM((ZROWS, 128), F32),
        ],
        compiler_params=params(16),
        name="pencil_blocks",
    )(core, own, other, q, eigs)


def select_kernel(bins_ref, onehot_ref, out_ref):
    onehot = onehot_ref[:, 0:64]
    bins = [bins_ref[z].astype(F32) for z in range(NZ)]
    for i in range(9):
        values = jnp.concatenate([x[8 * i : 8 * i + 8] for x in bins], axis=0).astype(BF)
        picked = dot(onehot, values).astype(BF)
        out_ref[:, i * SLOTS : (i + 1) * SLOTS, :] = picked.reshape(NG, SLOTS, 128)


def select_bins(bins, onehot):
    return pl.pallas_call(
        select_kernel,
        in_specs=[VMEM, VMEM],
        out_specs=VMEM,
        out_shape=jax.ShapeDtypeStruct((NG, ROWS, 128), BF),
        compiler_params=params(16),
        name="select_bins",
    )(bins, onehot)


def collect_kernel(onehot_ref, recv_ref, out_ref):
    onehot = onehot_ref[...].astype(BF)
    for i in range(9):
        values = recv_ref[:, i * SLOTS : (i + 1) * SLOTS, :].reshape(NG * SLOTS, 128)
        out_ref[i * CHILDREN_DEV : (i + 1) * CHILDREN_DEV, :] = dot(onehot, values).astype(BF)


def collect(onehot, recv):
    return pl.pallas_call(
        collect_kernel,
        in_specs=[VMEM, VMEM],
        out_specs=VMEM,
        out_shape=jax.ShapeDtypeStruct((9 * CHILDREN_DEV, 128), BF),
        compiler_params=params(16),
        name="collect",
    )(onehot, recv)


def strength_kernel(core_ref, mine_ref, theirs_ref, record_ref, out_ref, own_ref, other_ref):
    step = pl.program_id(0)

    @pl.when(step == 0)
    def _():
        own_ref[...] = mine_ref[...].astype(F32)
        other_ref[...] = theirs_ref[...].astype(F32)

    row, col, same = tile_index()
    first = core_ref[0] == 0
    lower = same & (row >= col)
    upper = same & (row < col)
    diagonal = same & (row == col)
    zero = jnp.zeros((HALF, 128), F32)
    for j in range(CB):
        c = step * CB + j
        own = own_ref[pl.ds(c, 8, stride=CHILDREN_DEV), :]
        other = other_ref[pl.ds(c, 8, stride=CHILDREN_DEV), :]
        r = pl.ds(8 * CHILDREN_DEV + c, 1)
        diag = jnp.where(first, other_ref[r, :], own_ref[r, :])
        cross = jnp.where(same, four(jnp.where(first, own, other)), 0.0)
        triangle = four(jnp.where(first, other, own))
        m11 = jnp.where(lower, triangle, 0.0)
        m22 = jnp.where(upper, triangle, jnp.where(diagonal, diag, 0.0))
        lhs = jnp.concatenate(
            [jnp.concatenate([m11, zero], axis=1), jnp.concatenate([cross, m22], axis=1)], axis=0
        ).astype(BF)
        record = record_ref[j]
        rhs = jnp.concatenate([four(record[:HALF]), four(record[HALF:])], axis=0)
        rotated = dot(lhs, rhs)
        out_ref[j : j + 1, :] = jnp.sum(rotated * record.astype(F32), axis=0, keepdims=True)


def strengths(core, own, other, record):
    whole = (9 * CHILDREN_DEV, 128)
    return pl.pallas_call(
        strength_kernel,
        grid=(STEPS,),
        in_specs=[
            SMEM,
            pl.BlockSpec(whole, lambda i: (0, 0)),
            pl.BlockSpec(whole, lambda i: (0, 0)),
            pl.BlockSpec((CB, BLK, 128), lambda i: (i, 0, 0)),
        ],
        out_specs=pl.BlockSpec((CB, 128), lambda i: (i, 0)),
        out_shape=jax.ShapeDtypeStruct((CHILDREN_DEV, 128), F32),
        scratch_shapes=[pltpu.VMEM(whole, F32), pltpu.VMEM(whole, F32)],
        compiler_params=params(16),
        name="strengths",
    )(core, own, other, record)


def swap(x):
    return lax.ppermute(x, "mode", [(0, 1), (1, 0)])


def exchange(x, axes):
    return lax.all_to_all(x, axes, split_axis=0, concat_axis=0, tiled=True)


def per_device(coupling, pairs, modes, weights, parent_of, row_block, parent_modes, parent_eigs):
    core = lax.axis_index("mode").astype(jnp.int32).reshape(1)
    parent = parent_of.reshape(CHILDREN_DEV)
    record, own, other, onehot = moments(core, pairs.T, parent, row_block, coupling, modes, weights)
    sent = dispatch(onehot, own, swap(other))
    binned, chosen = bin_slots(exchange(sent, ("y", "x")))
    bins = exchange(binned, "z")
    blocks = pencil_blocks(core, bins, swap(bins), parent_modes[0], parent_eigs)
    picked = select_bins(exchange(blocks, "z"), chosen)
    mine = collect(onehot, exchange(picked, ("y", "x")))
    return strengths(core, mine, swap(mine), record)


def solution(mesh):
    grid = Mesh(mesh.devices.reshape(NY, NZ, NX, 2), ("y", "z", "x", "mode"))
    sub = ("y", "z", "x")
    in_specs = (
        P(sub, None, None),
        P(sub, None),
        P(sub, None, "mode"),
        P(sub, "mode"),
        P(sub, None),
        P(sub),
        P(sub, None, None),
        P(sub, None),
    )
    return jax.shard_map(
        per_device, mesh=grid, in_specs=in_specs, out_specs=P(sub, "mode"), check_vma=False
    )
```

time: 123 us -> 93.6 us (0.76)
  Pallas kernels: 46.5 us -> 21.1 us
  local copies, waits for them, and re-layouts: 5.72 us -> 1.82 us
    pallas_call x1, Pallas kernels: 26.8 us -> 11.5 us  [pencil_blocks(): pl.pallas_call(pencil_kernel, in_specs=[SMEM, VMEM, VMEM, VMEM, VMEM], ou...]
    pallas_call x4 -> x3, Pallas kernels: 16.9 us -> 6.74 us  [the longest x1 6.15 us: moments(): pl.pallas_call(moments_kernel, grid=(STEPS,), in_specs=[SMEM, SMEM, SMEM,...]
    unnamed x17 -> x12, local copies, waits for them, and re-layouts: 5.72 us -> 1.82 us
where the time goes in v2:
time: 93.6 us; the launch traced here: 93.2 us
  blocking collectives  57.5 us (61%)
  Pallas kernels  21.1 us (23%)
  starting transfers between devices  9.28 us (10%)
  waiting for transfers between devices  3.46 us (4%)
  local copies, waits for them, and re-layouts  1.82 us (2%)
    all_to_all x4, blocking collectives, exchange(): return lax.all_to_all(x, axes, split_axis=0, concat_axis=0, tiled=True)  57.5 us
    pallas_call x1, Pallas kernels, pencil_blocks(): pl.pallas_call(pencil_kernel, in_specs=[SMEM, VMEM, VMEM, VMEM, VMEM], ou...  11.5 us
    ppermute x3, starting transfers between devices, swap(): return lax.ppermute(x, 'mode', [(0, 1), (1, 0)])  9.28 us
    pallas_call x1, Pallas kernels, moments(): pl.pallas_call(moments_kernel, grid=(STEPS,), in_specs=[SMEM, SMEM, SMEM,...  6.15 us
    ppermute x3, waiting for transfers between devices, swap(): return lax.ppermute(x, 'mode', [(0, 1), (1, 0)])  3.46 us
    pallas_call x1, Pallas kernels, strengths(): pl.pallas_call(strength_kernel, grid=(STEPS,), in_specs=[SMEM, pl.BlockSp...  2.16 us
  transfers between devices with their start and end apart: 3, of which 3 were waited for; matrix products, arithmetic and copies ran while one was open for 0% of the time, Pallas kernels for 0%

profile of v2, /device:TPU:1, one launch (start us, length us, event | category | flops | bytes accessed | tf_op | source)
XLA Modules:
  0.0 93.2 jit_solution(183445032048859681)
XLA Ops:
  0.0 0.0 copy-start.2
  0.0 0.0 copy-start.5
  0.0 6.1 %child_moments.1 = (bf16[64,64,128]{2,1,0:T(8,128)(2,1)}, f32[576,128]{1,0:T(8,128)}, f32[576,128]{1,0:T(8,128)}, f32[64,256]{1,0:T(8,128)}) custom-call(s32[1]{0:T(128)} %bitcast.core_ref, s32[2,64]{1,0:T(2,128)} %bitcast.5, s32[64]{0:T(128)} %bitcast.6, s32[64]{0:T(128)} %block_ref.1, bf16[64,64,128]{2,1,0:T(8,128)(2,1)} %coupling_ref.1, ...), custom_call_target="tpu_custom_call" | custom-call | tf_op jit(solution)/shard_map/child_moments/pallas_call | solution.py:118
  6.2 0.0 copy-start
  6.2 3.3 %collective-permute-start = (f32[576,128]{1,0:T(8,128)}, f32[576,128]{1,0:T(8,128)S(1)}, u32[]{:S(2)}, u32[]{:S(2)}) collective-permute-start(f32[576,128]{1,0:T(8,128)} %get-tuple-element.13), channel_id=1, source_target_pairs={{0,1},{1,0},{2,3},{3,2},{4,5},{5,4},{6,7},{7,6},{8,9},{9,8},{10,11... | collective-permute-start | bytes 884744 | tf_op jit(solution)/shard_map/ppermute | solution.py:436
  9.5 1.4 %collective-permute-done.recv_ref = f32[576,128]{1,0:T(8,128)S(1)} collective-permute-done((f32[576,128]{1,0:T(8,128)}, f32[576,128]{1,0:T(8,128)S(1)}, u32[]{:S(2)}, u32[]{:S(2)}) %collective-permute-start) | collective-permute-done | bytes 294944 | tf_op jit(solution)/shard_map/ppermute | solution.py:436
  10.9 0.0 copy-start.1
  10.9 1.0 %copy-done.1 = f32[576,128]{1,0:T(8,128)S(1)} copy-done((f32[576,128]{1,0:T(8,128)S(1)}, f32[576,128]{1,0:T(8,128)}, u32[]{:S(2)}) %copy-start.1) | copy-done | bytes 294936
  11.9 0.0 copy-start.3
  11.9 0.8 copy-done.3
  12.7 0.0 copy-start.4
  12.7 0.4 dispatch.1
  13.1 16.2 %all_to_all.20.recv_ref = bf16[16,144,128]{2,1,0:T(8,128)(2,1)S(1)} all-to-all(bf16[16,144,128]{2,1,0:T(8,128)(2,1)S(1)} %dispatch.1), channel_id=1, replica_groups=mesh['y'=4,'z'=8,'x'=4,'mode'=2] {'y','x'}, dimensions={0} | all-to-all | bytes 1179648 | tf_op jit(solution)/shard_map/all_to_all | solution.py:440
  29.3 0.4 bin_slots.1
  29.7 16.4 %all_to_all.21.mine_ref = bf16[8,80,128]{2,1,0:T(8,128)(2,1)S(1)} all-to-all(bf16[8,80,128]{2,1,0:T(8,128)(2,1)S(1)} %get-tuple-element.14), channel_id=1, replica_groups=mesh['y'=4,'z'=8,'x'=4,'mode'=2] {'z'}, dimensions={0} | all-to-all | bytes 327680 | tf_op jit(solution)/shard_map/all_to_all | solution.py:440
  46.1 3.1 %collective-permute-start.1 = (bf16[8,80,128]{2,1,0:T(8,128)(2,1)S(1)}, bf16[8,80,128]{2,1,0:T(8,128)(2,1)S(1)}, u32[]{:S(2)}, u32[]{:S(2)}) collective-permute-start(bf16[8,80,128]{2,1,0:T(8,128)(2,1)S(1)} %all_to_all.21.mine_ref), channel_id=1, source_target_pairs={{0,1},{1,0},{2,3},{3,2},{4,5},{5,4},{6,7},{7,6},{8,9},{9,8},{10,11... | collective-permute-start | bytes 491528 | tf_op jit(solution)/shard_map/ppermute | solution.py:436
  49.2 1.0 %collective-permute-done.1.theirs_ref = bf16[8,80,128]{2,1,0:T(8,128)(2,1)S(1)} collective-permute-done((bf16[8,80,128]{2,1,0:T(8,128)(2,1)S(1)}, bf16[8,80,128]{2,1,0:T(8,128)(2,1)S(1)}, u32[]{:S(2)}, u32[]{:S(2)}) %collective-permute-start.1) | collective-permute-done | bytes 163872 | tf_op jit(solution)/shard_map/ppermute | solution.py:436
  50.2 0.0 copy-done.2
  50.2 0.0 copy-done.5
  50.2 11.5 %pencil_blocks.1 = bf16[8,80,128]{2,1,0:T(8,128)(2,1)S(1)} custom-call(s32[1]{0:T(128)} %bitcast.core_ref, bf16[8,80,128]{2,1,0:T(8,128)(2,1)S(1)} %all_to_all.21.mine_ref, bf16[8,80,128]{2,1,0:T(8,128)(2,1)S(1)} %collective-permute-done.1.theirs_ref, bf16[512,256]{1,0:T(8,128)(2,1)S(1)} %bitcast.4, f32[1,256]{1,0:T(1,128)S(1)} %copy-done.5), custom_call_target="tpu_custom_call" | custom-call | tf_op jit(solution)/shard_map/pencil_blocks/pallas_call | solution.py:328
  61.8 11.5 %all_to_all.22.bins_ref = bf16[8,80,128]{2,1,0:T(8,128)(2,1)S(1)} all-to-all(bf16[8,80,128]{2,1,0:T(8,128)(2,1)S(1)} %pencil_blocks.1), channel_id=1, replica_groups=mesh['y'=4,'z'=8,'x'=4,'mode'=2] {'z'}, dimensions={0} | all-to-all | bytes 327680 | tf_op jit(solution)/shard_map/all_to_all | solution.py:440
  73.3 0.3 select_bins.1
  73.6 13.4 %all_to_all.23.recv_ref = bf16[16,144,128]{2,1,0:T(8,128)(2,1)S(1)} all-to-all(bf16[16,144,128]{2,1,0:T(8,128)(2,1)S(1)} %select_bins.1), channel_id=1, replica_groups=mesh['y'=4,'z'=8,'x'=4,'mode'=2] {'y','x'}, dimensions={0} | all-to-all | bytes 1179648 | tf_op jit(solution)/shard_map/all_to_all | solution.py:440
  87.0 0.0 copy-done.4
  87.0 0.2 collect.1.mine_ref
  87.2 2.8 %collective-permute-start.2 = (bf16[576,128]{1,0:T(8,128)(2,1)S(1)}, bf16[576,128]{1,0:T(8,128)(2,1)S(1)}, u32[]{:S(2)}, u32[]{:S(2)}) collective-permute-start(bf16[576,128]{1,0:T(8,128)(2,1)S(1)} %collect.1.mine_ref), channel_id=1, source_target_pairs={{0,1},{1,0},{2,3},{3,2},{4,5},{5,4},{6,7},{7,6},{8,9},{9,8},{10,11... | collective-permute-start | bytes 442376 | tf_op jit(solution)/shard_map/ppermute | solution.py:436
  90.0 1.0 %collective-permute-done.2.theirs_ref = bf16[576,128]{1,0:T(8,128)(2,1)S(1)} collective-permute-done((bf16[576,128]{1,0:T(8,128)(2,1)S(1)}, bf16[576,128]{1,0:T(8,128)(2,1)S(1)}, u32[]{:S(2)}, u32[]{:S(2)}) %collective-permute-start.2) | collective-permute-done | bytes 147488 | tf_op jit(solution)/shard_map/ppermute | solution.py:436
  91.1 0.0 copy-done
  91.1 2.2 %strengths.1 = f32[64,128]{1,0:T(8,128)} custom-call(s32[1]{0:T(128)} %bitcast.core_ref, bf16[576,128]{1,0:T(8,128)(2,1)S(1)} %collect.1.mine_ref, bf16[576,128]{1,0:T(8,128)(2,1)S(1)} %collective-permute-done.2.theirs_ref, bf16[64,64,128]{2,1,0:T(8,128)(2,1)S(1)} %copy-done), custom_call_target="tpu_custom_call" | custom-call | tf_op jit(solution)/shard_map/strengths/pallas_call | solution.py:418
Async XLA Ops:
  0.0 50.2 %copy-start.2 = (bf16[1,512,256]{2,1,0:T(8,128)(2,1)S(1)}, bf16[1,512,256]{2,1,0:T(8,128)(2,1)}, u32[]{:S(2)}) copy-start(bf16[1,512,256]{2,1,0:T(8,128)(2,1)} %param.14) | copy-start | bytes 786436
  0.0 50.2 %copy-start.5 = (f32[1,256]{1,0:T(1,128)S(1)}, f32[1,256]{1,0:T(1,128)}, u32[]{:S(2)}) copy-start(f32[1,256]{1,0:T(1,128)} %eigs_ref.1) | copy-start | bytes 3076
  6.2 84.9 %copy-start = (bf16[64,64,128]{2,1,0:T(8,128)(2,1)S(1)}, bf16[64,64,128]{2,1,0:T(8,128)(2,1)}, u32[]{:S(2)}) copy-start(bf16[64,64,128]{2,1,0:T(8,128)(2,1)} %get-tuple-element.16.record_ref) | copy-start | bytes 3145732
  6.2 4.8 %collective-permute-start = (f32[576,128]{1,0:T(8,128)}, f32[576,128]{1,0:T(8,128)S(1)}, u32[]{:S(2)}, u32[]{:S(2)}) collective-permute-start(f32[576,128]{1,0:T(8,128)} %get-tuple-element.13), channel_id=1, source_target_pairs={{0,1},{1,0},{2,3},{3,2},{4,5},{5,4},{6,7},{7,6},{8,9},{9,8},{10,11... | collective-permute-start | bytes 884744 | tf_op jit(solution)/shard_map/ppermute | solution.py:436
  10.9 1.0 %copy-start.1 = (f32[576,128]{1,0:T(8,128)S(1)}, f32[576,128]{1,0:T(8,128)}, u32[]{:S(2)}) copy-start(f32[576,128]{1,0:T(8,128)} %get-tuple-element.12.own_ref) | copy-start | bytes 884740
  11.9 0.8 copy-start.3
  12.7 74.3 %copy-start.4 = (f32[64,256]{1,0:T(8,128)S(1)}, f32[64,256]{1,0:T(8,128)}, u32[]{:S(2)}) copy-start(f32[64,256]{1,0:T(8,128)} %get-tuple-element.11.onehot_ref) | copy-start | bytes 196612
  46.1 4.2 %collective-permute-start.1 = (bf16[8,80,128]{2,1,0:T(8,128)(2,1)S(1)}, bf16[8,80,128]{2,1,0:T(8,128)(2,1)S(1)}, u32[]{:S(2)}, u32[]{:S(2)}) collective-permute-start(bf16[8,80,128]{2,1,0:T(8,128)(2,1)S(1)} %all_to_all.21.mine_ref), channel_id=1, source_target_pairs={{0,1},{1,0},{2,3},{3,2},{4,5},{5,4},{6,7},{7,6},{8,9},{9,8},{10,11... | collective-permute-start | bytes 491528 | tf_op jit(solution)/shard_map/ppermute | solution.py:436
  87.2 3.8 %collective-permute-start.2 = (bf16[576,128]{1,0:T(8,128)(2,1)S(1)}, bf16[576,128]{1,0:T(8,128)(2,1)S(1)}, u32[]{:S(2)}, u32[]{:S(2)}) collective-permute-start(bf16[576,128]{1,0:T(8,128)(2,1)S(1)} %collect.1.mine_ref), channel_id=1, source_target_pairs={{0,1},{1,0},{2,3},{3,2},{4,5},{5,4},{6,7},{7,6},{8,9},{9,8},{10,11... | collective-permute-start | bytes 442376 | tf_op jit(solution)/shard_map/ppermute | solution.py:436

commit v3 on v2

--- a/solution.py
+++ b/solution.py
@@ -3,7 +3,7 @@
 from jax import lax
 from jax.experimental import pallas as pl
 from jax.experimental.pallas import tpu as pltpu
-from jax.sharding import Mesh, PartitionSpec as P
+from jax.sharding import PartitionSpec as P
 
 MP = 256
 BLK = 64
@@ -12,11 +12,10 @@
 CHILDREN_DEV = 64
 CB = 16
 STEPS = CHILDREN_DEV // CB
-NY, NZ, NX = 4, 8, 4
-NG = NY * NX
-SLOTS = 2 * NZ
-ROWS = 9 * SLOTS
-ZROWS = 80
+PARENTS = 128
+SLOTS = 2 * PARENTS
+ROWS = 24
+BROWS = 72
 PB = 32
 BF = jnp.bfloat16
 F32 = jnp.float32
@@ -62,95 +61,109 @@
 
 
 def moments_kernel(
-    core_ref, pairs_ref, parent_ref, block_ref, coupling_ref, modes_ref, weights_ref,
-    record_ref, own_ref, other_ref, onehot_ref, count_ref,
+    core_ref, pairs_ref, parent_ref, block_ref, coupling_hbm, modes_hbm, weights_ref,
+    record_ref, own_ref, other_ref, onehot_ref, coupling_ref, modes_ref, count_ref, coupling_sem, modes_sem,
 ):
-    step = pl.program_id(0)
     row = lax.broadcasted_iota(jnp.int32, (HALF, HALF), 0)
     col = lax.broadcasted_iota(jnp.int32, (HALF, HALF), 1)
     lower = row >= col
     diagonal = lax.broadcasted_iota(jnp.int32, (HALF, BLK), 1) == (
         lax.broadcasted_iota(jnp.int32, (HALF, BLK), 0) + HALF
     )
-    slots = lax.broadcasted_iota(jnp.int32, (1, NG * SLOTS), 1)
+    slots = lax.broadcasted_iota(jnp.int32, (1, SLOTS), 1)
     first = core_ref[0] == 0
 
-    @pl.when(step == 0)
-    def _():
-        for p in range(NG * NZ):
-            count_ref[p] = 0
-
-    for pair in range(CB // 2):
-        records = []
-        for j in (2 * pair, 2 * pair + 1):
-            c = step * CB + j
-            top = modes_ref[j, pl.ds(pl.multiple_of(pairs_ref[0, c] * BLK, BLK), BLK), :]
-            bottom = modes_ref[j, pl.ds(pl.multiple_of(pairs_ref[1, c] * BLK, BLK), BLK), :]
-            record = dot(coupling_ref[j], jnp.concatenate([top, bottom], axis=0))
-            record = (record * weights_ref[j : j + 1, :].astype(F32)).astype(BF)
-            record_ref[j] = record
-            records.append(record)
-        both = jnp.concatenate(records, axis=0)
-        products = dot_nt(both, both)
-        for i in range(2):
-            c = step * CB + 2 * pair + i
-            s = products[i * BLK : (i + 1) * BLK, i * BLK : (i + 1) * BLK]
-            cross = side_by_side(s[HALF:, :HALF])
-            triangle = side_by_side(jnp.where(lower, s[:HALF, :HALF], s[HALF:, HALF:]))
-            own_ref[pl.ds(c, 8, stride=CHILDREN_DEV), :] = jnp.where(first, cross, triangle)
-            other_ref[pl.ds(c, 8, stride=CHILDREN_DEV), :] = jnp.where(first, triangle, cross)
-            diag = jnp.sum(jnp.where(diagonal, s[HALF:], 0.0), axis=0, keepdims=True)
-            zero = jnp.zeros((1, BLK), F32)
-            named = zero + (block_ref[c] + 1).astype(F32)
-            own_ref[pl.ds(8 * CHILDREN_DEV + c, 1), :] = jnp.concatenate([diag, named], axis=1)
-            other_ref[pl.ds(8 * CHILDREN_DEV + c, 1), :] = jnp.concatenate([diag, zero], axis=1)
-            p = parent_ref[c]
-            k = count_ref[p]
-            count_ref[p] = k + 1
-            group = (p // (NZ * NX)) * NX + p % NX
-            slot = group * SLOTS + ((p // NX) % NZ) * 2 + k
-            onehot_ref[pl.ds(c, 1), :] = jnp.where(slots == slot, 1.0, 0.0)
+    def copies(step):
+        part = pl.ds(step * CB, CB)
+        return (
+            pltpu.make_async_copy(modes_hbm.at[part], modes_ref.at[part], modes_sem.at[step]),
+            pltpu.make_async_copy(coupling_hbm.at[part], coupling_ref.at[part], coupling_sem.at[step]),
+        )
+
+    for step in range(STEPS):
+        for copy in copies(step):
+            copy.start()
+    for p in range(PARENTS):
+        count_ref[p] = 0
+
+    @pl.loop(0, STEPS)
+    def _(step):
+        for copy in copies(step):
+            copy.wait()
+        weights = weights_ref[pl.ds(pl.multiple_of(step * CB, CB), CB), :].astype(F32)
+        for pair in range(CB // 2):
+            records = []
+            for j in (2 * pair, 2 * pair + 1):
+                c = step * CB + j
+                top = modes_ref[c, pl.ds(pl.multiple_of(pairs_ref[0, c] * BLK, BLK), BLK), :]
+                bottom = modes_ref[c, pl.ds(pl.multiple_of(pairs_ref[1, c] * BLK, BLK), BLK), :]
+                record = dot(coupling_ref[c], jnp.concatenate([top, bottom], axis=0))
+                record = (record * weights[j : j + 1, :]).astype(BF)
+                record_ref[c] = record
+                records.append(record)
+            both = jnp.concatenate(records, axis=0)
+            products = dot_nt(both, both)
+            for i in range(2):
+                c = step * CB + 2 * pair + i
+                s = products[i * BLK : (i + 1) * BLK, i * BLK : (i + 1) * BLK]
+                cross = side_by_side(s[HALF:, :HALF])
+                triangle = side_by_side(jnp.where(lower, s[:HALF, :HALF], s[HALF:, HALF:]))
+                own_ref[pl.ds(c, 8, stride=CHILDREN_DEV), :] = jnp.where(first, cross, triangle)
+                other_ref[pl.ds(c, 8, stride=CHILDREN_DEV), :] = jnp.where(first, triangle, cross)
+                diag = jnp.sum(jnp.where(diagonal, s[HALF:], 0.0), axis=0, keepdims=True)
+                zero = jnp.zeros((1, BLK), F32)
+                named = zero + (block_ref[c] + 1).astype(F32)
+                own_ref[pl.ds(8 * CHILDREN_DEV + c, 1), :] = jnp.concatenate([diag, named], axis=1)
+                other_ref[pl.ds(8 * CHILDREN_DEV + c, 1), :] = jnp.concatenate([diag, zero], axis=1)
+                p = parent_ref[c]
+                k = count_ref[p]
+                count_ref[p] = k + 1
+                onehot_ref[pl.ds(c, 1), :] = jnp.where(slots == k * PARENTS + p, 1.0, 0.0)
 
 
 def moments(core, pairs, parent, block, coupling, modes, weights):
     whole = (9 * CHILDREN_DEV, 128)
-    onehot = (CHILDREN_DEV, NG * SLOTS)
+    hbm = pl.BlockSpec(memory_space=pltpu.HBM)
     return pl.pallas_call(
         moments_kernel,
-        grid=(STEPS,),
-        in_specs=[
-            SMEM,
-            SMEM,
-            SMEM,
-            SMEM,
-            pl.BlockSpec((CB, BLK, 128), lambda i: (i, 0, 0)),
-            pl.BlockSpec((CB, 256, 128), lambda i: (i, 0, 0)),
-            pl.BlockSpec((CB, 128), lambda i: (i, 0)),
-        ],
-        out_specs=[
-            pl.BlockSpec((CB, BLK, 128), lambda i: (i, 0, 0)),
-            pl.BlockSpec(whole, lambda i: (0, 0)),
-            pl.BlockSpec(whole, lambda i: (0, 0)),
-            pl.BlockSpec(onehot, lambda i: (0, 0)),
-        ],
+        in_specs=[SMEM, SMEM, SMEM, SMEM, hbm, hbm, VMEM],
+        out_specs=[VMEM, VMEM, VMEM, VMEM],
         out_shape=[
             jax.ShapeDtypeStruct((CHILDREN_DEV, BLK, 128), BF),
             jax.ShapeDtypeStruct(whole, F32),
             jax.ShapeDtypeStruct(whole, F32),
-            jax.ShapeDtypeStruct(onehot, F32),
+            jax.ShapeDtypeStruct((CHILDREN_DEV, SLOTS), F32),
         ],
-        scratch_shapes=[pltpu.SMEM((NG * NZ,), jnp.int32)],
-        compiler_params=params(60),
+        scratch_shapes=[
+            pltpu.VMEM((CHILDREN_DEV, BLK, 128), BF),
+            pltpu.VMEM((CHILDREN_DEV, 256, 128), BF),
+            pltpu.SMEM((PARENTS,), jnp.int32),
+            pltpu.SemaphoreType.DMA((STEPS,)),
+            pltpu.SemaphoreType.DMA((STEPS,)),
+        ],
+        compiler_params=params(52),
         name="child_moments",
     )(core, pairs, parent, block, coupling, modes, weights)
 
 
-def dispatch_kernel(onehot_ref, own_ref, recv_ref, out_ref):
+def message_row(i, k):
+    return k * 8 + i if i < 8 else 16 + k
+
+
+def every_device(i, k):
+    return pl.ds(message_row(i, k), PARENTS, stride=ROWS)
+
+
+def dispatch_kernel(onehot_ref, own_ref, recv_ref, out_ref, buf_ref):
     place = onehot_ref[...].T.astype(BF)
     for i in range(9):
         rows = slice(i * CHILDREN_DEV, (i + 1) * CHILDREN_DEV)
-        values = (own_ref[rows, :] + recv_ref[rows, :]).astype(BF)
-        out_ref[:, i * SLOTS : (i + 1) * SLOTS, :] = dot(place, values).astype(BF).reshape(NG, SLOTS, 128)
+        values = dot(place, (own_ref[rows, :] + recv_ref[rows, :]).astype(BF))
+        for k in range(2):
+            buf_ref[every_device(i, k), :] = values[k * PARENTS : (k + 1) * PARENTS]
+    for r in range(18, ROWS):
+        buf_ref[pl.ds(r, PARENTS, stride=ROWS), :] = jnp.zeros((PARENTS, 128), F32)
+    out_ref[...] = buf_ref[...].astype(BF).reshape(PARENTS, ROWS, 128)
 
 
 def dispatch(onehot, own, recv):
@@ -158,30 +171,29 @@
         dispatch_kernel,
         in_specs=[VMEM, VMEM, VMEM],
         out_specs=VMEM,
-        out_shape=jax.ShapeDtypeStruct((NG, ROWS, 128), BF),
+        out_shape=jax.ShapeDtypeStruct((PARENTS, ROWS, 128), BF),
+        scratch_shapes=[pltpu.VMEM((PARENTS * ROWS, 128), F32)],
         compiler_params=params(16),
         name="dispatch",
     )(onehot, own, recv)
 
 
-def bin_kernel(recv_ref, out_ref, onehot_ref):
-    count = NG * SLOTS
-    meta = recv_ref[:, 8 * SLOTS : ROWS, :].astype(F32).reshape(count, 128)
-    slot = lax.broadcasted_iota(jnp.int32, (count, 128), 0) % SLOTS
-    lane = lax.broadcasted_iota(jnp.int32, (count, 128), 1)
-    meta = pltpu.roll(meta, 64, 1)
-    target = meta + (SB * (slot // 2) - 1).astype(F32)
-    hit = (lane < 64) & (meta > 0.5) & (target == lane.astype(F32))
+def bin_kernel(recv_ref, out_ref, onehot_ref, buf_ref):
+    buf_ref[...] = recv_ref[...].astype(F32).reshape(PARENTS * ROWS, 128)
+
+    def both(i):
+        return jnp.concatenate([buf_ref[every_device(i, 0), :], buf_ref[every_device(i, 1), :]], axis=0)
+
+    lane = lax.broadcasted_iota(jnp.int32, (SLOTS, 128), 1)
+    last = both(8)
+    named = pltpu.roll(last, 64, 1)
+    hit = (lane < SB) & (named > 0.5) & (named - 1.0 == lane.astype(F32))
     onehot = jnp.where(hit, 1.0, 0.0).astype(BF)
     onehot_ref[...] = onehot
-    values = jnp.concatenate(
-        [recv_ref[:, i * SLOTS : (i + 1) * SLOTS, :].reshape(count, 128) for i in range(9)], axis=1
-    )
+    values = jnp.concatenate([both(i).astype(BF) for i in range(8)] + [last.astype(BF)], axis=1)
     bins = dot_tn(onehot, values)
-    zero = jnp.zeros((8, 128), F32)
-    for z in range(NZ):
-        rows = [bins[8 * z : 8 * z + 8, 128 * i : 128 * (i + 1)] for i in range(9)] + [zero]
-        out_ref[z] = jnp.concatenate(rows, axis=0).astype(BF)
+    for i in range(9):
+        out_ref[i * SB : (i + 1) * SB, :] = bins[:SB, 128 * i : 128 * (i + 1)]
 
 
 def bin_slots(recv):
@@ -190,9 +202,10 @@
         in_specs=[VMEM],
         out_specs=[VMEM, VMEM],
         out_shape=[
-            jax.ShapeDtypeStruct((NZ, ZROWS, 128), BF),
-            jax.ShapeDtypeStruct((NG * SLOTS, 128), BF),
+            jax.ShapeDtypeStruct((BROWS, 128), F32),
+            jax.ShapeDtypeStruct((SLOTS, 128), BF),
         ],
+        scratch_shapes=[pltpu.VMEM((PARENTS * ROWS, 128), F32)],
         compiler_params=params(16),
         name="bin_slots",
     )(recv)
@@ -268,13 +281,8 @@
 
 
 def pencil_kernel(
-    core_ref, mine_ref, theirs_ref, q_ref, eigs_ref, out_ref, a_ref, y_ref, pack_ref, own_ref, other_ref
+    core_ref, own_ref, other_ref, onehot_ref, q_ref, eigs_ref, out_ref, a_ref, y_ref, pack_ref, buf_ref
 ):
-    for source, target in ((mine_ref, own_ref), (theirs_ref, other_ref)):
-        parts = [source[z].astype(F32) for z in range(NZ)]
-        while len(parts) > 1:
-            parts = [x + y for x, y in zip(parts[::2], parts[1::2])]
-        target[...] = parts[0]
     row, col, same = tile_index()
     first = core_ref[0] == 0
     lane8 = lax.broadcasted_iota(jnp.int32, (8, 128), 1)
@@ -317,56 +325,40 @@
             jnp.where(row > col, 2.0 * u[:HALF], jnp.where(row == col, u[:HALF], 2.0 * v))
         )
         pack_ref[pl.ds(b, 8, stride=8), :] = jnp.where(first, cross, triangle)
-        pack_ref[64 + b : 65 + b, :] = jnp.sum(jnp.where(row == col, v, 0.0), axis=0, keepdims=True)
-    pack_ref[72:80, :] = jnp.zeros((8, 128), F32)
-    result = pack_ref[...].astype(BF)
-    for z in range(NZ):
-        out_ref[z] = result
-
-
-def pencil_blocks(core, own, other, q, eigs):
+        pack_ref[8 * SB + b : 8 * SB + b + 1, :] = jnp.sum(jnp.where(row == col, v, 0.0), axis=0, keepdims=True)
+    blocks = jnp.concatenate([pack_ref[i * SB : (i + 1) * SB, :] for i in range(9)], axis=1).astype(BF)
+    picked = dot(onehot_ref[:, :SB], blocks)
+    for i in range(9):
+        for k in range(2):
+            buf_ref[every_device(i, k), :] = picked[k * PARENTS : (k + 1) * PARENTS, 128 * i : 128 * (i + 1)]
+    for r in range(18, ROWS):
+        buf_ref[pl.ds(r, PARENTS, stride=ROWS), :] = jnp.zeros((PARENTS, 128), F32)
+    out_ref[...] = buf_ref[...].astype(BF).reshape(PARENTS, ROWS, 128)
+
+
+def pencil_blocks(core, own, other, onehot, q, eigs):
     return pl.pallas_call(
         pencil_kernel,
-        in_specs=[SMEM, VMEM, VMEM, VMEM, VMEM],
+        in_specs=[SMEM, VMEM, VMEM, VMEM, VMEM, VMEM],
         out_specs=VMEM,
-        out_shape=jax.ShapeDtypeStruct((NZ, ZROWS, 128), BF),
+        out_shape=jax.ShapeDtypeStruct((PARENTS, ROWS, 128), BF),
         scratch_shapes=[
             pltpu.VMEM((MP, MP), F32),
             pltpu.VMEM((SB * BLK, MP), BF),
-            pltpu.VMEM((ZROWS, 128), F32),
-            pltpu.VMEM((ZROWS, 128), F32),
-            pltpu.VMEM((ZROWS, 128), F32),
+            pltpu.VMEM((BROWS, 128), F32),
+            pltpu.VMEM((PARENTS * ROWS, 128), F32),
         ],
         compiler_params=params(16),
         name="pencil_blocks",
-    )(core, own, other, q, eigs)
-
-
-def select_kernel(bins_ref, onehot_ref, out_ref):
-    onehot = onehot_ref[:, 0:64]
-    bins = [bins_ref[z].astype(F32) for z in range(NZ)]
-    for i in range(9):
-        values = jnp.concatenate([x[8 * i : 8 * i + 8] for x in bins], axis=0).astype(BF)
-        picked = dot(onehot, values).astype(BF)
-        out_ref[:, i * SLOTS : (i + 1) * SLOTS, :] = picked.reshape(NG, SLOTS, 128)
-
-
-def select_bins(bins, onehot):
-    return pl.pallas_call(
-        select_kernel,
-        in_specs=[VMEM, VMEM],
-        out_specs=VMEM,
-        out_shape=jax.ShapeDtypeStruct((NG, ROWS, 128), BF),
-        compiler_params=params(16),
-        name="select_bins",
-    )(bins, onehot)
-
-
-def collect_kernel(onehot_ref, recv_ref, out_ref):
+    )(core, own, other, onehot, q, eigs)
+
+
+def collect_kernel(onehot_ref, recv_ref, out_ref, buf_ref):
+    buf_ref[...] = recv_ref[...].astype(F32).reshape(PARENTS * ROWS, 128)
     onehot = onehot_ref[...].astype(BF)
     for i in range(9):
-        values = recv_ref[:, i * SLOTS : (i + 1) * SLOTS, :].reshape(NG * SLOTS, 128)
-        out_ref[i * CHILDREN_DEV : (i + 1) * CHILDREN_DEV, :] = dot(onehot, values).astype(BF)
+        values = jnp.concatenate([buf_ref[every_device(i, 0), :], buf_ref[every_device(i, 1), :]], axis=0)
+        out_ref[i * CHILDREN_DEV : (i + 1) * CHILDREN_DEV, :] = dot(onehot, values.astype(BF)).astype(BF)
 
 
 def collect(onehot, recv):
@@ -375,6 +367,7 @@
         in_specs=[VMEM, VMEM],
         out_specs=VMEM,
         out_shape=jax.ShapeDtypeStruct((9 * CHILDREN_DEV, 128), BF),
+        scratch_shapes=[pltpu.VMEM((PARENTS * ROWS, 128), F32)],
         compiler_params=params(16),
         name="collect",
     )(onehot, recv)
@@ -436,36 +429,31 @@
     return lax.ppermute(x, "mode", [(0, 1), (1, 0)])
 
 
-def exchange(x, axes):
-    return lax.all_to_all(x, axes, split_axis=0, concat_axis=0, tiled=True)
+def exchange(x):
+    return lax.all_to_all(x, "sub", split_axis=0, concat_axis=0, tiled=True)
 
 
 def per_device(coupling, pairs, modes, weights, parent_of, row_block, parent_modes, parent_eigs):
     core = lax.axis_index("mode").astype(jnp.int32).reshape(1)
     parent = parent_of.reshape(CHILDREN_DEV)
     record, own, other, onehot = moments(core, pairs.T, parent, row_block, coupling, modes, weights)
-    sent = dispatch(onehot, own, swap(other))
-    binned, chosen = bin_slots(exchange(sent, ("y", "x")))
-    bins = exchange(binned, "z")
-    blocks = pencil_blocks(core, bins, swap(bins), parent_modes[0], parent_eigs)
-    picked = select_bins(exchange(blocks, "z"), chosen)
-    mine = collect(onehot, exchange(picked, ("y", "x")))
+    bins, chosen = bin_slots(exchange(dispatch(onehot, own, swap(other))))
+    picked = pencil_blocks(core, bins, swap(bins), chosen, parent_modes[0], parent_eigs)
+    mine = collect(onehot, exchange(picked))
     return strengths(core, mine, swap(mine), record)
 
 
 def solution(mesh):
-    grid = Mesh(mesh.devices.reshape(NY, NZ, NX, 2), ("y", "z", "x", "mode"))
-    sub = ("y", "z", "x")
     in_specs = (
-        P(sub, None, None),
-        P(sub, None),
-        P(sub, None, "mode"),
-        P(sub, "mode"),
-        P(sub, None),
-        P(sub),
-        P(sub, None, None),
-        P(sub, None),
+        P("sub", None, None),
+        P("sub", None),
+        P("sub", None, "mode"),
+        P("sub", "mode"),
+        P("sub", None),
+        P("sub"),
+        P("sub", None, None),
+        P("sub", None),
     )
     return jax.shard_map(
-        per_device, mesh=grid, in_specs=in_specs, out_specs=P(sub, "mode"), check_vma=False
+        per_device, mesh=mesh, in_specs=in_specs, out_specs=P("sub", "mode"), check_vma=False
     )

time: 93.6 us -> 101 us (1.079)
  blocking collectives: 57.5 us -> 64.9 us
    all_to_all x4 -> x2, blocking collectives: 57.5 us -> 64.9 us  [exchange(): return lax.all_to_all(x, 'sub', split_axis=0, concat_axis=0, tiled=True)]
    pallas_call x3 -> x2, Pallas kernels: 18 us -> 16.8 us  [the longest x1 12 us: pencil_blocks(): pl.pallas_call(pencil_kernel, in_specs=[SMEM, VMEM, VMEM, VMEM, VMEM, VME...]
where the time goes in v3:
time: 101 us
  blocking collectives  64.9 us (64%)
  Pallas kernels  20.5 us (20%)
  starting transfers between devices  9.95 us (10%)
  waiting for transfers between devices  3.08 us (3%)
  local copies, waits for them, and re-layouts  2.71 us (3%)
    all_to_all x2, blocking collectives, exchange(): return lax.all_to_all(x, 'sub', split_axis=0, concat_axis=0, tiled=True)  64.9 us
    pallas_call x1, Pallas kernels, pencil_blocks(): pl.pallas_call(pencil_kernel, in_specs=[SMEM, VMEM, VMEM, VMEM, VMEM, VME...  12 us
    ppermute x3, starting transfers between devices, swap(): return lax.ppermute(x, 'mode', [(0, 1), (1, 0)])  9.95 us
    pallas_call x1, Pallas kernels, moments(): pl.pallas_call(moments_kernel, in_specs=[SMEM, SMEM, SMEM, SMEM, hbm, hbm...  4.85 us
    ppermute x3, waiting for transfers between devices, swap(): return lax.ppermute(x, 'mode', [(0, 1), (1, 0)])  3.08 us
    unnamed x12, local copies, waits for them, and re-layouts  2.71 us
    pallas_call x1, Pallas kernels, strengths(): pl.pallas_call(strength_kernel, grid=(STEPS,), in_specs=[SMEM, pl.BlockSp...  2.16 us
  transfers between devices with their start and end apart: 3, of which 3 were waited for; matrix products, arithmetic and copies ran while one was open for 0% of the time, Pallas kernels for 0%

profile of v3, /device:TPU:1, one launch (start us, length us, event | category | flops | bytes accessed | tf_op | source)
XLA Modules:
  0.0 101.1 jit_solution(3690724720018334868)
XLA Ops:
  0.0 0.0 copy-start.1
  0.0 0.7 copy-done.1
  0.7 0.0 copy-start.2
  0.7 0.7 copy-done.2
  1.4 0.0 copy-start.4
  1.4 0.7 copy-done.4
  2.1 0.0 copy-start.5
  2.1 0.7 copy-done.5
  2.7 0.0 copy-start
  2.7 0.0 copy-start.3
  2.7 4.9 %child_moments.1 = (bf16[64,64,128]{2,1,0:T(8,128)(2,1)S(1)}, f32[576,128]{1,0:T(8,128)S(1)}, f32[576,128]{1,0:T(8,128)S(1)}, f32[64,256]{1,0:T(8,128)S(1)}) custom-call(s32[1]{0:T(128)} %bitcast.core_ref, s32[2,64]{1,0:T(2,128)S(1)} %bitcast.5, s32[64]{0:T(128)S(1)} %bitcast.6, s32[64]{0:T(128)S(1)} %copy-done.5, bf16[64,64,128]{2,1,0:T(8,128)(2,1)} %coupling_hbm.1, ...), custom_call_target="tpu_custom_call" | custom-call | tf_op jit(solution)/shard_map/child_moments/pallas_call | solution.py:127
  7.6 3.3 %collective-permute-start = (f32[576,128]{1,0:T(8,128)S(1)}, f32[576,128]{1,0:T(8,128)S(1)}, u32[]{:S(2)}, u32[]{:S(2)}) collective-permute-start(f32[576,128]{1,0:T(8,128)S(1)} %get-tuple-element.13), channel_id=1, source_target_pairs={{0,1},{1,0},{2,3},{3,2},{4,5},{5,4},{6,7},{7,6},{8,9},{9,8},{10,11... | collective-permute-start | bytes 884744 | tf_op jit(solution)/shard_map/ppermute | solution.py:429
  10.9 1.2 %collective-permute-done.recv_ref = f32[576,128]{1,0:T(8,128)S(1)} collective-permute-done((f32[576,128]{1,0:T(8,128)S(1)}, f32[576,128]{1,0:T(8,128)S(1)}, u32[]{:S(2)}, u32[]{:S(2)}) %collective-permute-start) | collective-permute-done | bytes 294944 | tf_op jit(solution)/shard_map/ppermute | solution.py:429
  12.1 0.6 dispatch.1
  12.7 35.7 %all_to_all.10.recv_ref = bf16[128,24,128]{2,1,0:T(8,128)(2,1)S(1)} all-to-all(bf16[128,24,128]{2,1,0:T(8,128)(2,1)S(1)} %dispatch.1), channel_id=1, replica_groups=mesh['sub'=128,'mode'=2] {'sub'}, dimensions={0} | all-to-all | bytes 1572864 | tf_op jit(solution)/shard_map/all_to_all | solution.py:433
  48.4 0.5 bin_slots.1
  48.9 3.4 %collective-permute-start.1 = (f32[72,128]{1,0:T(8,128)S(1)}, f32[72,128]{1,0:T(8,128)S(1)}, u32[]{:S(2)}, u32[]{:S(2)}) collective-permute-start(f32[72,128]{1,0:T(8,128)S(1)} %get-tuple-element.14.own_ref), channel_id=1, source_target_pairs={{0,1},{1,0},{2,3},{3,2},{4,5},{5,4},{6,7},{7,6},{8,9},{9,8},{10,11... | collective-permute-start | bytes 110600 | tf_op jit(solution)/shard_map/ppermute | solution.py:429
  52.2 0.9 collective-permute-done.1.other_ref
  53.1 0.0 copy-done
  53.1 0.0 copy-done.3
  53.1 12.0 %pencil_blocks.1 = bf16[128,24,128]{2,1,0:T(8,128)(2,1)S(1)} custom-call(s32[1]{0:T(128)} %bitcast.core_ref, f32[72,128]{1,0:T(8,128)S(1)} %get-tuple-element.14.own_ref, f32[72,128]{1,0:T(8,128)S(1)} %collective-permute-done.1.other_ref, bf16[256,128]{1,0:T(8,128)(2,1)S(1)} %get-tuple-element.15.onehot_ref, bf16[512,256]{1,0:T(8,128)(2,1)S(1)} %bitcast.4, ...), custom_call_target="tpu_custom_call" | custom-call | tf_op jit(solution)/shard_map/pencil_blocks/pallas_call | solution.py:340
  65.1 29.2 %all_to_all.11.recv_ref = bf16[128,24,128]{2,1,0:T(8,128)(2,1)S(1)} all-to-all(bf16[128,24,128]{2,1,0:T(8,128)(2,1)S(1)} %pencil_blocks.1), channel_id=1, replica_groups=mesh['sub'=128,'mode'=2] {'sub'}, dimensions={0} | all-to-all | bytes 1572864 | tf_op jit(solution)/shard_map/all_to_all | solution.py:433
  94.3 0.4 collect.1.mine_ref
  94.7 3.2 %collective-permute-start.2 = (bf16[576,128]{1,0:T(8,128)(2,1)S(1)}, bf16[576,128]{1,0:T(8,128)(2,1)S(1)}, u32[]{:S(2)}, u32[]{:S(2)}) collective-permute-start(bf16[576,128]{1,0:T(8,128)(2,1)S(1)} %collect.1.mine_ref), channel_id=1, source_target_pairs={{0,1},{1,0},{2,3},{3,2},{4,5},{5,4},{6,7},{7,6},{8,9},{9,8},{10,11... | collective-permute-start | bytes 442376 | tf_op jit(solution)/shard_map/ppermute | solution.py:429
  98.0 1.0 collective-permute-done.2.theirs_ref
  99.0 2.2 %strengths.1 = f32[64,128]{1,0:T(8,128)} custom-call(s32[1]{0:T(128)} %bitcast.core_ref, bf16[576,128]{1,0:T(8,128)(2,1)S(1)} %collect.1.mine_ref, bf16[576,128]{1,0:T(8,128)(2,1)S(1)} %collective-permute-done.2.theirs_ref, bf16[64,64,128]{2,1,0:T(8,128)(2,1)S(1)} %get-tuple-element.16.record_ref), custom_call_target="tpu_custom_call" | custom-call | tf_op jit(solution)/shard_map/strengths/pallas_call | solution.py:411
Async XLA Ops:
  0.0 0.7 copy-start.1
  0.7 0.7 copy-start.2
  1.4 0.7 copy-start.4
  2.1 0.7 copy-start.5
  2.7 50.4 %copy-start = (bf16[1,512,256]{2,1,0:T(8,128)(2,1)S(1)}, bf16[1,512,256]{2,1,0:T(8,128)(2,1)}, u32[]{:S(2)}) copy-start(bf16[1,512,256]{2,1,0:T(8,128)(2,1)} %param.14) | copy-start | bytes 786436
  2.7 50.4 %copy-start.3 = (f32[1,256]{1,0:T(1,128)S(1)}, f32[1,256]{1,0:T(1,128)}, u32[]{:S(2)}) copy-start(f32[1,256]{1,0:T(1,128)} %eigs_ref.1) | copy-start | bytes 3076
  7.6 4.5 %collective-permute-start = (f32[576,128]{1,0:T(8,128)S(1)}, f32[576,128]{1,0:T(8,128)S(1)}, u32[]{:S(2)}, u32[]{:S(2)}) collective-permute-start(f32[576,128]{1,0:T(8,128)S(1)} %get-tuple-element.13), channel_id=1, source_target_pairs={{0,1},{1,0},{2,3},{3,2},{4,5},{5,4},{6,7},{7,6},{8,9},{9,8},{10,11... | collective-permute-start | bytes 884744 | tf_op jit(solution)/shard_map/ppermute | solution.py:429
  48.9 4.2 %collective-permute-start.1 = (f32[72,128]{1,0:T(8,128)S(1)}, f32[72,128]{1,0:T(8,128)S(1)}, u32[]{:S(2)}, u32[]{:S(2)}) collective-permute-start(f32[72,128]{1,0:T(8,128)S(1)} %get-tuple-element.14.own_ref), channel_id=1, source_target_pairs={{0,1},{1,0},{2,3},{3,2},{4,5},{5,4},{6,7},{7,6},{8,9},{9,8},{10,11... | collective-permute-start | bytes 110600 | tf_op jit(solution)/shard_map/ppermute | solution.py:429
  94.7 4.3 %collective-permute-start.2 = (bf16[576,128]{1,0:T(8,128)(2,1)S(1)}, bf16[576,128]{1,0:T(8,128)(2,1)S(1)}, u32[]{:S(2)}, u32[]{:S(2)}) collective-permute-start(bf16[576,128]{1,0:T(8,128)(2,1)S(1)} %collect.1.mine_ref), channel_id=1, source_target_pairs={{0,1},{1,0},{2,3},{3,2},{4,5},{5,4},{6,7},{7,6},{8,9},{9,8},{10,11... | collective-permute-start | bytes 442376 | tf_op jit(solution)/shard_map/ppermute | solution.py:429

commit v4 on v2

--- a/solution.py
+++ b/solution.py
@@ -10,7 +10,7 @@
 HALF = 32
 SB = 8
 CHILDREN_DEV = 64
-CB = 16
+CB = 32
 STEPS = CHILDREN_DEV // CB
 NY, NZ, NX = 4, 8, 4
 NG = NY * NX
@@ -62,98 +62,134 @@
 
 
 def moments_kernel(
-    core_ref, pairs_ref, parent_ref, block_ref, coupling_ref, modes_ref, weights_ref,
-    record_ref, own_ref, other_ref, onehot_ref, count_ref,
+    core_ref, pairs_ref, parent_ref, block_ref, coupling_hbm, modes_hbm, weights_ref,
+    record_ref, own_ref, other_ref, coupling_ref, modes_ref, count_ref, coupling_sem, modes_sem,
 ):
-    step = pl.program_id(0)
     row = lax.broadcasted_iota(jnp.int32, (HALF, HALF), 0)
     col = lax.broadcasted_iota(jnp.int32, (HALF, HALF), 1)
     lower = row >= col
     diagonal = lax.broadcasted_iota(jnp.int32, (HALF, BLK), 1) == (
         lax.broadcasted_iota(jnp.int32, (HALF, BLK), 0) + HALF
     )
-    slots = lax.broadcasted_iota(jnp.int32, (1, NG * SLOTS), 1)
+    slots = lax.broadcasted_iota(jnp.int32, (1, 128), 1)
     first = core_ref[0] == 0
 
-    @pl.when(step == 0)
-    def _():
-        for p in range(NG * NZ):
-            count_ref[p] = 0
-
-    for pair in range(CB // 2):
-        records = []
-        for j in (2 * pair, 2 * pair + 1):
-            c = step * CB + j
-            top = modes_ref[j, pl.ds(pl.multiple_of(pairs_ref[0, c] * BLK, BLK), BLK), :]
-            bottom = modes_ref[j, pl.ds(pl.multiple_of(pairs_ref[1, c] * BLK, BLK), BLK), :]
-            record = dot(coupling_ref[j], jnp.concatenate([top, bottom], axis=0))
-            record = (record * weights_ref[j : j + 1, :].astype(F32)).astype(BF)
-            record_ref[j] = record
-            records.append(record)
-        both = jnp.concatenate(records, axis=0)
-        products = dot_nt(both, both)
-        for i in range(2):
-            c = step * CB + 2 * pair + i
-            s = products[i * BLK : (i + 1) * BLK, i * BLK : (i + 1) * BLK]
-            cross = side_by_side(s[HALF:, :HALF])
-            triangle = side_by_side(jnp.where(lower, s[:HALF, :HALF], s[HALF:, HALF:]))
-            own_ref[pl.ds(c, 8, stride=CHILDREN_DEV), :] = jnp.where(first, cross, triangle)
-            other_ref[pl.ds(c, 8, stride=CHILDREN_DEV), :] = jnp.where(first, triangle, cross)
-            diag = jnp.sum(jnp.where(diagonal, s[HALF:], 0.0), axis=0, keepdims=True)
-            zero = jnp.zeros((1, BLK), F32)
-            named = zero + (block_ref[c] + 1).astype(F32)
-            own_ref[pl.ds(8 * CHILDREN_DEV + c, 1), :] = jnp.concatenate([diag, named], axis=1)
-            other_ref[pl.ds(8 * CHILDREN_DEV + c, 1), :] = jnp.concatenate([diag, zero], axis=1)
-            p = parent_ref[c]
-            k = count_ref[p]
-            count_ref[p] = k + 1
-            group = (p // (NZ * NX)) * NX + p % NX
-            slot = group * SLOTS + ((p // NX) % NZ) * 2 + k
-            onehot_ref[pl.ds(c, 1), :] = jnp.where(slots == slot, 1.0, 0.0)
+    def copies(step):
+        part = pl.ds(step * CB, CB)
+        return (
+            pltpu.make_async_copy(modes_hbm.at[part], modes_ref.at[part], modes_sem.at[step]),
+            pltpu.make_async_copy(coupling_hbm.at[part], coupling_ref.at[part], coupling_sem.at[step]),
+        )
+
+    for step in range(STEPS):
+        for copy in copies(step):
+            copy.start()
+    for p in range(NG * NZ):
+        count_ref[p] = 0
+
+    @pl.loop(0, STEPS)
+    def _(step):
+        for copy in copies(step):
+            copy.wait()
+        weights = weights_ref[pl.ds(pl.multiple_of(step * CB, CB), CB), :].astype(F32)
+        for pair in range(CB // 2):
+            records = []
+            for j in (2 * pair, 2 * pair + 1):
+                c = step * CB + j
+                top = modes_ref[c, pl.ds(pl.multiple_of(pairs_ref[0, c] * BLK, BLK), BLK), :]
+                bottom = modes_ref[c, pl.ds(pl.multiple_of(pairs_ref[1, c] * BLK, BLK), BLK), :]
+                record = dot(coupling_ref[c], jnp.concatenate([top, bottom], axis=0))
+                record = (record * weights[j : j + 1, :]).astype(BF)
+                record_ref[c] = record
+                records.append(record)
+            both = jnp.concatenate(records, axis=0)
+            products = dot_nt(both, both)
+            for i in range(2):
+                c = step * CB + 2 * pair + i
+                s = products[i * BLK : (i + 1) * BLK, i * BLK : (i + 1) * BLK]
+                cross = side_by_side(s[HALF:, :HALF])
+                triangle = side_by_side(jnp.where(lower, s[:HALF, :HALF], s[HALF:, HALF:]))
+                own_ref[pl.ds(c, 8, stride=CHILDREN_DEV), :] = jnp.where(first, cross, triangle)
+                other_ref[pl.ds(c, 8, stride=CHILDREN_DEV), :] = jnp.where(first, triangle, cross)
+                diag = jnp.sum(jnp.where(diagonal, s[HALF:], 0.0), axis=0, keepdims=True)
+                zero = jnp.zeros((1, BLK), F32)
+                named = zero + (block_ref[c] + 1).astype(F32)
+                own_ref[pl.ds(8 * CHILDREN_DEV + c, 1), :] = jnp.concatenate([diag, named], axis=1)
+                other_ref[pl.ds(8 * CHILDREN_DEV + c, 1), :] = jnp.concatenate([diag, zero], axis=1)
+                p = parent_ref[c]
+                k = count_ref[p]
+                count_ref[p] = k + 1
+                group = (p // (NZ * NX)) * NX + p % NX
+                slot = group * SLOTS + ((p // NX) % NZ) * 2 + k
+                for h in range(2):
+                    hit = jnp.where(slots == slot - 128 * h, 1.0, 0.0)
+                    own_ref[pl.ds((9 + h) * CHILDREN_DEV + c, 1), :] = hit
 
 
 def moments(core, pairs, parent, block, coupling, modes, weights):
-    whole = (9 * CHILDREN_DEV, 128)
-    onehot = (CHILDREN_DEV, NG * SLOTS)
+    hbm = pl.BlockSpec(memory_space=pltpu.HBM)
     return pl.pallas_call(
         moments_kernel,
-        grid=(STEPS,),
-        in_specs=[
-            SMEM,
-            SMEM,
-            SMEM,
-            SMEM,
-            pl.BlockSpec((CB, BLK, 128), lambda i: (i, 0, 0)),
-            pl.BlockSpec((CB, 256, 128), lambda i: (i, 0, 0)),
-            pl.BlockSpec((CB, 128), lambda i: (i, 0)),
-        ],
-        out_specs=[
-            pl.BlockSpec((CB, BLK, 128), lambda i: (i, 0, 0)),
-            pl.BlockSpec(whole, lambda i: (0, 0)),
-            pl.BlockSpec(whole, lambda i: (0, 0)),
-            pl.BlockSpec(onehot, lambda i: (0, 0)),
-        ],
+        in_specs=[SMEM, SMEM, SMEM, SMEM, hbm, hbm, VMEM],
+        out_specs=[VMEM, VMEM, VMEM],
         out_shape=[
             jax.ShapeDtypeStruct((CHILDREN_DEV, BLK, 128), BF),
-            jax.ShapeDtypeStruct(whole, F32),
-            jax.ShapeDtypeStruct(whole, F32),
-            jax.ShapeDtypeStruct(onehot, F32),
+            jax.ShapeDtypeStruct((11 * CHILDREN_DEV, 128), F32),
+            jax.ShapeDtypeStruct((9 * CHILDREN_DEV, 128), F32),
         ],
-        scratch_shapes=[pltpu.SMEM((NG * NZ,), jnp.int32)],
+        scratch_shapes=[
+            pltpu.VMEM((CHILDREN_DEV, BLK, 128), BF),
+            pltpu.VMEM((CHILDREN_DEV, 256, 128), BF),
+            pltpu.SMEM((NG * NZ,), jnp.int32),
+            pltpu.SemaphoreType.DMA((STEPS,)),
+            pltpu.SemaphoreType.DMA((STEPS,)),
+        ],
         compiler_params=params(60),
         name="child_moments",
     )(core, pairs, parent, block, coupling, modes, weights)
 
 
-def dispatch_kernel(onehot_ref, own_ref, recv_ref, out_ref):
-    place = onehot_ref[...].T.astype(BF)
+def message_row(i, k):
+    return k * 8 + i if i < 8 else 16 + k
+
+
+def every_device(i, k):
+    return pl.ds(message_row(i, k), PARENTS, stride=ROWS)
+
+
+def stage_kernel(own_ref, sums_ref, place_ref, onehot_ref):
+    sums_ref[...] = own_ref[: 9 * CHILDREN_DEV, :]
+    onehot = jnp.concatenate(
+        [own_ref[9 * CHILDREN_DEV : 10 * CHILDREN_DEV, :], own_ref[10 * CHILDREN_DEV :, :]], axis=1
+    )
+    place_ref[...] = onehot.T.astype(BF)
+    onehot_ref[...] = onehot.astype(BF)
+
+
+def stage(own):
+    return pl.pallas_call(
+        stage_kernel,
+        in_specs=[VMEM],
+        out_specs=[VMEM, VMEM, VMEM],
+        out_shape=[
+            jax.ShapeDtypeStruct((9 * CHILDREN_DEV, 128), F32),
+            jax.ShapeDtypeStruct((NG * SLOTS, CHILDREN_DEV), BF),
+            jax.ShapeDtypeStruct((CHILDREN_DEV, NG * SLOTS), BF),
+        ],
+        compiler_params=params(16),
+        name="stage",
+    )(own)
+
+
+def dispatch_kernel(place_ref, own_ref, recv_ref, out_ref):
+    place = place_ref[...]
     for i in range(9):
         rows = slice(i * CHILDREN_DEV, (i + 1) * CHILDREN_DEV)
         values = (own_ref[rows, :] + recv_ref[rows, :]).astype(BF)
         out_ref[:, i * SLOTS : (i + 1) * SLOTS, :] = dot(place, values).astype(BF).reshape(NG, SLOTS, 128)
 
 
-def dispatch(onehot, own, recv):
+def dispatch(place, own, recv):
     return pl.pallas_call(
         dispatch_kernel,
         in_specs=[VMEM, VMEM, VMEM],
@@ -161,7 +197,7 @@
         out_shape=jax.ShapeDtypeStruct((NG, ROWS, 128), BF),
         compiler_params=params(16),
         name="dispatch",
-    )(onehot, own, recv)
+    )(place, own, recv)
 
 
 def bin_kernel(recv_ref, out_ref, onehot_ref):
@@ -198,53 +234,68 @@
     )(recv)
 
 
+def wide(x):
+    return jnp.concatenate([x, x], axis=1)
+
+
+def pivot_block(c, j):
+    a00, a01, a11 = c[0][j : j + 1], c[1][j : j + 1], c[1][j + 1 : j + 2]
+    a02, a12, a22 = c[2][j : j + 1], c[2][j + 1 : j + 2], c[2][j + 2 : j + 3]
+    a03, a13, a23 = c[3][j : j + 1], c[3][j + 1 : j + 2], c[3][j + 2 : j + 3]
+    a33 = c[3][j + 3 : j + 4]
+    scale = 1.0 / (a00 * a11 - a01 * a01)
+    p00, p01, p11 = a11 * scale, -a01 * scale, a00 * scale
+    t00, t10 = p00 * a02 + p01 * a12, p01 * a02 + p11 * a12
+    t01, t11 = p00 * a03 + p01 * a13, p01 * a03 + p11 * a13
+    s00 = a22 - (a02 * t00 + a12 * t10)
+    s01 = a23 - (a02 * t01 + a12 * t11)
+    s11 = a33 - (a03 * t01 + a13 * t11)
+    scale = 1.0 / (s00 * s11 - s01 * s01)
+    return p00, p01, p11, t00, t10, t01, t11, s11 * scale, -s01 * scale, s00 * scale
+
+
+def solve_block(block, p):
+    p00, p01, p11, t00, t10, t01, t11, q00, q01, q11 = block
+    u2 = p[2] - (t00 * p[0] + t10 * p[1])
+    u3 = p[3] - (t01 * p[0] + t11 * p[1])
+    x2, x3 = q00 * u2 + q01 * u3, q01 * u2 + q11 * u3
+    x0 = (p00 * p[0] + p01 * p[1]) - (t00 * x2 + t01 * x3)
+    x1 = (p01 * p[0] + p11 * p[1]) - (t10 * x2 + t11 * x3)
+    return x0, x1, x2, x3
+
+
+def eliminate(row, j, rest, c, x):
+    rest = rest - ((c[0] * x[0] + c[1] * x[1]) + (c[2] * x[2] + c[3] * x[3]))
+    low = jnp.where(row == j, x[0], jnp.where(row == j + 1, x[1], rest))
+    return jnp.where(row == j + 2, x[2], jnp.where(row == j + 3, x[3], low))
+
+
 def invert(a_ref):
     lane = lax.broadcasted_iota(jnp.int32, (PB, MP), 1)
     row = lax.broadcasted_iota(jnp.int32, (PB, MP), 0)
     lane_all = lax.broadcasted_iota(jnp.int32, (MP, MP), 1)
     line = lane[:1]
-
-    def wide(x):
-        return jnp.concatenate([x, x], axis=1)
-
     for b in range(MP // PB):
         r = b * PB
         panel = a_ref[r : r + PB, :]
-        for j in range(0, PB, 4):
-            k = r + j
-            inside = (line >= k) & (line < k + 4)
-            c = [jnp.broadcast_to(panel[:, k + i : k + i + 1], (PB, 128)) for i in range(4)]
-            p = [
-                jnp.where(line == k + i, 1.0, jnp.where(inside, 0.0, panel[j + i : j + i + 1]))
-                for i in range(4)
-            ]
-            a00, a01, a11 = c[0][j : j + 1], c[1][j : j + 1], c[1][j + 1 : j + 2]
-            a02, a12, a22 = c[2][j : j + 1], c[2][j + 1 : j + 2], c[2][j + 2 : j + 3]
-            a03, a13, a23 = c[3][j : j + 1], c[3][j + 1 : j + 2], c[3][j + 2 : j + 3]
-            a33 = c[3][j + 3 : j + 4]
-            scale = 1.0 / (a00 * a11 - a01 * a01)
-            p00, p01, p11 = a11 * scale, -a01 * scale, a00 * scale
-            t00, t10 = p00 * a02 + p01 * a12, p01 * a02 + p11 * a12
-            t01, t11 = p00 * a03 + p01 * a13, p01 * a03 + p11 * a13
-            s00 = a22 - (a02 * t00 + a12 * t10)
-            s01 = a23 - (a02 * t01 + a12 * t11)
-            s11 = a33 - (a03 * t01 + a13 * t11)
-            scale = 1.0 / (s00 * s11 - s01 * s01)
-            q00, q01, q11 = s11 * scale, -s01 * scale, s00 * scale
-            t00, t10, t01, t11 = wide(t00), wide(t10), wide(t01), wide(t11)
-            p00, p01, p11 = wide(p00), wide(p01), wide(p11)
-            q00, q01, q11 = wide(q00), wide(q01), wide(q11)
-            u2 = p[2] - (t00 * p[0] + t10 * p[1])
-            u3 = p[3] - (t01 * p[0] + t11 * p[1])
-            x2, x3 = q00 * u2 + q01 * u3, q01 * u2 + q11 * u3
-            x0 = (p00 * p[0] + p01 * p[1]) - (t00 * x2 + t01 * x3)
-            x1 = (p01 * p[0] + p11 * p[1]) - (t10 * x2 + t11 * x3)
-            c = [wide(v) for v in c]
-            rest = jnp.where((lane >= k) & (lane < k + 4), 0.0, panel) - (
-                (c[0] * x0 + c[1] * x1) + (c[2] * x2 + c[3] * x3)
-            )
-            low = jnp.where(row == j, x0, jnp.where(row == j + 1, x1, rest))
-            panel = jnp.where(row == j + 2, x2, jnp.where(row == j + 3, x3, low))
+        for j8 in range(0, PB, 8):
+            c = [jnp.broadcast_to(panel[:, r + j8 + i : r + j8 + i + 1], (PB, 128)) for i in range(8)]
+            for h in (0, 4):
+                j = j8 + h
+                k = r + j
+                lead = c[h : h + 4]
+                block = pivot_block(lead, j)
+                for m in range(h + 4, 8):
+                    x = solve_block(block, [c[m][j + i : j + i + 1] for i in range(4)])
+                    c[m] = eliminate(row[:, :128], j, c[m], lead, x)
+                inside = (line >= k) & (line < k + 4)
+                p = [
+                    jnp.where(line == k + i, 1.0, jnp.where(inside, 0.0, panel[j + i : j + i + 1]))
+                    for i in range(4)
+                ]
+                x = solve_block([wide(v) for v in block], p)
+                rest = jnp.where((lane >= k) & (lane < k + 4), 0.0, panel)
+                panel = eliminate(row, j, rest, [wide(v) for v in lead], x)
         ch, cm, cl = split3(a_ref[:, r : r + PB])
         ph, pm, pw = split3(panel)
         update = dot(
@@ -363,7 +414,7 @@
 
 
 def collect_kernel(onehot_ref, recv_ref, out_ref):
-    onehot = onehot_ref[...].astype(BF)
+    onehot = onehot_ref[...]
     for i in range(9):
         values = recv_ref[:, i * SLOTS : (i + 1) * SLOTS, :].reshape(NG * SLOTS, 128)
         out_ref[i * CHILDREN_DEV : (i + 1) * CHILDREN_DEV, :] = dot(onehot, values).astype(BF)
@@ -443,8 +494,9 @@
 def per_device(coupling, pairs, modes, weights, parent_of, row_block, parent_modes, parent_eigs):
     core = lax.axis_index("mode").astype(jnp.int32).reshape(1)
     parent = parent_of.reshape(CHILDREN_DEV)
-    record, own, other, onehot = moments(core, pairs.T, parent, row_block, coupling, modes, weights)
-    sent = dispatch(onehot, own, swap(other))
+    record, own, other = moments(core, pairs.T, parent, row_block, coupling, modes, weights)
+    sums, place, onehot = stage(own)
+    sent = dispatch(place, sums, swap(other))
     binned, chosen = bin_slots(exchange(sent, ("y", "x")))
     bins = exchange(binned, "z")
     blocks = pencil_blocks(core, bins, swap(bins), parent_modes[0], parent_eigs)

time: 93.6 us -> 89.4 us (0.955)
  Pallas kernels: 21.1 us -> 18.9 us
  waiting for transfers between devices: 3.46 us -> 2.35 us
    pallas_call x1, Pallas kernels: 11.5 us -> 9.99 us  [pencil_blocks(): pl.pallas_call(pencil_kernel, in_specs=[SMEM, VMEM, VMEM, VMEM, VMEM], ou...]
    ppermute x3, waiting for transfers between devices: 3.46 us -> 2.35 us  [swap(): return lax.ppermute(x, 'mode', [(0, 1), (1, 0)])]
    pallas_call x1 -> x2, Pallas kernels: 6.15 us -> 6.13 us  [the longest x1 6.02 us: moments(): pl.pallas_call(moments_kernel, in_specs=[SMEM, SMEM, SMEM, SMEM, hbm, hbm...]
where the time goes in v4:
time: 89.4 us; the launch traced here: 89.1 us
  blocking collectives  57.5 us (64%)
  Pallas kernels  18.9 us (21%)
  starting transfers between devices  9.28 us (10%)
  waiting for transfers between devices  2.35 us (3%)
  local copies, waits for them, and re-layouts  1 us (1%)
    all_to_all x4, blocking collectives, exchange(): return lax.all_to_all(x, axes, split_axis=0, concat_axis=0, tiled=True)  57.5 us
    pallas_call x1, Pallas kernels, pencil_blocks(): pl.pallas_call(pencil_kernel, in_specs=[SMEM, VMEM, VMEM, VMEM, VMEM], ou...  9.99 us
    ppermute x3, starting transfers between devices, swap(): return lax.ppermute(x, 'mode', [(0, 1), (1, 0)])  9.28 us
    pallas_call x1, Pallas kernels, moments(): pl.pallas_call(moments_kernel, in_specs=[SMEM, SMEM, SMEM, SMEM, hbm, hbm...  6.02 us
    ppermute x3, waiting for transfers between devices, swap(): return lax.ppermute(x, 'mode', [(0, 1), (1, 0)])  2.35 us
  transfers between devices with their start and end apart: 3, of which 3 were waited for; matrix products, arithmetic and copies ran while one was open for 0% of the time, Pallas kernels for 0%

profile of v4, /device:TPU:1, one launch (start us, length us, event | category | flops | bytes accessed | tf_op | source)
XLA Modules:
  0.0 89.1 jit_solution(1928272093791737479)
XLA Ops:
  0.0 0.0 copy-start.2
  0.0 0.0 copy-start.3
  0.0 6.0 %child_moments.1 = (bf16[64,64,128]{2,1,0:T(8,128)(2,1)}, f32[704,128]{1,0:T(8,128)}, f32[576,128]{1,0:T(8,128)}) custom-call(s32[1]{0:T(128)} %bitcast.core_ref, s32[2,64]{1,0:T(2,128)} %bitcast.5, s32[64]{0:T(128)} %bitcast.6, s32[64]{0:T(128)} %block_ref.1, bf16[64,64,128]{2,1,0:T(8,128)(2,1)} %coupling_hbm.1, bf16[64,256,128]{2,1,0:T(8,128)(2,1)} %modes_hbm.1, ...), custom_call_target="tpu_custom_call" | custom-call | tf_op jit(solution)/shard_map/child_moments/pallas_call | solution.py:131
  6.0 0.0 copy-start
  6.0 3.3 %collective-permute-start = (f32[576,128]{1,0:T(8,128)}, f32[576,128]{1,0:T(8,128)S(1)}, u32[]{:S(2)}, u32[]{:S(2)}) collective-permute-start(f32[576,128]{1,0:T(8,128)} %get-tuple-element.17), channel_id=1, source_target_pairs={{0,1},{1,0},{2,3},{3,2},{4,5},{5,4},{6,7},{7,6},{8,9},{9,8},{10,11... | collective-permute-start | bytes 884744 | tf_op jit(solution)/shard_map/ppermute | solution.py:487
  9.4 0.0 copy-start.1
  9.4 1.0 %copy-done.1 = f32[704,128]{1,0:T(8,128)S(1)} copy-done((f32[704,128]{1,0:T(8,128)S(1)}, f32[704,128]{1,0:T(8,128)}, u32[]{:S(2)}) %copy-start.1) | copy-done | bytes 360472
  10.4 0.1 stage.1
  10.5 0.3 collective-permute-done.recv_ref
  10.8 0.3 dispatch.1
  11.1 16.2 %all_to_all.20.recv_ref = bf16[16,144,128]{2,1,0:T(8,128)(2,1)S(1)} all-to-all(bf16[16,144,128]{2,1,0:T(8,128)(2,1)S(1)} %dispatch.1), channel_id=1, replica_groups=mesh['y'=4,'z'=8,'x'=4,'mode'=2] {'y','x'}, dimensions={0} | all-to-all | bytes 1179648 | tf_op jit(solution)/shard_map/all_to_all | solution.py:491
  27.3 0.4 bin_slots.1
  27.7 16.4 %all_to_all.21.mine_ref = bf16[8,80,128]{2,1,0:T(8,128)(2,1)S(1)} all-to-all(bf16[8,80,128]{2,1,0:T(8,128)(2,1)S(1)} %get-tuple-element.18), channel_id=1, replica_groups=mesh['y'=4,'z'=8,'x'=4,'mode'=2] {'z'}, dimensions={0} | all-to-all | bytes 327680 | tf_op jit(solution)/shard_map/all_to_all | solution.py:491
  44.1 3.1 %collective-permute-start.1 = (bf16[8,80,128]{2,1,0:T(8,128)(2,1)S(1)}, bf16[8,80,128]{2,1,0:T(8,128)(2,1)S(1)}, u32[]{:S(2)}, u32[]{:S(2)}) collective-permute-start(bf16[8,80,128]{2,1,0:T(8,128)(2,1)S(1)} %all_to_all.21.mine_ref), channel_id=1, source_target_pairs={{0,1},{1,0},{2,3},{3,2},{4,5},{5,4},{6,7},{7,6},{8,9},{9,8},{10,11... | collective-permute-start | bytes 491528 | tf_op jit(solution)/shard_map/ppermute | solution.py:487
  47.2 1.0 %collective-permute-done.1.theirs_ref = bf16[8,80,128]{2,1,0:T(8,128)(2,1)S(1)} collective-permute-done((bf16[8,80,128]{2,1,0:T(8,128)(2,1)S(1)}, bf16[8,80,128]{2,1,0:T(8,128)(2,1)S(1)}, u32[]{:S(2)}, u32[]{:S(2)}) %collective-permute-start.1) | collective-permute-done | bytes 163872 | tf_op jit(solution)/shard_map/ppermute | solution.py:487
  48.2 0.0 copy-done.2
  48.2 0.0 copy-done.3
  48.2 10.0 %pencil_blocks.1 = bf16[8,80,128]{2,1,0:T(8,128)(2,1)S(1)} custom-call(s32[1]{0:T(128)} %bitcast.core_ref, bf16[8,80,128]{2,1,0:T(8,128)(2,1)S(1)} %all_to_all.21.mine_ref, bf16[8,80,128]{2,1,0:T(8,128)(2,1)S(1)} %collective-permute-done.1.theirs_ref, bf16[512,256]{1,0:T(8,128)(2,1)S(1)} %bitcast.4, f32[1,256]{1,0:T(1,128)S(1)} %copy-done.3), custom_call_target="tpu_custom_call" | custom-call | tf_op jit(solution)/shard_map/pencil_blocks/pallas_call | solution.py:379
  58.2 11.5 %all_to_all.22.bins_ref = bf16[8,80,128]{2,1,0:T(8,128)(2,1)S(1)} all-to-all(bf16[8,80,128]{2,1,0:T(8,128)(2,1)S(1)} %pencil_blocks.1), channel_id=1, replica_groups=mesh['y'=4,'z'=8,'x'=4,'mode'=2] {'z'}, dimensions={0} | all-to-all | bytes 327680 | tf_op jit(solution)/shard_map/all_to_all | solution.py:491
  69.8 0.3 select_bins.1
  70.1 13.4 %all_to_all.23.recv_ref = bf16[16,144,128]{2,1,0:T(8,128)(2,1)S(1)} all-to-all(bf16[16,144,128]{2,1,0:T(8,128)(2,1)S(1)} %select_bins.1), channel_id=1, replica_groups=mesh['y'=4,'z'=8,'x'=4,'mode'=2] {'y','x'}, dimensions={0} | all-to-all | bytes 1179648 | tf_op jit(solution)/shard_map/all_to_all | solution.py:491
  83.4 0.2 collect.1.mine_ref
  83.7 2.8 %collective-permute-start.2 = (bf16[576,128]{1,0:T(8,128)(2,1)S(1)}, bf16[576,128]{1,0:T(8,128)(2,1)S(1)}, u32[]{:S(2)}, u32[]{:S(2)}) collective-permute-start(bf16[576,128]{1,0:T(8,128)(2,1)S(1)} %collect.1.mine_ref), channel_id=1, source_target_pairs={{0,1},{1,0},{2,3},{3,2},{4,5},{5,4},{6,7},{7,6},{8,9},{9,8},{10,11... | collective-permute-start | bytes 442376 | tf_op jit(solution)/shard_map/ppermute | solution.py:487
  86.5 1.0 %collective-permute-done.2.theirs_ref = bf16[576,128]{1,0:T(8,128)(2,1)S(1)} collective-permute-done((bf16[576,128]{1,0:T(8,128)(2,1)S(1)}, bf16[576,128]{1,0:T(8,128)(2,1)S(1)}, u32[]{:S(2)}, u32[]{:S(2)}) %collective-permute-start.2) | collective-permute-done | bytes 147488 | tf_op jit(solution)/shard_map/ppermute | solution.py:487
  87.5 0.0 copy-done
  87.5 1.6 %strengths.1 = f32[64,128]{1,0:T(8,128)} custom-call(s32[1]{0:T(128)} %bitcast.core_ref, bf16[576,128]{1,0:T(8,128)(2,1)S(1)} %collect.1.mine_ref, bf16[576,128]{1,0:T(8,128)(2,1)S(1)} %collective-permute-done.2.theirs_ref, bf16[64,64,128]{2,1,0:T(8,128)(2,1)S(1)} %copy-done), custom_call_target="tpu_custom_call" | custom-call | tf_op jit(solution)/shard_map/strengths/pallas_call | solution.py:469
Async XLA Ops:
  0.0 48.2 %copy-start.2 = (bf16[1,512,256]{2,1,0:T(8,128)(2,1)S(1)}, bf16[1,512,256]{2,1,0:T(8,128)(2,1)}, u32[]{:S(2)}) copy-start(bf16[1,512,256]{2,1,0:T(8,128)(2,1)} %param.14) | copy-start | bytes 786436
  0.0 48.2 %copy-start.3 = (f32[1,256]{1,0:T(1,128)S(1)}, f32[1,256]{1,0:T(1,128)}, u32[]{:S(2)}) copy-start(f32[1,256]{1,0:T(1,128)} %eigs_ref.1) | copy-start | bytes 3076
  6.0 81.5 %copy-start = (bf16[64,64,128]{2,1,0:T(8,128)(2,1)S(1)}, bf16[64,64,128]{2,1,0:T(8,128)(2,1)}, u32[]{:S(2)}) copy-start(bf16[64,64,128]{2,1,0:T(8,128)(2,1)} %get-tuple-element.20.record_ref) | copy-start | bytes 3145732
  6.0 4.7 %collective-permute-start = (f32[576,128]{1,0:T(8,128)}, f32[576,128]{1,0:T(8,128)S(1)}, u32[]{:S(2)}, u32[]{:S(2)}) collective-permute-start(f32[576,128]{1,0:T(8,128)} %get-tuple-element.17), channel_id=1, source_target_pairs={{0,1},{1,0},{2,3},{3,2},{4,5},{5,4},{6,7},{7,6},{8,9},{9,8},{10,11... | collective-permute-start | bytes 884744 | tf_op jit(solution)/shard_map/ppermute | solution.py:487
  9.4 1.0 %copy-start.1 = (f32[704,128]{1,0:T(8,128)S(1)}, f32[704,128]{1,0:T(8,128)}, u32[]{:S(2)}) copy-start(f32[704,128]{1,0:T(8,128)} %get-tuple-element.13.own_ref) | copy-start | bytes 1081348
  44.1 4.2 %collective-permute-start.1 = (bf16[8,80,128]{2,1,0:T(8,128)(2,1)S(1)}, bf16[8,80,128]{2,1,0:T(8,128)(2,1)S(1)}, u32[]{:S(2)}, u32[]{:S(2)}) collective-permute-start(bf16[8,80,128]{2,1,0:T(8,128)(2,1)S(1)} %all_to_all.21.mine_ref), channel_id=1, source_target_pairs={{0,1},{1,0},{2,3},{3,2},{4,5},{5,4},{6,7},{7,6},{8,9},{9,8},{10,11... | collective-permute-start | bytes 491528 | tf_op jit(solution)/shard_map/ppermute | solution.py:487
  83.7 3.8 %collective-permute-start.2 = (bf16[576,128]{1,0:T(8,128)(2,1)S(1)}, bf16[576,128]{1,0:T(8,128)(2,1)S(1)}, u32[]{:S(2)}, u32[]{:S(2)}) collective-permute-start(bf16[576,128]{1,0:T(8,128)(2,1)S(1)} %collect.1.mine_ref), channel_id=1, source_target_pairs={{0,1},{1,0},{2,3},{3,2},{4,5},{5,4},{6,7},{7,6},{8,9},{9,8},{10,11... | collective-permute-start | bytes 442376 | tf_op jit(solution)/shard_map/ppermute | solution.py:487

commit v5 on v4

--- a/solution.py
+++ b/solution.py
@@ -62,9 +62,24 @@
 
 
 def moments_kernel(
-    core_ref, pairs_ref, parent_ref, block_ref, coupling_hbm, modes_hbm, weights_ref,
-    record_ref, own_ref, other_ref, coupling_ref, modes_ref, count_ref, coupling_sem, modes_sem,
+    core_ref, pairs_hbm, parent_hbm, block_hbm, coupling_hbm, modes_hbm, weights_hbm,
+    record_hbm, own_hbm, other_hbm,
+    pairs_ref, parent_ref, block_ref, coupling_ref, modes_ref, weights_ref, record_ref, own_ref, other_ref,
+    count_ref, small_sem, coupling_sem, modes_sem, record_sem, result_sem,
 ):
+    small = [
+        pltpu.make_async_copy(source, target, small_sem.at[i])
+        for i, (source, target) in enumerate(
+            (
+                (pairs_hbm, pairs_ref),
+                (parent_hbm, parent_ref),
+                (block_hbm, block_ref),
+                (weights_hbm, weights_ref),
+            )
+        )
+    ]
+    for copy in small:
+        copy.start()
     row = lax.broadcasted_iota(jnp.int32, (HALF, HALF), 0)
     col = lax.broadcasted_iota(jnp.int32, (HALF, HALF), 1)
     lower = row >= col
@@ -81,11 +96,17 @@
             pltpu.make_async_copy(coupling_hbm.at[part], coupling_ref.at[part], coupling_sem.at[step]),
         )
 
+    def record_copy(step):
+        part = pl.ds(step * CB, CB)
+        return pltpu.make_async_copy(record_ref.at[part], record_hbm.at[part], record_sem.at[step])
+
     for step in range(STEPS):
         for copy in copies(step):
             copy.start()
     for p in range(NG * NZ):
         count_ref[p] = 0
+    for copy in small:
+        copy.wait()
 
     @pl.loop(0, STEPS)
     def _(step):
@@ -124,25 +145,47 @@
                 for h in range(2):
                     hit = jnp.where(slots == slot - 128 * h, 1.0, 0.0)
                     own_ref[pl.ds((9 + h) * CHILDREN_DEV + c, 1), :] = hit
+        record_copy(step).start()
+
+    results = (
+        pltpu.make_async_copy(other_ref, other_hbm, result_sem.at[0]),
+        pltpu.make_async_copy(own_ref, own_hbm, result_sem.at[1]),
+    )
+    for copy in results:
+        copy.start()
+    for step in range(STEPS):
+        record_copy(step).wait()
+    for copy in results:
+        copy.wait()
 
 
 def moments(core, pairs, parent, block, coupling, modes, weights):
     hbm = pl.BlockSpec(memory_space=pltpu.HBM)
     return pl.pallas_call(
         moments_kernel,
-        in_specs=[SMEM, SMEM, SMEM, SMEM, hbm, hbm, VMEM],
-        out_specs=[VMEM, VMEM, VMEM],
+        in_specs=[SMEM, hbm, hbm, hbm, hbm, hbm, hbm],
+        out_specs=[hbm, hbm, hbm],
         out_shape=[
             jax.ShapeDtypeStruct((CHILDREN_DEV, BLK, 128), BF),
             jax.ShapeDtypeStruct((11 * CHILDREN_DEV, 128), F32),
             jax.ShapeDtypeStruct((9 * CHILDREN_DEV, 128), F32),
         ],
         scratch_shapes=[
+            pltpu.SMEM((2, CHILDREN_DEV), jnp.int32),
+            pltpu.SMEM((CHILDREN_DEV,), jnp.int32),
+            pltpu.SMEM((CHILDREN_DEV,), jnp.int32),
             pltpu.VMEM((CHILDREN_DEV, BLK, 128), BF),
             pltpu.VMEM((CHILDREN_DEV, 256, 128), BF),
+            pltpu.VMEM((CHILDREN_DEV, 128), BF),
+            pltpu.VMEM((CHILDREN_DEV, BLK, 128), BF),
+            pltpu.VMEM((11 * CHILDREN_DEV, 128), F32),
+            pltpu.VMEM((9 * CHILDREN_DEV, 128), F32),
             pltpu.SMEM((NG * NZ,), jnp.int32),
+            pltpu.SemaphoreType.DMA((4,)),
             pltpu.SemaphoreType.DMA((STEPS,)),
             pltpu.SemaphoreType.DMA((STEPS,)),
+            pltpu.SemaphoreType.DMA((STEPS,)),
+            pltpu.SemaphoreType.DMA((2,)),
         ],
         compiler_params=params(60),
         name="child_moments",
@@ -217,7 +260,9 @@
     zero = jnp.zeros((8, 128), F32)
     for z in range(NZ):
         rows = [bins[8 * z : 8 * z + 8, 128 * i : 128 * (i + 1)] for i in range(9)] + [zero]
-        out_ref[z] = jnp.concatenate(rows, axis=0).astype(BF)
+        message = jnp.concatenate(rows, axis=0).astype(BF)
+        out_ref[2 * z] = message
+        out_ref[2 * z + 1] = message
 
 
 def bin_slots(recv):
@@ -226,7 +271,7 @@
         in_specs=[VMEM],
         out_specs=[VMEM, VMEM],
         out_shape=[
-            jax.ShapeDtypeStruct((NZ, ZROWS, 128), BF),
+            jax.ShapeDtypeStruct((2 * NZ, ZROWS, 128), BF),
             jax.ShapeDtypeStruct((NG * SLOTS, 128), BF),
         ],
         compiler_params=params(16),
@@ -319,26 +364,24 @@
 
 
 def pencil_kernel(
-    core_ref, mine_ref, theirs_ref, q_ref, eigs_ref, out_ref, a_ref, y_ref, pack_ref, own_ref, other_ref
+    core_ref, recv_ref, q_ref, eigs_ref, out_ref, a_ref, y_ref, pack_ref, cross_ref, triangle_ref
 ):
-    for source, target in ((mine_ref, own_ref), (theirs_ref, other_ref)):
-        parts = [source[z].astype(F32) for z in range(NZ)]
+    for half, target in ((0, cross_ref), (1, triangle_ref)):
+        parts = [recv_ref[2 * z + half].astype(F32) for z in range(NZ)]
         while len(parts) > 1:
             parts = [x + y for x, y in zip(parts[::2], parts[1::2])]
         target[...] = parts[0]
     row, col, same = tile_index()
     first = core_ref[0] == 0
     lane8 = lax.broadcasted_iota(jnp.int32, (8, 128), 1)
-    diags = jnp.where(first, other_ref[64:72, :], own_ref[64:72, :])
+    diags = triangle_ref[64:72, :]
     diags = jnp.where((lane8 >= 32) & (lane8 < 64), diags, 0.0)
     diags = diags + pltpu.roll(diags, 32, 1)
     diags = diags + pltpu.roll(diags, 64, 1)
     zero = jnp.zeros((HALF, 128), F32)
     for b in range(SB):
-        own = own_ref[pl.ds(b, 8, stride=8), :]
-        other = other_ref[pl.ds(b, 8, stride=8), :]
-        cross = jnp.where(same, four(jnp.where(first, own, other)), 0.0)
-        triangle = jnp.where(same, four(jnp.where(first, other, own)), 0.0)
+        cross = jnp.where(same, four(cross_ref[pl.ds(b, 8, stride=8), :]), 0.0)
+        triangle = jnp.where(same, four(triangle_ref[pl.ds(b, 8, stride=8), :]), 0.0)
         n11 = jnp.where(row > col, triangle, jnp.where(row == col, 0.5 * triangle, 0.0))
         half = jnp.where(same & (row == col), 0.5 * diags[b : b + 1, :], 0.0)
         n22 = jnp.where(row < col, triangle, half)
@@ -375,10 +418,10 @@
         out_ref[z] = result
 
 
-def pencil_blocks(core, own, other, q, eigs):
+def pencil_blocks(core, recv, q, eigs):
     return pl.pallas_call(
         pencil_kernel,
-        in_specs=[SMEM, VMEM, VMEM, VMEM, VMEM],
+        in_specs=[SMEM, VMEM, VMEM, VMEM],
         out_specs=VMEM,
         out_shape=jax.ShapeDtypeStruct((NZ, ZROWS, 128), BF),
         scratch_shapes=[
@@ -390,7 +433,7 @@
         ],
         compiler_params=params(16),
         name="pencil_blocks",
-    )(core, own, other, q, eigs)
+    )(core, recv, q, eigs)
 
 
 def select_kernel(bins_ref, onehot_ref, out_ref):
@@ -498,8 +541,8 @@
     sums, place, onehot = stage(own)
     sent = dispatch(place, sums, swap(other))
     binned, chosen = bin_slots(exchange(sent, ("y", "x")))
-    bins = exchange(binned, "z")
-    blocks = pencil_blocks(core, bins, swap(bins), parent_modes[0], parent_eigs)
+    bins = exchange(binned, ("z", "mode"))
+    blocks = pencil_blocks(core, bins, parent_modes[0], parent_eigs)
     picked = select_bins(exchange(blocks, "z"), chosen)
     mine = collect(onehot, exchange(picked, ("y", "x")))
     return strengths(core, mine, swap(mine), record)

time: 89.4 us -> 91.2 us (1.020)
  blocking collectives: 57.5 us -> 64.3 us
  starting transfers between devices: 9.28 us -> 6.13 us
  waiting for transfers between devices: 2.35 us -> 1.32 us
    all_to_all x4, blocking collectives: 57.5 us -> 64.3 us  [exchange(): return lax.all_to_all(x, axes, split_axis=0, concat_axis=0, tiled=True)]
    ppermute x3 -> x2, starting transfers between devices: 9.28 us -> 6.13 us  [swap(): return lax.ppermute(x, 'mode', [(0, 1), (1, 0)])]
    ppermute x3 -> x2, waiting for transfers between devices: 2.35 us -> 1.32 us  [swap(): return lax.ppermute(x, 'mode', [(0, 1), (1, 0)])]
  transfers between devices with their start and end apart: 3 -> 2, of which waited for: 3 -> 2; matrix products, arithmetic and copies ran while one was open for 0% -> 0% of each run, Pallas kernels for 0% -> 0%
where the time goes in v5:
time: 91.2 us; the launch traced here: 91 us
  blocking collectives  64.3 us (71%)
  Pallas kernels  18.1 us (20%)
  starting transfers between devices  6.13 us (7%)
  waiting for transfers between devices  1.32 us (1%)
  local copies, waits for them, and re-layouts  1 us (1%)
    all_to_all x4, blocking collectives, exchange(): return lax.all_to_all(x, axes, split_axis=0, concat_axis=0, tiled=True)  64.3 us
    pallas_call x1, Pallas kernels, pencil_blocks(): pl.pallas_call(pencil_kernel, in_specs=[SMEM, VMEM, VMEM, VMEM], out_spec...  9.98 us
    ppermute x2, starting transfers between devices, swap(): return lax.ppermute(x, 'mode', [(0, 1), (1, 0)])  6.13 us
    pallas_call x1, Pallas kernels, moments(): pl.pallas_call(moments_kernel, in_specs=[SMEM, hbm, hbm, hbm, hbm, hbm, h...  5.24 us
  transfers between devices with their start and end apart: 2, of which 2 were waited for; matrix products, arithmetic and copies ran while one was open for 0% of the time, Pallas kernels for 0%

profile of v5, /device:TPU:1, one launch (start us, length us, event | category | flops | bytes accessed | tf_op | source)
XLA Modules:
  0.0 91.0 jit_solution(10983207238217317106)
XLA Ops:
  0.0 0.0 copy-start.2
  0.0 0.0 copy-start.3
  0.0 5.2 %child_moments.1 = (bf16[64,64,128]{2,1,0:T(8,128)(2,1)}, f32[704,128]{1,0:T(8,128)}, f32[576,128]{1,0:T(8,128)}) custom-call(s32[1]{0:T(128)} %bitcast.core_ref, s32[2,64]{1,0:T(2,128)} %bitcast.5, s32[64]{0:T(128)} %bitcast.6, s32[64]{0:T(128)} %block_hbm.1, bf16[64,64,128]{2,1,0:T(8,128)(2,1)} %coupling_hbm.1, bf16[64,256,128]{2,1,0:T(8,128)(2,1)} %modes_hbm.1, ...), custom_call_target="tpu_custom_call" | custom-call | tf_op jit(solution)/shard_map/child_moments/pallas_call | solution.py:164
  5.3 0.0 copy-start
  5.3 3.3 %collective-permute-start = (f32[576,128]{1,0:T(8,128)}, f32[576,128]{1,0:T(8,128)S(1)}, u32[]{:S(2)}, u32[]{:S(2)}) collective-permute-start(f32[576,128]{1,0:T(8,128)} %get-tuple-element.17), channel_id=1, source_target_pairs={{0,1},{1,0},{2,3},{3,2},{4,5},{5,4},{6,7},{7,6},{8,9},{9,8},{10,11... | collective-permute-start | bytes 884744 | tf_op jit(solution)/shard_map/ppermute | solution.py:530
  8.6 0.0 copy-start.1
  8.6 1.0 %copy-done.1 = f32[704,128]{1,0:T(8,128)S(1)} copy-done((f32[704,128]{1,0:T(8,128)S(1)}, f32[704,128]{1,0:T(8,128)}, u32[]{:S(2)}) %copy-start.1) | copy-done | bytes 360472
  9.6 0.1 stage.1
  9.7 0.3 collective-permute-done.recv_ref
  10.0 0.3 dispatch.1
  10.3 16.2 %all_to_all.20.recv_ref = bf16[16,144,128]{2,1,0:T(8,128)(2,1)S(1)} all-to-all(bf16[16,144,128]{2,1,0:T(8,128)(2,1)S(1)} %dispatch.1), channel_id=1, replica_groups=mesh['y'=4,'z'=8,'x'=4,'mode'=2] {'y','x'}, dimensions={0} | all-to-all | bytes 1179648 | tf_op jit(solution)/shard_map/all_to_all | solution.py:534
  26.6 0.4 bin_slots.1
  26.9 23.1 %all_to_all.21.recv_ref = bf16[16,80,128]{2,1,0:T(8,128)(2,1)S(1)} all-to-all(bf16[16,80,128]{2,1,0:T(8,128)(2,1)S(1)} %get-tuple-element.18), channel_id=1, replica_groups=mesh['y'=4,'z'=8,'x'=4,'mode'=2] {'z','mode'}, dimensions={0} | all-to-all | bytes 655360 | tf_op jit(solution)/shard_map/all_to_all | solution.py:534
  50.1 0.0 copy-done.2
  50.1 0.0 copy-done.3
  50.1 10.0 %pencil_blocks.1 = bf16[8,80,128]{2,1,0:T(8,128)(2,1)S(1)} custom-call(s32[1]{0:T(128)} %bitcast.core_ref, bf16[16,80,128]{2,1,0:T(8,128)(2,1)S(1)} %all_to_all.21.recv_ref, bf16[512,256]{1,0:T(8,128)(2,1)S(1)} %bitcast.4, f32[1,256]{1,0:T(1,128)S(1)} %copy-done.3), custom_call_target="tpu_custom_call" | custom-call | tf_op jit(solution)/shard_map/pencil_blocks/pallas_call | solution.py:422
  60.1 11.6 %all_to_all.22.bins_ref = bf16[8,80,128]{2,1,0:T(8,128)(2,1)S(1)} all-to-all(bf16[8,80,128]{2,1,0:T(8,128)(2,1)S(1)} %pencil_blocks.1), channel_id=1, replica_groups=mesh['y'=4,'z'=8,'x'=4,'mode'=2] {'z'}, dimensions={0} | all-to-all | bytes 327680 | tf_op jit(solution)/shard_map/all_to_all | solution.py:534
  71.7 0.3 select_bins.1
  72.0 13.4 %all_to_all.23.recv_ref = bf16[16,144,128]{2,1,0:T(8,128)(2,1)S(1)} all-to-all(bf16[16,144,128]{2,1,0:T(8,128)(2,1)S(1)} %select_bins.1), channel_id=1, replica_groups=mesh['y'=4,'z'=8,'x'=4,'mode'=2] {'y','x'}, dimensions={0} | all-to-all | bytes 1179648 | tf_op jit(solution)/shard_map/all_to_all | solution.py:534
  85.3 0.2 collect.1.mine_ref
  85.5 2.8 %collective-permute-start.1 = (bf16[576,128]{1,0:T(8,128)(2,1)S(1)}, bf16[576,128]{1,0:T(8,128)(2,1)S(1)}, u32[]{:S(2)}, u32[]{:S(2)}) collective-permute-start(bf16[576,128]{1,0:T(8,128)(2,1)S(1)} %collect.1.mine_ref), channel_id=1, source_target_pairs={{0,1},{1,0},{2,3},{3,2},{4,5},{5,4},{6,7},{7,6},{8,9},{9,8},{10,11... | collective-permute-start | bytes 442376 | tf_op jit(solution)/shard_map/ppermute | solution.py:530
  88.4 1.0 %collective-permute-done.1.theirs_ref = bf16[576,128]{1,0:T(8,128)(2,1)S(1)} collective-permute-done((bf16[576,128]{1,0:T(8,128)(2,1)S(1)}, bf16[576,128]{1,0:T(8,128)(2,1)S(1)}, u32[]{:S(2)}, u32[]{:S(2)}) %collective-permute-start.1) | collective-permute-done | bytes 147488 | tf_op jit(solution)/shard_map/ppermute | solution.py:530
  89.4 0.0 copy-done
  89.4 1.6 %strengths.1 = f32[64,128]{1,0:T(8,128)} custom-call(s32[1]{0:T(128)} %bitcast.core_ref, bf16[576,128]{1,0:T(8,128)(2,1)S(1)} %collect.1.mine_ref, bf16[576,128]{1,0:T(8,128)(2,1)S(1)} %collective-permute-done.1.theirs_ref, bf16[64,64,128]{2,1,0:T(8,128)(2,1)S(1)} %copy-done), custom_call_target="tpu_custom_call" | custom-call | tf_op jit(solution)/shard_map/strengths/pallas_call | solution.py:512
Async XLA Ops:
  0.0 50.1 %copy-start.2 = (bf16[1,512,256]{2,1,0:T(8,128)(2,1)S(1)}, bf16[1,512,256]{2,1,0:T(8,128)(2,1)}, u32[]{:S(2)}) copy-start(bf16[1,512,256]{2,1,0:T(8,128)(2,1)} %param.14) | copy-start | bytes 786436
  0.0 50.1 %copy-start.3 = (f32[1,256]{1,0:T(1,128)S(1)}, f32[1,256]{1,0:T(1,128)}, u32[]{:S(2)}) copy-start(f32[1,256]{1,0:T(1,128)} %eigs_ref.1) | copy-start | bytes 3076
  5.3 84.1 %copy-start = (bf16[64,64,128]{2,1,0:T(8,128)(2,1)S(1)}, bf16[64,64,128]{2,1,0:T(8,128)(2,1)}, u32[]{:S(2)}) copy-start(bf16[64,64,128]{2,1,0:T(8,128)(2,1)} %get-tuple-element.20.record_ref) | copy-start | bytes 3145732
  5.3 4.7 %collective-permute-start = (f32[576,128]{1,0:T(8,128)}, f32[576,128]{1,0:T(8,128)S(1)}, u32[]{:S(2)}, u32[]{:S(2)}) collective-permute-start(f32[576,128]{1,0:T(8,128)} %get-tuple-element.17), channel_id=1, source_target_pairs={{0,1},{1,0},{2,3},{3,2},{4,5},{5,4},{6,7},{7,6},{8,9},{9,8},{10,11... | collective-permute-start | bytes 884744 | tf_op jit(solution)/shard_map/ppermute | solution.py:530
  8.6 1.0 %copy-start.1 = (f32[704,128]{1,0:T(8,128)S(1)}, f32[704,128]{1,0:T(8,128)}, u32[]{:S(2)}) copy-start(f32[704,128]{1,0:T(8,128)} %get-tuple-element.13.own_ref) | copy-start | bytes 1081348
  85.5 3.8 %collective-permute-start.1 = (bf16[576,128]{1,0:T(8,128)(2,1)S(1)}, bf16[576,128]{1,0:T(8,128)(2,1)S(1)}, u32[]{:S(2)}, u32[]{:S(2)}) collective-permute-start(bf16[576,128]{1,0:T(8,128)(2,1)S(1)} %collect.1.mine_ref), channel_id=1, source_target_pairs={{0,1},{1,0},{2,3},{3,2},{4,5},{5,4},{6,7},{7,6},{8,9},{9,8},{10,11... | collective-permute-start | bytes 442376 | tf_op jit(solution)/shard_map/ppermute | solution.py:530

commit v6 on v5

--- a/solution.py
+++ b/solution.py
@@ -17,7 +17,7 @@
 SLOTS = 2 * NZ
 ROWS = 9 * SLOTS
 ZROWS = 80
-PB = 32
+PB = 64
 BF = jnp.bfloat16
 F32 = jnp.float32
 VMEM = pl.BlockSpec(memory_space=pltpu.VMEM)
@@ -260,9 +260,7 @@
     zero = jnp.zeros((8, 128), F32)
     for z in range(NZ):
         rows = [bins[8 * z : 8 * z + 8, 128 * i : 128 * (i + 1)] for i in range(9)] + [zero]
-        message = jnp.concatenate(rows, axis=0).astype(BF)
-        out_ref[2 * z] = message
-        out_ref[2 * z + 1] = message
+        out_ref[z] = jnp.concatenate(rows, axis=0).astype(BF)
 
 
 def bin_slots(recv):
@@ -271,7 +269,7 @@
         in_specs=[VMEM],
         out_specs=[VMEM, VMEM],
         out_shape=[
-            jax.ShapeDtypeStruct((2 * NZ, ZROWS, 128), BF),
+            jax.ShapeDtypeStruct((NZ, ZROWS, 128), BF),
             jax.ShapeDtypeStruct((NG * SLOTS, 128), BF),
         ],
         compiler_params=params(16),
@@ -283,7 +281,7 @@
     return jnp.concatenate([x, x], axis=1)
 
 
-def pivot_block(c, j):
+def pivot_block(c, row, j):
     a00, a01, a11 = c[0][j : j + 1], c[1][j : j + 1], c[1][j + 1 : j + 2]
     a02, a12, a22 = c[2][j : j + 1], c[2][j + 1 : j + 2], c[2][j + 2 : j + 3]
     a03, a13, a23 = c[3][j : j + 1], c[3][j + 1 : j + 2], c[3][j + 2 : j + 3]
@@ -296,28 +294,29 @@
     s01 = a23 - (a02 * t01 + a12 * t11)
     s11 = a33 - (a03 * t01 + a13 * t11)
     scale = 1.0 / (s00 * s11 - s01 * s01)
-    return p00, p01, p11, t00, t10, t01, t11, s11 * scale, -s01 * scale, s00 * scale
-
-
-def solve_block(block, p):
-    p00, p01, p11, t00, t10, t01, t11, q00, q01, q11 = block
+    inside = (row >= j) & (row < j + 4)
+    m = [jnp.where(row == j + i, -1.0, jnp.where(inside, 0.0, c[i])) for i in range(4)]
+    m[2] = m[2] - (m[0] * t00 + m[1] * t10)
+    m[3] = m[3] - (m[0] * t01 + m[1] * t11)
+    return (p00, p01, p11), (t00, t10, t01, t11), (s11 * scale, -s01 * scale, s00 * scale), m
+
+
+def eliminate(rest, block, p, spread):
+    (p00, p01, p11), (t00, t10, t01, t11), (q00, q01, q11), m = (
+        [spread(v) for v in part] for part in block
+    )
+    y0, y1 = p00 * p[0] + p01 * p[1], p01 * p[0] + p11 * p[1]
     u2 = p[2] - (t00 * p[0] + t10 * p[1])
     u3 = p[3] - (t01 * p[0] + t11 * p[1])
+    rest = rest - (m[0] * y0 + m[1] * y1)
     x2, x3 = q00 * u2 + q01 * u3, q01 * u2 + q11 * u3
-    x0 = (p00 * p[0] + p01 * p[1]) - (t00 * x2 + t01 * x3)
-    x1 = (p01 * p[0] + p11 * p[1]) - (t10 * x2 + t11 * x3)
-    return x0, x1, x2, x3
-
-
-def eliminate(row, j, rest, c, x):
-    rest = rest - ((c[0] * x[0] + c[1] * x[1]) + (c[2] * x[2] + c[3] * x[3]))
-    low = jnp.where(row == j, x[0], jnp.where(row == j + 1, x[1], rest))
-    return jnp.where(row == j + 2, x[2], jnp.where(row == j + 3, x[3], low))
+    return (rest - m[2] * x2) - m[3] * x3
 
 
 def invert(a_ref):
     lane = lax.broadcasted_iota(jnp.int32, (PB, MP), 1)
     row = lax.broadcasted_iota(jnp.int32, (PB, MP), 0)
+    row_half = row[:, :128]
     lane_all = lax.broadcasted_iota(jnp.int32, (MP, MP), 1)
     line = lane[:1]
     for b in range(MP // PB):
@@ -328,19 +327,17 @@
             for h in (0, 4):
                 j = j8 + h
                 k = r + j
-                lead = c[h : h + 4]
-                block = pivot_block(lead, j)
+                block = pivot_block(c[h : h + 4], row_half, j)
                 for m in range(h + 4, 8):
-                    x = solve_block(block, [c[m][j + i : j + i + 1] for i in range(4)])
-                    c[m] = eliminate(row[:, :128], j, c[m], lead, x)
+                    rest = jnp.where((row_half >= j) & (row_half < j + 4), 0.0, c[m])
+                    c[m] = eliminate(rest, block, [c[m][j + i : j + i + 1] for i in range(4)], lambda v: v)
                 inside = (line >= k) & (line < k + 4)
                 p = [
                     jnp.where(line == k + i, 1.0, jnp.where(inside, 0.0, panel[j + i : j + i + 1]))
                     for i in range(4)
                 ]
-                x = solve_block([wide(v) for v in block], p)
-                rest = jnp.where((lane >= k) & (lane < k + 4), 0.0, panel)
-                panel = eliminate(row, j, rest, [wide(v) for v in lead], x)
+                cleared = ((lane >= k) & (lane < k + 4)) | ((row >= j) & (row < j + 4))
+                panel = eliminate(jnp.where(cleared, 0.0, panel), block, p, wide)
         ch, cm, cl = split3(a_ref[:, r : r + PB])
         ph, pm, pw = split3(panel)
         update = dot(
@@ -364,24 +361,26 @@
 
 
 def pencil_kernel(
-    core_ref, recv_ref, q_ref, eigs_ref, out_ref, a_ref, y_ref, pack_ref, cross_ref, triangle_ref
+    core_ref, mine_ref, theirs_ref, q_ref, eigs_ref, out_ref, a_ref, y_ref, pack_ref, own_ref, other_ref
 ):
-    for half, target in ((0, cross_ref), (1, triangle_ref)):
-        parts = [recv_ref[2 * z + half].astype(F32) for z in range(NZ)]
+    for source, target in ((mine_ref, own_ref), (theirs_ref, other_ref)):
+        parts = [source[z].astype(F32) for z in range(NZ)]
         while len(parts) > 1:
             parts = [x + y for x, y in zip(parts[::2], parts[1::2])]
         target[...] = parts[0]
     row, col, same = tile_index()
     first = core_ref[0] == 0
     lane8 = lax.broadcasted_iota(jnp.int32, (8, 128), 1)
-    diags = triangle_ref[64:72, :]
+    diags = jnp.where(first, other_ref[64:72, :], own_ref[64:72, :])
     diags = jnp.where((lane8 >= 32) & (lane8 < 64), diags, 0.0)
     diags = diags + pltpu.roll(diags, 32, 1)
     diags = diags + pltpu.roll(diags, 64, 1)
     zero = jnp.zeros((HALF, 128), F32)
     for b in range(SB):
-        cross = jnp.where(same, four(cross_ref[pl.ds(b, 8, stride=8), :]), 0.0)
-        triangle = jnp.where(same, four(triangle_ref[pl.ds(b, 8, stride=8), :]), 0.0)
+        own = own_ref[pl.ds(b, 8, stride=8), :]
+        other = other_ref[pl.ds(b, 8, stride=8), :]
+        cross = jnp.where(same, four(jnp.where(first, own, other)), 0.0)
+        triangle = jnp.where(same, four(jnp.where(first, other, own)), 0.0)
         n11 = jnp.where(row > col, triangle, jnp.where(row == col, 0.5 * triangle, 0.0))
         half = jnp.where(same & (row == col), 0.5 * diags[b : b + 1, :], 0.0)
         n22 = jnp.where(row < col, triangle, half)
@@ -418,10 +417,10 @@
         out_ref[z] = result
 
 
-def pencil_blocks(core, recv, q, eigs):
+def pencil_blocks(core, own, other, q, eigs):
     return pl.pallas_call(
         pencil_kernel,
-        in_specs=[SMEM, VMEM, VMEM, VMEM],
+        in_specs=[SMEM, VMEM, VMEM, VMEM, VMEM],
         out_specs=VMEM,
         out_shape=jax.ShapeDtypeStruct((NZ, ZROWS, 128), BF),
         scratch_shapes=[
@@ -433,7 +432,7 @@
         ],
         compiler_params=params(16),
         name="pencil_blocks",
-    )(core, recv, q, eigs)
+    )(core, own, other, q, eigs)
 
 
 def select_kernel(bins_ref, onehot_ref, out_ref):
@@ -541,8 +540,8 @@
     sums, place, onehot = stage(own)
     sent = dispatch(place, sums, swap(other))
     binned, chosen = bin_slots(exchange(sent, ("y", "x")))
-    bins = exchange(binned, ("z", "mode"))
-    blocks = pencil_blocks(core, bins, parent_modes[0], parent_eigs)
+    bins = exchange(binned, "z")
+    blocks = pencil_blocks(core, bins, swap(bins), parent_modes[0], parent_eigs)
     picked = select_bins(exchange(blocks, "z"), chosen)
     mine = collect(onehot, exchange(picked, ("y", "x")))
     return strengths(core, mine, swap(mine), record)

time: 91.2 us -> 88.8 us (0.974)
  blocking collectives: 64.3 us -> 57.5 us
  starting transfers between devices: 6.13 us -> 9.29 us
  waiting for transfers between devices: 1.32 us -> 2.35 us
    all_to_all x4, blocking collectives: 64.3 us -> 57.5 us  [exchange(): return lax.all_to_all(x, axes, split_axis=0, concat_axis=0, tiled=True)]
    ppermute x2 -> x3, starting transfers between devices: 6.13 us -> 9.29 us  [swap(): return lax.ppermute(x, 'mode', [(0, 1), (1, 0)])]
    ppermute x2 -> x3, waiting for transfers between devices: 1.32 us -> 2.35 us  [swap(): return lax.ppermute(x, 'mode', [(0, 1), (1, 0)])]
  transfers between devices with their start and end apart: 2 -> 3, of which waited for: 2 -> 3; matrix products, arithmetic and copies ran while one was open for 0% -> 0% of each run, Pallas kernels for 0% -> 0%
where the time goes in v6:
time: 88.8 us; the launch traced here: 88.5 us
  blocking collectives  57.5 us (65%)
  Pallas kernels  18.3 us (21%)
  starting transfers between devices  9.29 us (10%)
  waiting for transfers between devices  2.35 us (3%)
  local copies, waits for them, and re-layouts  1 us (1%)
    all_to_all x4, blocking collectives, exchange(): return lax.all_to_all(x, axes, split_axis=0, concat_axis=0, tiled=True)  57.5 us
    pallas_call x1, Pallas kernels, pencil_blocks(): pl.pallas_call(pencil_kernel, in_specs=[SMEM, VMEM, VMEM, VMEM, VMEM], ou...  10.2 us
    ppermute x3, starting transfers between devices, swap(): return lax.ppermute(x, 'mode', [(0, 1), (1, 0)])  9.29 us
    pallas_call x1, Pallas kernels, moments(): pl.pallas_call(moments_kernel, in_specs=[SMEM, hbm, hbm, hbm, hbm, hbm, h...  5.24 us
    ppermute x3, waiting for transfers between devices, swap(): return lax.ppermute(x, 'mode', [(0, 1), (1, 0)])  2.35 us
  transfers between devices with their start and end apart: 3, of which 3 were waited for; matrix products, arithmetic and copies ran while one was open for 0% of the time, Pallas kernels for 0%

profile of v6, /device:TPU:1, one launch (start us, length us, event | category | flops | bytes accessed | tf_op | source)
XLA Modules:
  0.0 88.5 jit_solution(9635720693083727625)
XLA Ops:
  0.0 0.0 copy-start.2
  0.0 0.0 copy-start.3
  0.0 5.2 %child_moments.1 = (bf16[64,64,128]{2,1,0:T(8,128)(2,1)}, f32[704,128]{1,0:T(8,128)}, f32[576,128]{1,0:T(8,128)}) custom-call(s32[1]{0:T(128)} %bitcast.core_ref, s32[2,64]{1,0:T(2,128)} %bitcast.5, s32[64]{0:T(128)} %bitcast.6, s32[64]{0:T(128)} %block_hbm.1, bf16[64,64,128]{2,1,0:T(8,128)(2,1)} %coupling_hbm.1, bf16[64,256,128]{2,1,0:T(8,128)(2,1)} %modes_hbm.1, ...), custom_call_target="tpu_custom_call" | custom-call | tf_op jit(solution)/shard_map/child_moments/pallas_call | solution.py:164
  5.2 0.0 copy-start
  5.3 3.3 %collective-permute-start = (f32[576,128]{1,0:T(8,128)}, f32[576,128]{1,0:T(8,128)S(1)}, u32[]{:S(2)}, u32[]{:S(2)}) collective-permute-start(f32[576,128]{1,0:T(8,128)} %get-tuple-element.17), channel_id=1, source_target_pairs={{0,1},{1,0},{2,3},{3,2},{4,5},{5,4},{6,7},{7,6},{8,9},{9,8},{10,11... | collective-permute-start | bytes 884744 | tf_op jit(solution)/shard_map/ppermute | solution.py:529
  8.6 0.0 copy-start.1
  8.6 1.0 %copy-done.1 = f32[704,128]{1,0:T(8,128)S(1)} copy-done((f32[704,128]{1,0:T(8,128)S(1)}, f32[704,128]{1,0:T(8,128)}, u32[]{:S(2)}) %copy-start.1) | copy-done | bytes 360472
  9.6 0.1 stage.1
  9.7 0.3 collective-permute-done.recv_ref
  10.0 0.3 dispatch.1
  10.3 16.2 %all_to_all.20.recv_ref = bf16[16,144,128]{2,1,0:T(8,128)(2,1)S(1)} all-to-all(bf16[16,144,128]{2,1,0:T(8,128)(2,1)S(1)} %dispatch.1), channel_id=1, replica_groups=mesh['y'=4,'z'=8,'x'=4,'mode'=2] {'y','x'}, dimensions={0} | all-to-all | bytes 1179648 | tf_op jit(solution)/shard_map/all_to_all | solution.py:533
  26.5 0.4 bin_slots.1
  26.9 16.4 %all_to_all.21.mine_ref = bf16[8,80,128]{2,1,0:T(8,128)(2,1)S(1)} all-to-all(bf16[8,80,128]{2,1,0:T(8,128)(2,1)S(1)} %get-tuple-element.18), channel_id=1, replica_groups=mesh['y'=4,'z'=8,'x'=4,'mode'=2] {'z'}, dimensions={0} | all-to-all | bytes 327680 | tf_op jit(solution)/shard_map/all_to_all | solution.py:533
  43.3 3.1 %collective-permute-start.1 = (bf16[8,80,128]{2,1,0:T(8,128)(2,1)S(1)}, bf16[8,80,128]{2,1,0:T(8,128)(2,1)S(1)}, u32[]{:S(2)}, u32[]{:S(2)}) collective-permute-start(bf16[8,80,128]{2,1,0:T(8,128)(2,1)S(1)} %all_to_all.21.mine_ref), channel_id=1, source_target_pairs={{0,1},{1,0},{2,3},{3,2},{4,5},{5,4},{6,7},{7,6},{8,9},{9,8},{10,11... | collective-permute-start | bytes 491528 | tf_op jit(solution)/shard_map/ppermute | solution.py:529
  46.4 1.0 %collective-permute-done.1.theirs_ref = bf16[8,80,128]{2,1,0:T(8,128)(2,1)S(1)} collective-permute-done((bf16[8,80,128]{2,1,0:T(8,128)(2,1)S(1)}, bf16[8,80,128]{2,1,0:T(8,128)(2,1)S(1)}, u32[]{:S(2)}, u32[]{:S(2)}) %collective-permute-start.1) | collective-permute-done | bytes 163872 | tf_op jit(solution)/shard_map/ppermute | solution.py:529
  47.4 0.0 copy-done.2
  47.4 0.0 copy-done.3
  47.4 10.2 %pencil_blocks.1 = bf16[8,80,128]{2,1,0:T(8,128)(2,1)S(1)} custom-call(s32[1]{0:T(128)} %bitcast.core_ref, bf16[8,80,128]{2,1,0:T(8,128)(2,1)S(1)} %all_to_all.21.mine_ref, bf16[8,80,128]{2,1,0:T(8,128)(2,1)S(1)} %collective-permute-done.1.theirs_ref, bf16[512,256]{1,0:T(8,128)(2,1)S(1)} %bitcast.4, f32[1,256]{1,0:T(1,128)S(1)} %copy-done.3), custom_call_target="tpu_custom_call" | custom-call | tf_op jit(solution)/shard_map/pencil_blocks/pallas_call | solution.py:421
  57.7 11.5 %all_to_all.22.bins_ref = bf16[8,80,128]{2,1,0:T(8,128)(2,1)S(1)} all-to-all(bf16[8,80,128]{2,1,0:T(8,128)(2,1)S(1)} %pencil_blocks.1), channel_id=1, replica_groups=mesh['y'=4,'z'=8,'x'=4,'mode'=2] {'z'}, dimensions={0} | all-to-all | bytes 327680 | tf_op jit(solution)/shard_map/all_to_all | solution.py:533
  69.2 0.3 select_bins.1
  69.5 13.4 %all_to_all.23.recv_ref = bf16[16,144,128]{2,1,0:T(8,128)(2,1)S(1)} all-to-all(bf16[16,144,128]{2,1,0:T(8,128)(2,1)S(1)} %select_bins.1), channel_id=1, replica_groups=mesh['y'=4,'z'=8,'x'=4,'mode'=2] {'y','x'}, dimensions={0} | all-to-all | bytes 1179648 | tf_op jit(solution)/shard_map/all_to_all | solution.py:533
  82.9 0.2 collect.1.mine_ref
  83.1 2.8 %collective-permute-start.2 = (bf16[576,128]{1,0:T(8,128)(2,1)S(1)}, bf16[576,128]{1,0:T(8,128)(2,1)S(1)}, u32[]{:S(2)}, u32[]{:S(2)}) collective-permute-start(bf16[576,128]{1,0:T(8,128)(2,1)S(1)} %collect.1.mine_ref), channel_id=1, source_target_pairs={{0,1},{1,0},{2,3},{3,2},{4,5},{5,4},{6,7},{7,6},{8,9},{9,8},{10,11... | collective-permute-start | bytes 442376 | tf_op jit(solution)/shard_map/ppermute | solution.py:529
  85.9 1.0 %collective-permute-done.2.theirs_ref = bf16[576,128]{1,0:T(8,128)(2,1)S(1)} collective-permute-done((bf16[576,128]{1,0:T(8,128)(2,1)S(1)}, bf16[576,128]{1,0:T(8,128)(2,1)S(1)}, u32[]{:S(2)}, u32[]{:S(2)}) %collective-permute-start.2) | collective-permute-done | bytes 147488 | tf_op jit(solution)/shard_map/ppermute | solution.py:529
  86.9 0.0 copy-done
  86.9 1.6 %strengths.1 = f32[64,128]{1,0:T(8,128)} custom-call(s32[1]{0:T(128)} %bitcast.core_ref, bf16[576,128]{1,0:T(8,128)(2,1)S(1)} %collect.1.mine_ref, bf16[576,128]{1,0:T(8,128)(2,1)S(1)} %collective-permute-done.2.theirs_ref, bf16[64,64,128]{2,1,0:T(8,128)(2,1)S(1)} %copy-done), custom_call_target="tpu_custom_call" | custom-call | tf_op jit(solution)/shard_map/strengths/pallas_call | solution.py:511
Async XLA Ops:
  0.0 47.4 %copy-start.2 = (bf16[1,512,256]{2,1,0:T(8,128)(2,1)S(1)}, bf16[1,512,256]{2,1,0:T(8,128)(2,1)}, u32[]{:S(2)}) copy-start(bf16[1,512,256]{2,1,0:T(8,128)(2,1)} %param.14) | copy-start | bytes 786436
  0.0 47.4 %copy-start.3 = (f32[1,256]{1,0:T(1,128)S(1)}, f32[1,256]{1,0:T(1,128)}, u32[]{:S(2)}) copy-start(f32[1,256]{1,0:T(1,128)} %eigs_ref.1) | copy-start | bytes 3076
  5.2 81.7 %copy-start = (bf16[64,64,128]{2,1,0:T(8,128)(2,1)S(1)}, bf16[64,64,128]{2,1,0:T(8,128)(2,1)}, u32[]{:S(2)}) copy-start(bf16[64,64,128]{2,1,0:T(8,128)(2,1)} %get-tuple-element.20.record_ref) | copy-start | bytes 3145732
  5.3 4.7 %collective-permute-start = (f32[576,128]{1,0:T(8,128)}, f32[576,128]{1,0:T(8,128)S(1)}, u32[]{:S(2)}, u32[]{:S(2)}) collective-permute-start(f32[576,128]{1,0:T(8,128)} %get-tuple-element.17), channel_id=1, source_target_pairs={{0,1},{1,0},{2,3},{3,2},{4,5},{5,4},{6,7},{7,6},{8,9},{9,8},{10,11... | collective-permute-start | bytes 884744 | tf_op jit(solution)/shard_map/ppermute | solution.py:529
  8.6 1.0 %copy-start.1 = (f32[704,128]{1,0:T(8,128)S(1)}, f32[704,128]{1,0:T(8,128)}, u32[]{:S(2)}) copy-start(f32[704,128]{1,0:T(8,128)} %get-tuple-element.13.own_ref) | copy-start | bytes 1081348
  43.3 4.2 %collective-permute-start.1 = (bf16[8,80,128]{2,1,0:T(8,128)(2,1)S(1)}, bf16[8,80,128]{2,1,0:T(8,128)(2,1)S(1)}, u32[]{:S(2)}, u32[]{:S(2)}) collective-permute-start(bf16[8,80,128]{2,1,0:T(8,128)(2,1)S(1)} %all_to_all.21.mine_ref), channel_id=1, source_target_pairs={{0,1},{1,0},{2,3},{3,2},{4,5},{5,4},{6,7},{7,6},{8,9},{9,8},{10,11... | collective-permute-start | bytes 491528 | tf_op jit(solution)/shard_map/ppermute | solution.py:529
  83.1 3.8 %collective-permute-start.2 = (bf16[576,128]{1,0:T(8,128)(2,1)S(1)}, bf16[576,128]{1,0:T(8,128)(2,1)S(1)}, u32[]{:S(2)}, u32[]{:S(2)}) collective-permute-start(bf16[576,128]{1,0:T(8,128)(2,1)S(1)} %collect.1.mine_ref), channel_id=1, source_target_pairs={{0,1},{1,0},{2,3},{3,2},{4,5},{5,4},{6,7},{7,6},{8,9},{9,8},{10,11... | collective-permute-start | bytes 442376 | tf_op jit(solution)/shard_map/ppermute | solution.py:529

commit v7 on v6

--- a/solution.py
+++ b/solution.py
@@ -17,7 +17,7 @@
 SLOTS = 2 * NZ
 ROWS = 9 * SLOTS
 ZROWS = 80
-PB = 64
+PB = 32
 BF = jnp.bfloat16
 F32 = jnp.float32
 VMEM = pl.BlockSpec(memory_space=pltpu.VMEM)
@@ -40,21 +40,15 @@
     return lax.dot_general(a, b, (((0,), (0,)), ((), ())), preferred_element_type=F32)
 
 
-def four(x):
-    return jnp.concatenate([x, x, x, x], axis=0)
-
-
-def tile_index():
-    row = lax.broadcasted_iota(jnp.int32, (HALF, 128), 0)
-    lane = lax.broadcasted_iota(jnp.int32, (HALF, 128), 1)
-    return row, lane % HALF, (lane // HALF) == (row // 8)
-
-
-def pack(x):
-    lane = lax.broadcasted_iota(jnp.int32, (8, 128), 1)
-    low = jnp.where(lane < 32, x[0:8], x[8:16])
-    high = jnp.where(lane < 96, x[16:24], x[24:32])
-    return jnp.where(lane < 64, low, high)
+def square_index():
+    return (
+        lax.broadcasted_iota(jnp.int32, (HALF, HALF), 0),
+        lax.broadcasted_iota(jnp.int32, (HALF, HALF), 1),
+    )
+
+
+def stacked(x):
+    return jnp.concatenate([x[:, 0:32], x[:, 32:64], x[:, 64:96], x[:, 96:128]], axis=0)
 
 
 def side_by_side(x):
@@ -80,8 +74,7 @@
     ]
     for copy in small:
         copy.start()
-    row = lax.broadcasted_iota(jnp.int32, (HALF, HALF), 0)
-    col = lax.broadcasted_iota(jnp.int32, (HALF, HALF), 1)
+    row, col = square_index()
     lower = row >= col
     diagonal = lax.broadcasted_iota(jnp.int32, (HALF, BLK), 1) == (
         lax.broadcasted_iota(jnp.int32, (HALF, BLK), 0) + HALF
@@ -368,28 +361,21 @@
         while len(parts) > 1:
             parts = [x + y for x, y in zip(parts[::2], parts[1::2])]
         target[...] = parts[0]
-    row, col, same = tile_index()
+    row, col = square_index()
     first = core_ref[0] == 0
-    lane8 = lax.broadcasted_iota(jnp.int32, (8, 128), 1)
-    diags = jnp.where(first, other_ref[64:72, :], own_ref[64:72, :])
-    diags = jnp.where((lane8 >= 32) & (lane8 < 64), diags, 0.0)
-    diags = diags + pltpu.roll(diags, 32, 1)
-    diags = diags + pltpu.roll(diags, 64, 1)
-    zero = jnp.zeros((HALF, 128), F32)
+    diags = jnp.where(first, other_ref[64:72, 32:64], own_ref[64:72, 32:64])
     for b in range(SB):
         own = own_ref[pl.ds(b, 8, stride=8), :]
         other = other_ref[pl.ds(b, 8, stride=8), :]
-        cross = jnp.where(same, four(jnp.where(first, own, other)), 0.0)
-        triangle = jnp.where(same, four(jnp.where(first, other, own)), 0.0)
+        cross = stacked(jnp.where(first, own, other))
+        triangle = stacked(jnp.where(first, other, own))
         n11 = jnp.where(row > col, triangle, jnp.where(row == col, 0.5 * triangle, 0.0))
-        half = jnp.where(same & (row == col), 0.5 * diags[b : b + 1, :], 0.0)
-        n22 = jnp.where(row < col, triangle, half)
-        lhs = jnp.concatenate(
-            [jnp.concatenate([n11, zero], axis=1), jnp.concatenate([cross, n22], axis=1)], axis=0
-        ).astype(BF)
+        n22 = jnp.where(row < col, triangle, jnp.where(row == col, 0.5 * diags[b : b + 1, :], 0.0))
         q1 = q_ref[b * BLK : b * BLK + HALF, :]
         q2 = q_ref[b * BLK + HALF : (b + 1) * BLK, :]
-        y_ref[b * BLK : (b + 1) * BLK, :] = dot(lhs, jnp.concatenate([four(q1), four(q2)], axis=0)).astype(BF)
+        y = dot(jnp.concatenate([n11, cross], axis=0).astype(BF), q1)
+        bottom = y[HALF:] + dot(n22.astype(BF), q2)
+        y_ref[b * BLK : (b + 1) * BLK, :] = jnp.concatenate([y[:HALF], bottom], axis=0).astype(BF)
     x = dot_tn(q_ref[...], y_ref[...])
     r = lax.broadcasted_iota(jnp.int32, (MP, MP), 0)
     c = lax.broadcasted_iota(jnp.int32, (MP, MP), 1)
@@ -401,16 +387,13 @@
     for b in range(SB):
         s = b * BLK
         qb = q_ref[s : s + BLK, :]
-        u = dot_nt(qb, four(y_high[s : s + HALF])) + dot_nt(qb, four(y_low[s : s + HALF]))
-        v = dot_nt(qb[HALF:], four(y_high[s + HALF : s + BLK])) + dot_nt(
-            qb[HALF:], four(y_low[s + HALF : s + BLK])
-        )
-        cross = pack(2.0 * u[HALF:])
-        triangle = pack(
-            jnp.where(row > col, 2.0 * u[:HALF], jnp.where(row == col, u[:HALF], 2.0 * v))
-        )
+        h = dot_nt(qb, y_high[s : s + BLK]) + dot_nt(qb, y_low[s : s + BLK])
+        h11, h22 = h[:HALF, :HALF], h[HALF:, HALF:]
+        cross = side_by_side(2.0 * h[HALF:, :HALF])
+        triangle = side_by_side(jnp.where(row > col, 2.0 * h11, jnp.where(row == col, h11, 2.0 * h22)))
+        diag = jnp.sum(jnp.where(row == col, h22, 0.0), axis=0, keepdims=True)
         pack_ref[pl.ds(b, 8, stride=8), :] = jnp.where(first, cross, triangle)
-        pack_ref[64 + b : 65 + b, :] = jnp.sum(jnp.where(row == col, v, 0.0), axis=0, keepdims=True)
+        pack_ref[64 + b : 65 + b, :] = jnp.concatenate([diag, jnp.zeros((1, 96), F32)], axis=1)
     pack_ref[72:80, :] = jnp.zeros((8, 128), F32)
     result = pack_ref[...].astype(BF)
     for z in range(NZ):
@@ -481,29 +464,24 @@
         own_ref[...] = mine_ref[...].astype(F32)
         other_ref[...] = theirs_ref[...].astype(F32)
 
-    row, col, same = tile_index()
+    row, col = square_index()
     first = core_ref[0] == 0
-    lower = same & (row >= col)
-    upper = same & (row < col)
-    diagonal = same & (row == col)
-    zero = jnp.zeros((HALF, 128), F32)
     for j in range(CB):
         c = step * CB + j
         own = own_ref[pl.ds(c, 8, stride=CHILDREN_DEV), :]
         other = other_ref[pl.ds(c, 8, stride=CHILDREN_DEV), :]
         r = pl.ds(8 * CHILDREN_DEV + c, 1)
-        diag = jnp.where(first, other_ref[r, :], own_ref[r, :])
-        cross = jnp.where(same, four(jnp.where(first, own, other)), 0.0)
-        triangle = four(jnp.where(first, other, own))
-        m11 = jnp.where(lower, triangle, 0.0)
-        m22 = jnp.where(upper, triangle, jnp.where(diagonal, diag, 0.0))
-        lhs = jnp.concatenate(
-            [jnp.concatenate([m11, zero], axis=1), jnp.concatenate([cross, m22], axis=1)], axis=0
-        ).astype(BF)
+        diag = jnp.where(first, other_ref[r, :], own_ref[r, :])[:, :HALF]
+        cross = stacked(jnp.where(first, own, other))
+        triangle = stacked(jnp.where(first, other, own))
+        m11 = jnp.where(row >= col, triangle, 0.0)
+        m22 = jnp.where(row < col, triangle, jnp.where(row == col, diag, 0.0))
         record = record_ref[j]
-        rhs = jnp.concatenate([four(record[:HALF]), four(record[HALF:])], axis=0)
-        rotated = dot(lhs, rhs)
-        out_ref[j : j + 1, :] = jnp.sum(rotated * record.astype(F32), axis=0, keepdims=True)
+        left = dot(jnp.concatenate([m11, cross], axis=0).astype(BF), record[:HALF])
+        right = dot(m22.astype(BF), record[HALF:])
+        wide_record = record.astype(F32)
+        terms = left[:HALF] * wide_record[:HALF] + (left[HALF:] + right) * wide_record[HALF:]
+        out_ref[j : j + 1, :] = jnp.sum(terms, axis=0, keepdims=True)
 
 
 def strengths(core, own, other, record):

time: 88.8 us -> 87.8 us (0.989)
  Pallas kernels: 18.3 us -> 17.4 us
    pallas_call x1, Pallas kernels: 10.2 us -> 9.18 us  [pencil_blocks(): pl.pallas_call(pencil_kernel, in_specs=[SMEM, VMEM, VMEM, VMEM, VMEM], ou...]
where the time goes in v7:
time: 87.8 us; the launch traced here: 87.6 us
  blocking collectives  57.5 us (65%)
  Pallas kernels  17.4 us (20%)
  starting transfers between devices  9.28 us (11%)
  waiting for transfers between devices  2.35 us (3%)
  local copies, waits for them, and re-layouts  1 us (1%)
    all_to_all x4, blocking collectives, exchange(): return lax.all_to_all(x, axes, split_axis=0, concat_axis=0, tiled=True)  57.5 us
    ppermute x3, starting transfers between devices, swap(): return lax.ppermute(x, 'mode', [(0, 1), (1, 0)])  9.28 us
    pallas_call x1, Pallas kernels, pencil_blocks(): pl.pallas_call(pencil_kernel, in_specs=[SMEM, VMEM, VMEM, VMEM, VMEM], ou...  9.18 us
    pallas_call x1, Pallas kernels, moments(): pl.pallas_call(moments_kernel, in_specs=[SMEM, hbm, hbm, hbm, hbm, hbm, h...  5.24 us
    ppermute x3, waiting for transfers between devices, swap(): return lax.ppermute(x, 'mode', [(0, 1), (1, 0)])  2.35 us
  transfers between devices with their start and end apart: 3, of which 3 were waited for; matrix products, arithmetic and copies ran while one was open for 0% of the time, Pallas kernels for 0%

profile of v7, /device:TPU:1, one launch (start us, length us, event | category | flops | bytes accessed | tf_op | source)
XLA Modules:
  0.0 87.6 jit_solution(2836281950581092067)
XLA Ops:
  0.0 0.0 copy-start.2
  0.0 0.0 copy-start.3
  0.0 5.2 %child_moments.1 = (bf16[64,64,128]{2,1,0:T(8,128)(2,1)}, f32[704,128]{1,0:T(8,128)}, f32[576,128]{1,0:T(8,128)}) custom-call(s32[1]{0:T(128)} %bitcast.core_ref, s32[2,64]{1,0:T(2,128)} %bitcast.5, s32[64]{0:T(128)} %bitcast.6, s32[64]{0:T(128)} %block_hbm.1, bf16[64,64,128]{2,1,0:T(8,128)(2,1)} %coupling_hbm.1, bf16[64,256,128]{2,1,0:T(8,128)(2,1)} %modes_hbm.1, ...), custom_call_target="tpu_custom_call" | custom-call | tf_op jit(solution)/shard_map/child_moments/pallas_call | solution.py:157
  5.2 0.0 copy-start
  5.3 3.3 %collective-permute-start = (f32[576,128]{1,0:T(8,128)}, f32[576,128]{1,0:T(8,128)S(1)}, u32[]{:S(2)}, u32[]{:S(2)}) collective-permute-start(f32[576,128]{1,0:T(8,128)} %get-tuple-element.17), channel_id=1, source_target_pairs={{0,1},{1,0},{2,3},{3,2},{4,5},{5,4},{6,7},{7,6},{8,9},{9,8},{10,11... | collective-permute-start | bytes 884744 | tf_op jit(solution)/shard_map/ppermute | solution.py:507
  8.6 0.0 copy-start.1
  8.6 1.0 %copy-done.1 = f32[704,128]{1,0:T(8,128)S(1)} copy-done((f32[704,128]{1,0:T(8,128)S(1)}, f32[704,128]{1,0:T(8,128)}, u32[]{:S(2)}) %copy-start.1) | copy-done | bytes 360472
  9.6 0.1 stage.1
  9.7 0.3 collective-permute-done.recv_ref
  10.0 0.3 dispatch.1
  10.3 16.2 %all_to_all.20.recv_ref = bf16[16,144,128]{2,1,0:T(8,128)(2,1)S(1)} all-to-all(bf16[16,144,128]{2,1,0:T(8,128)(2,1)S(1)} %dispatch.1), channel_id=1, replica_groups=mesh['y'=4,'z'=8,'x'=4,'mode'=2] {'y','x'}, dimensions={0} | all-to-all | bytes 1179648 | tf_op jit(solution)/shard_map/all_to_all | solution.py:511
  26.5 0.4 bin_slots.1
  26.9 16.4 %all_to_all.21.mine_ref = bf16[8,80,128]{2,1,0:T(8,128)(2,1)S(1)} all-to-all(bf16[8,80,128]{2,1,0:T(8,128)(2,1)S(1)} %get-tuple-element.18), channel_id=1, replica_groups=mesh['y'=4,'z'=8,'x'=4,'mode'=2] {'z'}, dimensions={0} | all-to-all | bytes 327680 | tf_op jit(solution)/shard_map/all_to_all | solution.py:511
  43.3 3.1 %collective-permute-start.1 = (bf16[8,80,128]{2,1,0:T(8,128)(2,1)S(1)}, bf16[8,80,128]{2,1,0:T(8,128)(2,1)S(1)}, u32[]{:S(2)}, u32[]{:S(2)}) collective-permute-start(bf16[8,80,128]{2,1,0:T(8,128)(2,1)S(1)} %all_to_all.21.mine_ref), channel_id=1, source_target_pairs={{0,1},{1,0},{2,3},{3,2},{4,5},{5,4},{6,7},{7,6},{8,9},{9,8},{10,11... | collective-permute-start | bytes 491528 | tf_op jit(solution)/shard_map/ppermute | solution.py:507
  46.4 1.0 %collective-permute-done.1.theirs_ref = bf16[8,80,128]{2,1,0:T(8,128)(2,1)S(1)} collective-permute-done((bf16[8,80,128]{2,1,0:T(8,128)(2,1)S(1)}, bf16[8,80,128]{2,1,0:T(8,128)(2,1)S(1)}, u32[]{:S(2)}, u32[]{:S(2)}) %collective-permute-start.1) | collective-permute-done | bytes 163872 | tf_op jit(solution)/shard_map/ppermute | solution.py:507
  47.4 0.0 copy-done.2
  47.4 0.0 copy-done.3
  47.4 9.2 %pencil_blocks.1 = bf16[8,80,128]{2,1,0:T(8,128)(2,1)S(1)} custom-call(s32[1]{0:T(128)} %bitcast.core_ref, bf16[8,80,128]{2,1,0:T(8,128)(2,1)S(1)} %all_to_all.21.mine_ref, bf16[8,80,128]{2,1,0:T(8,128)(2,1)S(1)} %collective-permute-done.1.theirs_ref, bf16[512,256]{1,0:T(8,128)(2,1)S(1)} %bitcast.4, f32[1,256]{1,0:T(1,128)S(1)} %copy-done.3), custom_call_target="tpu_custom_call" | custom-call | tf_op jit(solution)/shard_map/pencil_blocks/pallas_call | solution.py:404
  56.6 11.5 %all_to_all.22.bins_ref = bf16[8,80,128]{2,1,0:T(8,128)(2,1)S(1)} all-to-all(bf16[8,80,128]{2,1,0:T(8,128)(2,1)S(1)} %pencil_blocks.1), channel_id=1, replica_groups=mesh['y'=4,'z'=8,'x'=4,'mode'=2] {'z'}, dimensions={0} | all-to-all | bytes 327680 | tf_op jit(solution)/shard_map/all_to_all | solution.py:511
  68.2 0.3 select_bins.1
  68.5 13.4 %all_to_all.23.recv_ref = bf16[16,144,128]{2,1,0:T(8,128)(2,1)S(1)} all-to-all(bf16[16,144,128]{2,1,0:T(8,128)(2,1)S(1)} %select_bins.1), channel_id=1, replica_groups=mesh['y'=4,'z'=8,'x'=4,'mode'=2] {'y','x'}, dimensions={0} | all-to-all | bytes 1179648 | tf_op jit(solution)/shard_map/all_to_all | solution.py:511
  81.8 0.2 collect.1.mine_ref
  82.1 2.8 %collective-permute-start.2 = (bf16[576,128]{1,0:T(8,128)(2,1)S(1)}, bf16[576,128]{1,0:T(8,128)(2,1)S(1)}, u32[]{:S(2)}, u32[]{:S(2)}) collective-permute-start(bf16[576,128]{1,0:T(8,128)(2,1)S(1)} %collect.1.mine_ref), channel_id=1, source_target_pairs={{0,1},{1,0},{2,3},{3,2},{4,5},{5,4},{6,7},{7,6},{8,9},{9,8},{10,11... | collective-permute-start | bytes 442376 | tf_op jit(solution)/shard_map/ppermute | solution.py:507
  84.9 1.0 %collective-permute-done.2.theirs_ref = bf16[576,128]{1,0:T(8,128)(2,1)S(1)} collective-permute-done((bf16[576,128]{1,0:T(8,128)(2,1)S(1)}, bf16[576,128]{1,0:T(8,128)(2,1)S(1)}, u32[]{:S(2)}, u32[]{:S(2)}) %collective-permute-start.2) | collective-permute-done | bytes 147488 | tf_op jit(solution)/shard_map/ppermute | solution.py:507
  85.9 0.0 copy-done
  85.9 1.7 %strengths.1 = f32[64,128]{1,0:T(8,128)} custom-call(s32[1]{0:T(128)} %bitcast.core_ref, bf16[576,128]{1,0:T(8,128)(2,1)S(1)} %collect.1.mine_ref, bf16[576,128]{1,0:T(8,128)(2,1)S(1)} %collective-permute-done.2.theirs_ref, bf16[64,64,128]{2,1,0:T(8,128)(2,1)S(1)} %copy-done), custom_call_target="tpu_custom_call" | custom-call | tf_op jit(solution)/shard_map/strengths/pallas_call | solution.py:489
Async XLA Ops:
  0.0 47.4 %copy-start.2 = (bf16[1,512,256]{2,1,0:T(8,128)(2,1)S(1)}, bf16[1,512,256]{2,1,0:T(8,128)(2,1)}, u32[]{:S(2)}) copy-start(bf16[1,512,256]{2,1,0:T(8,128)(2,1)} %param.14) | copy-start | bytes 786436
  0.0 47.4 %copy-start.3 = (f32[1,256]{1,0:T(1,128)S(1)}, f32[1,256]{1,0:T(1,128)}, u32[]{:S(2)}) copy-start(f32[1,256]{1,0:T(1,128)} %eigs_ref.1) | copy-start | bytes 3076
  5.2 80.7 %copy-start = (bf16[64,64,128]{2,1,0:T(8,128)(2,1)S(1)}, bf16[64,64,128]{2,1,0:T(8,128)(2,1)}, u32[]{:S(2)}) copy-start(bf16[64,64,128]{2,1,0:T(8,128)(2,1)} %get-tuple-element.20.record_ref) | copy-start | bytes 3145732
  5.3 4.7 %collective-permute-start = (f32[576,128]{1,0:T(8,128)}, f32[576,128]{1,0:T(8,128)S(1)}, u32[]{:S(2)}, u32[]{:S(2)}) collective-permute-start(f32[576,128]{1,0:T(8,128)} %get-tuple-element.17), channel_id=1, source_target_pairs={{0,1},{1,0},{2,3},{3,2},{4,5},{5,4},{6,7},{7,6},{8,9},{9,8},{10,11... | collective-permute-start | bytes 884744 | tf_op jit(solution)/shard_map/ppermute | solution.py:507
  8.6 1.0 %copy-start.1 = (f32[704,128]{1,0:T(8,128)S(1)}, f32[704,128]{1,0:T(8,128)}, u32[]{:S(2)}) copy-start(f32[704,128]{1,0:T(8,128)} %get-tuple-element.13.own_ref) | copy-start | bytes 1081348
  43.3 4.2 %collective-permute-start.1 = (bf16[8,80,128]{2,1,0:T(8,128)(2,1)S(1)}, bf16[8,80,128]{2,1,0:T(8,128)(2,1)S(1)}, u32[]{:S(2)}, u32[]{:S(2)}) collective-permute-start(bf16[8,80,128]{2,1,0:T(8,128)(2,1)S(1)} %all_to_all.21.mine_ref), channel_id=1, source_target_pairs={{0,1},{1,0},{2,3},{3,2},{4,5},{5,4},{6,7},{7,6},{8,9},{9,8},{10,11... | collective-permute-start | bytes 491528 | tf_op jit(solution)/shard_map/ppermute | solution.py:507
  82.1 3.8 %collective-permute-start.2 = (bf16[576,128]{1,0:T(8,128)(2,1)S(1)}, bf16[576,128]{1,0:T(8,128)(2,1)S(1)}, u32[]{:S(2)}, u32[]{:S(2)}) collective-permute-start(bf16[576,128]{1,0:T(8,128)(2,1)S(1)} %collect.1.mine_ref), channel_id=1, source_target_pairs={{0,1},{1,0},{2,3},{3,2},{4,5},{5,4},{6,7},{7,6},{8,9},{9,8},{10,11... | collective-permute-start | bytes 442376 | tf_op jit(solution)/shard_map/ppermute | solution.py:507

commit v8 on v7

--- a/solution.py
+++ b/solution.py
@@ -59,7 +59,7 @@
     core_ref, pairs_hbm, parent_hbm, block_hbm, coupling_hbm, modes_hbm, weights_hbm,
     record_hbm, own_hbm, other_hbm,
     pairs_ref, parent_ref, block_ref, coupling_ref, modes_ref, weights_ref, record_ref, own_ref, other_ref,
-    count_ref, small_sem, coupling_sem, modes_sem, record_sem, result_sem,
+    sent_ref, count_ref, small_sem, coupling_sem, modes_sem, record_sem, result_sem,
 ):
     small = [
         pltpu.make_async_copy(source, target, small_sem.at[i])
@@ -140,8 +140,9 @@
                     own_ref[pl.ds((9 + h) * CHILDREN_DEV + c, 1), :] = hit
         record_copy(step).start()
 
+    sent_ref[...] = other_ref[...].astype(BF)
     results = (
-        pltpu.make_async_copy(other_ref, other_hbm, result_sem.at[0]),
+        pltpu.make_async_copy(sent_ref, other_hbm, result_sem.at[0]),
         pltpu.make_async_copy(own_ref, own_hbm, result_sem.at[1]),
     )
     for copy in results:
@@ -161,7 +162,7 @@
         out_shape=[
             jax.ShapeDtypeStruct((CHILDREN_DEV, BLK, 128), BF),
             jax.ShapeDtypeStruct((11 * CHILDREN_DEV, 128), F32),
-            jax.ShapeDtypeStruct((9 * CHILDREN_DEV, 128), F32),
+            jax.ShapeDtypeStruct((9 * CHILDREN_DEV, 128), BF),
         ],
         scratch_shapes=[
             pltpu.SMEM((2, CHILDREN_DEV), jnp.int32),
@@ -173,6 +174,7 @@
             pltpu.VMEM((CHILDREN_DEV, BLK, 128), BF),
             pltpu.VMEM((11 * CHILDREN_DEV, 128), F32),
             pltpu.VMEM((9 * CHILDREN_DEV, 128), F32),
+            pltpu.VMEM((9 * CHILDREN_DEV, 128), BF),
             pltpu.SMEM((NG * NZ,), jnp.int32),
             pltpu.SemaphoreType.DMA((4,)),
             pltpu.SemaphoreType.DMA((STEPS,)),
@@ -221,7 +223,7 @@
     place = place_ref[...]
     for i in range(9):
         rows = slice(i * CHILDREN_DEV, (i + 1) * CHILDREN_DEV)
-        values = (own_ref[rows, :] + recv_ref[rows, :]).astype(BF)
+        values = (own_ref[rows, :] + recv_ref[rows, :].astype(F32)).astype(BF)
         out_ref[:, i * SLOTS : (i + 1) * SLOTS, :] = dot(place, values).astype(BF).reshape(NG, SLOTS, 128)
 
 

time: 87.8 us -> 87.5 us (level)
  no operation moved by 1% of the time
where the time goes in v8:
time: 87.5 us; the launch traced here: 87.3 us
  blocking collectives  57.5 us (66%)
  Pallas kernels  17.3 us (20%)
  starting transfers between devices  9.27 us (11%)
  waiting for transfers between devices  2.15 us (2%)
  local copies, waits for them, and re-layouts  1 us (1%)
    all_to_all x4, blocking collectives, exchange(): return lax.all_to_all(x, axes, split_axis=0, concat_axis=0, tiled=True)  57.5 us
    ppermute x3, starting transfers between devices, swap(): return lax.ppermute(x, 'mode', [(0, 1), (1, 0)])  9.27 us
    pallas_call x1, Pallas kernels, pencil_blocks(): pl.pallas_call(pencil_kernel, in_specs=[SMEM, VMEM, VMEM, VMEM, VMEM], ou...  9.18 us
    pallas_call x1, Pallas kernels, moments(): pl.pallas_call(moments_kernel, in_specs=[SMEM, hbm, hbm, hbm, hbm, hbm, h...  5.17 us
    ppermute x3, waiting for transfers between devices, swap(): return lax.ppermute(x, 'mode', [(0, 1), (1, 0)])  2.15 us
  transfers between devices with their start and end apart: 3, of which 3 were waited for; matrix products, arithmetic and copies ran while one was open for 0% of the time, Pallas kernels for 0%

profile of v8, /device:TPU:1, one launch (start us, length us, event | category | flops | bytes accessed | tf_op | source)
XLA Modules:
  0.0 87.3 jit_solution(575464752237546134)
XLA Ops:
  0.0 0.0 copy-start.2
  0.0 0.0 copy-start.3
  0.0 5.2 %child_moments.1 = (bf16[64,64,128]{2,1,0:T(8,128)(2,1)}, f32[704,128]{1,0:T(8,128)}, bf16[576,128]{1,0:T(8,128)(2,1)}) custom-call(s32[1]{0:T(128)} %bitcast.core_ref, s32[2,64]{1,0:T(2,128)} %bitcast.5, s32[64]{0:T(128)} %bitcast.6, s32[64]{0:T(128)} %block_hbm.1, bf16[64,64,128]{2,1,0:T(8,128)(2,1)} %coupling_hbm.1, bf16[64,256,128]{2,1,0:T(8,128)(2,1)} %modes_hbm.1, ...), custom_call_target="tpu_custom_call" | custom-call | tf_op jit(solution)/shard_map/child_moments/pallas_call | solution.py:158
  5.2 0.0 copy-start
  5.2 3.3 %collective-permute-start = (bf16[576,128]{1,0:T(8,128)(2,1)}, bf16[576,128]{1,0:T(8,128)(2,1)S(1)}, u32[]{:S(2)}, u32[]{:S(2)}) collective-permute-start(bf16[576,128]{1,0:T(8,128)(2,1)} %get-tuple-element.17), channel_id=1, source_target_pairs={{0,1},{1,0},{2,3},{3,2},{4,5},{5,4},{6,7},{7,6},{8,9},{9,8},{10,11... | collective-permute-start | bytes 442376 | tf_op jit(solution)/shard_map/ppermute | solution.py:509
  8.5 0.0 copy-start.1
  8.5 1.0 %copy-done.1 = f32[704,128]{1,0:T(8,128)S(1)} copy-done((f32[704,128]{1,0:T(8,128)S(1)}, f32[704,128]{1,0:T(8,128)}, u32[]{:S(2)}) %copy-start.1) | copy-done | bytes 360472
  9.5 0.1 stage.1
  9.6 0.1 collective-permute-done.recv_ref
  9.7 0.3 dispatch.1
  10.0 16.2 %all_to_all.20.recv_ref = bf16[16,144,128]{2,1,0:T(8,128)(2,1)S(1)} all-to-all(bf16[16,144,128]{2,1,0:T(8,128)(2,1)S(1)} %dispatch.1), channel_id=1, replica_groups=mesh['y'=4,'z'=8,'x'=4,'mode'=2] {'y','x'}, dimensions={0} | all-to-all | bytes 1179648 | tf_op jit(solution)/shard_map/all_to_all | solution.py:513
  26.3 0.4 bin_slots.1
  26.6 16.4 %all_to_all.21.mine_ref = bf16[8,80,128]{2,1,0:T(8,128)(2,1)S(1)} all-to-all(bf16[8,80,128]{2,1,0:T(8,128)(2,1)S(1)} %get-tuple-element.18), channel_id=1, replica_groups=mesh['y'=4,'z'=8,'x'=4,'mode'=2] {'z'}, dimensions={0} | all-to-all | bytes 327680 | tf_op jit(solution)/shard_map/all_to_all | solution.py:513
  43.0 3.1 %collective-permute-start.1 = (bf16[8,80,128]{2,1,0:T(8,128)(2,1)S(1)}, bf16[8,80,128]{2,1,0:T(8,128)(2,1)S(1)}, u32[]{:S(2)}, u32[]{:S(2)}) collective-permute-start(bf16[8,80,128]{2,1,0:T(8,128)(2,1)S(1)} %all_to_all.21.mine_ref), channel_id=1, source_target_pairs={{0,1},{1,0},{2,3},{3,2},{4,5},{5,4},{6,7},{7,6},{8,9},{9,8},{10,11... | collective-permute-start | bytes 491528 | tf_op jit(solution)/shard_map/ppermute | solution.py:509
  46.1 1.0 %collective-permute-done.1.theirs_ref = bf16[8,80,128]{2,1,0:T(8,128)(2,1)S(1)} collective-permute-done((bf16[8,80,128]{2,1,0:T(8,128)(2,1)S(1)}, bf16[8,80,128]{2,1,0:T(8,128)(2,1)S(1)}, u32[]{:S(2)}, u32[]{:S(2)}) %collective-permute-start.1) | collective-permute-done | bytes 163872 | tf_op jit(solution)/shard_map/ppermute | solution.py:509
  47.2 0.0 copy-done.2
  47.2 0.0 copy-done.3
  47.2 9.2 %pencil_blocks.1 = bf16[8,80,128]{2,1,0:T(8,128)(2,1)S(1)} custom-call(s32[1]{0:T(128)} %bitcast.core_ref, bf16[8,80,128]{2,1,0:T(8,128)(2,1)S(1)} %all_to_all.21.mine_ref, bf16[8,80,128]{2,1,0:T(8,128)(2,1)S(1)} %collective-permute-done.1.theirs_ref, bf16[512,256]{1,0:T(8,128)(2,1)S(1)} %bitcast.4, f32[1,256]{1,0:T(1,128)S(1)} %copy-done.3), custom_call_target="tpu_custom_call" | custom-call | tf_op jit(solution)/shard_map/pencil_blocks/pallas_call | solution.py:406
  56.4 11.5 %all_to_all.22.bins_ref = bf16[8,80,128]{2,1,0:T(8,128)(2,1)S(1)} all-to-all(bf16[8,80,128]{2,1,0:T(8,128)(2,1)S(1)} %pencil_blocks.1), channel_id=1, replica_groups=mesh['y'=4,'z'=8,'x'=4,'mode'=2] {'z'}, dimensions={0} | all-to-all | bytes 327680 | tf_op jit(solution)/shard_map/all_to_all | solution.py:513
  67.9 0.3 select_bins.1
  68.2 13.4 %all_to_all.23.recv_ref = bf16[16,144,128]{2,1,0:T(8,128)(2,1)S(1)} all-to-all(bf16[16,144,128]{2,1,0:T(8,128)(2,1)S(1)} %select_bins.1), channel_id=1, replica_groups=mesh['y'=4,'z'=8,'x'=4,'mode'=2] {'y','x'}, dimensions={0} | all-to-all | bytes 1179648 | tf_op jit(solution)/shard_map/all_to_all | solution.py:513
  81.6 0.2 collect.1.mine_ref
  81.8 2.8 %collective-permute-start.2 = (bf16[576,128]{1,0:T(8,128)(2,1)S(1)}, bf16[576,128]{1,0:T(8,128)(2,1)S(1)}, u32[]{:S(2)}, u32[]{:S(2)}) collective-permute-start(bf16[576,128]{1,0:T(8,128)(2,1)S(1)} %collect.1.mine_ref), channel_id=1, source_target_pairs={{0,1},{1,0},{2,3},{3,2},{4,5},{5,4},{6,7},{7,6},{8,9},{9,8},{10,11... | collective-permute-start | bytes 442376 | tf_op jit(solution)/shard_map/ppermute | solution.py:509
  84.6 1.0 %collective-permute-done.2.theirs_ref = bf16[576,128]{1,0:T(8,128)(2,1)S(1)} collective-permute-done((bf16[576,128]{1,0:T(8,128)(2,1)S(1)}, bf16[576,128]{1,0:T(8,128)(2,1)S(1)}, u32[]{:S(2)}, u32[]{:S(2)}) %collective-permute-start.2) | collective-permute-done | bytes 147488 | tf_op jit(solution)/shard_map/ppermute | solution.py:509
  85.6 0.0 copy-done
  85.6 1.6 %strengths.1 = f32[64,128]{1,0:T(8,128)} custom-call(s32[1]{0:T(128)} %bitcast.core_ref, bf16[576,128]{1,0:T(8,128)(2,1)S(1)} %collect.1.mine_ref, bf16[576,128]{1,0:T(8,128)(2,1)S(1)} %collective-permute-done.2.theirs_ref, bf16[64,64,128]{2,1,0:T(8,128)(2,1)S(1)} %copy-done), custom_call_target="tpu_custom_call" | custom-call | tf_op jit(solution)/shard_map/strengths/pallas_call | solution.py:491
Async XLA Ops:
  0.0 47.2 %copy-start.2 = (bf16[1,512,256]{2,1,0:T(8,128)(2,1)S(1)}, bf16[1,512,256]{2,1,0:T(8,128)(2,1)}, u32[]{:S(2)}) copy-start(bf16[1,512,256]{2,1,0:T(8,128)(2,1)} %param.14) | copy-start | bytes 786436
  0.0 47.2 %copy-start.3 = (f32[1,256]{1,0:T(1,128)S(1)}, f32[1,256]{1,0:T(1,128)}, u32[]{:S(2)}) copy-start(f32[1,256]{1,0:T(1,128)} %eigs_ref.1) | copy-start | bytes 3076
  5.2 80.5 %copy-start = (bf16[64,64,128]{2,1,0:T(8,128)(2,1)S(1)}, bf16[64,64,128]{2,1,0:T(8,128)(2,1)}, u32[]{:S(2)}) copy-start(bf16[64,64,128]{2,1,0:T(8,128)(2,1)} %get-tuple-element.20.record_ref) | copy-start | bytes 3145732
  5.2 4.5 %collective-permute-start = (bf16[576,128]{1,0:T(8,128)(2,1)}, bf16[576,128]{1,0:T(8,128)(2,1)S(1)}, u32[]{:S(2)}, u32[]{:S(2)}) collective-permute-start(bf16[576,128]{1,0:T(8,128)(2,1)} %get-tuple-element.17), channel_id=1, source_target_pairs={{0,1},{1,0},{2,3},{3,2},{4,5},{5,4},{6,7},{7,6},{8,9},{9,8},{10,11... | collective-permute-start | bytes 442376 | tf_op jit(solution)/shard_map/ppermute | solution.py:509
  8.5 1.0 %copy-start.1 = (f32[704,128]{1,0:T(8,128)S(1)}, f32[704,128]{1,0:T(8,128)}, u32[]{:S(2)}) copy-start(f32[704,128]{1,0:T(8,128)} %get-tuple-element.13.own_ref) | copy-start | bytes 1081348
  43.0 4.2 %collective-permute-start.1 = (bf16[8,80,128]{2,1,0:T(8,128)(2,1)S(1)}, bf16[8,80,128]{2,1,0:T(8,128)(2,1)S(1)}, u32[]{:S(2)}, u32[]{:S(2)}) collective-permute-start(bf16[8,80,128]{2,1,0:T(8,128)(2,1)S(1)} %all_to_all.21.mine_ref), channel_id=1, source_target_pairs={{0,1},{1,0},{2,3},{3,2},{4,5},{5,4},{6,7},{7,6},{8,9},{9,8},{10,11... | collective-permute-start | bytes 491528 | tf_op jit(solution)/shard_map/ppermute | solution.py:509
  81.8 3.8 %collective-permute-start.2 = (bf16[576,128]{1,0:T(8,128)(2,1)S(1)}, bf16[576,128]{1,0:T(8,128)(2,1)S(1)}, u32[]{:S(2)}, u32[]{:S(2)}) collective-permute-start(bf16[576,128]{1,0:T(8,128)(2,1)S(1)} %collect.1.mine_ref), channel_id=1, source_target_pairs={{0,1},{1,0},{2,3},{3,2},{4,5},{5,4},{6,7},{7,6},{8,9},{9,8},{10,11... | collective-permute-start | bytes 442376 | tf_op jit(solution)/shard_map/ppermute | solution.py:509

commit v9 on v8

--- a/solution.py
+++ b/solution.py
@@ -84,8 +84,10 @@
 
     def copies(step):
         part = pl.ds(step * CB, CB)
+        low, high = pl.ds(step * CB, CB // 2), pl.ds(step * CB + CB // 2, CB // 2)
         return (
-            pltpu.make_async_copy(modes_hbm.at[part], modes_ref.at[part], modes_sem.at[step]),
+            pltpu.make_async_copy(modes_hbm.at[low], modes_ref.at[low], modes_sem.at[2 * step]),
+            pltpu.make_async_copy(modes_hbm.at[high], modes_ref.at[high], modes_sem.at[2 * step + 1]),
             pltpu.make_async_copy(coupling_hbm.at[part], coupling_ref.at[part], coupling_sem.at[step]),
         )
 
@@ -178,7 +180,7 @@
             pltpu.SMEM((NG * NZ,), jnp.int32),
             pltpu.SemaphoreType.DMA((4,)),
             pltpu.SemaphoreType.DMA((STEPS,)),
-            pltpu.SemaphoreType.DMA((STEPS,)),
+            pltpu.SemaphoreType.DMA((2 * STEPS,)),
             pltpu.SemaphoreType.DMA((STEPS,)),
             pltpu.SemaphoreType.DMA((2,)),
         ],

time: 87.5 us -> 87.7 us (level)
  no operation moved by 1% of the time
where the time goes in v9:
time: 87.7 us; the launch traced here: 87.5 us
  blocking collectives  57.5 us (66%)
  Pallas kernels  17.5 us (20%)
  starting transfers between devices  9.27 us (11%)
  waiting for transfers between devices  2.15 us (2%)
  local copies, waits for them, and re-layouts  1 us (1%)
    all_to_all x4, blocking collectives, exchange(): return lax.all_to_all(x, axes, split_axis=0, concat_axis=0, tiled=True)  57.5 us
    ppermute x3, starting transfers between devices, swap(): return lax.ppermute(x, 'mode', [(0, 1), (1, 0)])  9.27 us
    pallas_call x1, Pallas kernels, pencil_blocks(): pl.pallas_call(pencil_kernel, in_specs=[SMEM, VMEM, VMEM, VMEM, VMEM], ou...  9.18 us
    pallas_call x1, Pallas kernels, moments(): pl.pallas_call(moments_kernel, in_specs=[SMEM, hbm, hbm, hbm, hbm, hbm, h...  5.36 us
    ppermute x3, waiting for transfers between devices, swap(): return lax.ppermute(x, 'mode', [(0, 1), (1, 0)])  2.15 us
  transfers between devices with their start and end apart: 3, of which 3 were waited for; matrix products, arithmetic and copies ran while one was open for 0% of the time, Pallas kernels for 0%

profile of v9, /device:TPU:1, one launch (start us, length us, event | category | flops | bytes accessed | tf_op | source)
XLA Modules:
  0.0 87.5 jit_solution(12113057919396195018)
XLA Ops:
  0.0 0.0 copy-start.2
  0.0 0.0 copy-start.3
  0.0 5.4 %child_moments.1 = (bf16[64,64,128]{2,1,0:T(8,128)(2,1)}, f32[704,128]{1,0:T(8,128)}, bf16[576,128]{1,0:T(8,128)(2,1)}) custom-call(s32[1]{0:T(128)} %bitcast.core_ref, s32[2,64]{1,0:T(2,128)} %bitcast.5, s32[64]{0:T(128)} %bitcast.6, s32[64]{0:T(128)} %block_hbm.1, bf16[64,64,128]{2,1,0:T(8,128)(2,1)} %coupling_hbm.1, bf16[64,256,128]{2,1,0:T(8,128)(2,1)} %modes_hbm.1, ...), custom_call_target="tpu_custom_call" | custom-call | tf_op jit(solution)/shard_map/child_moments/pallas_call | solution.py:160
  5.4 0.0 copy-start
  5.4 3.3 %collective-permute-start = (bf16[576,128]{1,0:T(8,128)(2,1)}, bf16[576,128]{1,0:T(8,128)(2,1)S(1)}, u32[]{:S(2)}, u32[]{:S(2)}) collective-permute-start(bf16[576,128]{1,0:T(8,128)(2,1)} %get-tuple-element.17), channel_id=1, source_target_pairs={{0,1},{1,0},{2,3},{3,2},{4,5},{5,4},{6,7},{7,6},{8,9},{9,8},{10,11... | collective-permute-start | bytes 442376 | tf_op jit(solution)/shard_map/ppermute | solution.py:511
  8.7 0.0 copy-start.1
  8.7 1.0 %copy-done.1 = f32[704,128]{1,0:T(8,128)S(1)} copy-done((f32[704,128]{1,0:T(8,128)S(1)}, f32[704,128]{1,0:T(8,128)}, u32[]{:S(2)}) %copy-start.1) | copy-done | bytes 360472
  9.7 0.1 stage.1
  9.8 0.1 collective-permute-done.recv_ref
  9.9 0.3 dispatch.1
  10.2 16.2 %all_to_all.20.recv_ref = bf16[16,144,128]{2,1,0:T(8,128)(2,1)S(1)} all-to-all(bf16[16,144,128]{2,1,0:T(8,128)(2,1)S(1)} %dispatch.1), channel_id=1, replica_groups=mesh['y'=4,'z'=8,'x'=4,'mode'=2] {'y','x'}, dimensions={0} | all-to-all | bytes 1179648 | tf_op jit(solution)/shard_map/all_to_all | solution.py:515
  26.5 0.4 bin_slots.1
  26.8 16.4 %all_to_all.21.mine_ref = bf16[8,80,128]{2,1,0:T(8,128)(2,1)S(1)} all-to-all(bf16[8,80,128]{2,1,0:T(8,128)(2,1)S(1)} %get-tuple-element.18), channel_id=1, replica_groups=mesh['y'=4,'z'=8,'x'=4,'mode'=2] {'z'}, dimensions={0} | all-to-all | bytes 327680 | tf_op jit(solution)/shard_map/all_to_all | solution.py:515
  43.2 3.1 %collective-permute-start.1 = (bf16[8,80,128]{2,1,0:T(8,128)(2,1)S(1)}, bf16[8,80,128]{2,1,0:T(8,128)(2,1)S(1)}, u32[]{:S(2)}, u32[]{:S(2)}) collective-permute-start(bf16[8,80,128]{2,1,0:T(8,128)(2,1)S(1)} %all_to_all.21.mine_ref), channel_id=1, source_target_pairs={{0,1},{1,0},{2,3},{3,2},{4,5},{5,4},{6,7},{7,6},{8,9},{9,8},{10,11... | collective-permute-start | bytes 491528 | tf_op jit(solution)/shard_map/ppermute | solution.py:511
  46.3 1.0 %collective-permute-done.1.theirs_ref = bf16[8,80,128]{2,1,0:T(8,128)(2,1)S(1)} collective-permute-done((bf16[8,80,128]{2,1,0:T(8,128)(2,1)S(1)}, bf16[8,80,128]{2,1,0:T(8,128)(2,1)S(1)}, u32[]{:S(2)}, u32[]{:S(2)}) %collective-permute-start.1) | collective-permute-done | bytes 163872 | tf_op jit(solution)/shard_map/ppermute | solution.py:511
  47.4 0.0 copy-done.2
  47.4 0.0 copy-done.3
  47.4 9.2 %pencil_blocks.1 = bf16[8,80,128]{2,1,0:T(8,128)(2,1)S(1)} custom-call(s32[1]{0:T(128)} %bitcast.core_ref, bf16[8,80,128]{2,1,0:T(8,128)(2,1)S(1)} %all_to_all.21.mine_ref, bf16[8,80,128]{2,1,0:T(8,128)(2,1)S(1)} %collective-permute-done.1.theirs_ref, bf16[512,256]{1,0:T(8,128)(2,1)S(1)} %bitcast.4, f32[1,256]{1,0:T(1,128)S(1)} %copy-done.3), custom_call_target="tpu_custom_call" | custom-call | tf_op jit(solution)/shard_map/pencil_blocks/pallas_call | solution.py:408
  56.6 11.5 %all_to_all.22.bins_ref = bf16[8,80,128]{2,1,0:T(8,128)(2,1)S(1)} all-to-all(bf16[8,80,128]{2,1,0:T(8,128)(2,1)S(1)} %pencil_blocks.1), channel_id=1, replica_groups=mesh['y'=4,'z'=8,'x'=4,'mode'=2] {'z'}, dimensions={0} | all-to-all | bytes 327680 | tf_op jit(solution)/shard_map/all_to_all | solution.py:515
  68.1 0.3 select_bins.1
  68.4 13.4 %all_to_all.23.recv_ref = bf16[16,144,128]{2,1,0:T(8,128)(2,1)S(1)} all-to-all(bf16[16,144,128]{2,1,0:T(8,128)(2,1)S(1)} %select_bins.1), channel_id=1, replica_groups=mesh['y'=4,'z'=8,'x'=4,'mode'=2] {'y','x'}, dimensions={0} | all-to-all | bytes 1179648 | tf_op jit(solution)/shard_map/all_to_all | solution.py:515
  81.8 0.2 collect.1.mine_ref
  82.0 2.8 %collective-permute-start.2 = (bf16[576,128]{1,0:T(8,128)(2,1)S(1)}, bf16[576,128]{1,0:T(8,128)(2,1)S(1)}, u32[]{:S(2)}, u32[]{:S(2)}) collective-permute-start(bf16[576,128]{1,0:T(8,128)(2,1)S(1)} %collect.1.mine_ref), channel_id=1, source_target_pairs={{0,1},{1,0},{2,3},{3,2},{4,5},{5,4},{6,7},{7,6},{8,9},{9,8},{10,11... | collective-permute-start | bytes 442376 | tf_op jit(solution)/shard_map/ppermute | solution.py:511
  84.8 1.0 %collective-permute-done.2.theirs_ref = bf16[576,128]{1,0:T(8,128)(2,1)S(1)} collective-permute-done((bf16[576,128]{1,0:T(8,128)(2,1)S(1)}, bf16[576,128]{1,0:T(8,128)(2,1)S(1)}, u32[]{:S(2)}, u32[]{:S(2)}) %collective-permute-start.2) | collective-permute-done | bytes 147488 | tf_op jit(solution)/shard_map/ppermute | solution.py:511
  85.8 0.0 copy-done
  85.8 1.6 %strengths.1 = f32[64,128]{1,0:T(8,128)} custom-call(s32[1]{0:T(128)} %bitcast.core_ref, bf16[576,128]{1,0:T(8,128)(2,1)S(1)} %collect.1.mine_ref, bf16[576,128]{1,0:T(8,128)(2,1)S(1)} %collective-permute-done.2.theirs_ref, bf16[64,64,128]{2,1,0:T(8,128)(2,1)S(1)} %copy-done), custom_call_target="tpu_custom_call" | custom-call | tf_op jit(solution)/shard_map/strengths/pallas_call | solution.py:493
Async XLA Ops:
  0.0 47.4 %copy-start.2 = (bf16[1,512,256]{2,1,0:T(8,128)(2,1)S(1)}, bf16[1,512,256]{2,1,0:T(8,128)(2,1)}, u32[]{:S(2)}) copy-start(bf16[1,512,256]{2,1,0:T(8,128)(2,1)} %param.14) | copy-start | bytes 786436
  0.0 47.4 %copy-start.3 = (f32[1,256]{1,0:T(1,128)S(1)}, f32[1,256]{1,0:T(1,128)}, u32[]{:S(2)}) copy-start(f32[1,256]{1,0:T(1,128)} %eigs_ref.1) | copy-start | bytes 3076
  5.4 80.5 %copy-start = (bf16[64,64,128]{2,1,0:T(8,128)(2,1)S(1)}, bf16[64,64,128]{2,1,0:T(8,128)(2,1)}, u32[]{:S(2)}) copy-start(bf16[64,64,128]{2,1,0:T(8,128)(2,1)} %get-tuple-element.20.record_ref) | copy-start | bytes 3145732
  5.4 4.6 %collective-permute-start = (bf16[576,128]{1,0:T(8,128)(2,1)}, bf16[576,128]{1,0:T(8,128)(2,1)S(1)}, u32[]{:S(2)}, u32[]{:S(2)}) collective-permute-start(bf16[576,128]{1,0:T(8,128)(2,1)} %get-tuple-element.17), channel_id=1, source_target_pairs={{0,1},{1,0},{2,3},{3,2},{4,5},{5,4},{6,7},{7,6},{8,9},{9,8},{10,11... | collective-permute-start | bytes 442376 | tf_op jit(solution)/shard_map/ppermute | solution.py:511
  8.7 1.0 %copy-start.1 = (f32[704,128]{1,0:T(8,128)S(1)}, f32[704,128]{1,0:T(8,128)}, u32[]{:S(2)}) copy-start(f32[704,128]{1,0:T(8,128)} %get-tuple-element.13.own_ref) | copy-start | bytes 1081348
  43.2 4.2 %collective-permute-start.1 = (bf16[8,80,128]{2,1,0:T(8,128)(2,1)S(1)}, bf16[8,80,128]{2,1,0:T(8,128)(2,1)S(1)}, u32[]{:S(2)}, u32[]{:S(2)}) collective-permute-start(bf16[8,80,128]{2,1,0:T(8,128)(2,1)S(1)} %all_to_all.21.mine_ref), channel_id=1, source_target_pairs={{0,1},{1,0},{2,3},{3,2},{4,5},{5,4},{6,7},{7,6},{8,9},{9,8},{10,11... | collective-permute-start | bytes 491528 | tf_op jit(solution)/shard_map/ppermute | solution.py:511
  82.0 3.8 %collective-permute-start.2 = (bf16[576,128]{1,0:T(8,128)(2,1)S(1)}, bf16[576,128]{1,0:T(8,128)(2,1)S(1)}, u32[]{:S(2)}, u32[]{:S(2)}) collective-permute-start(bf16[576,128]{1,0:T(8,128)(2,1)S(1)} %collect.1.mine_ref), channel_id=1, source_target_pairs={{0,1},{1,0},{2,3},{3,2},{4,5},{5,4},{6,7},{7,6},{8,9},{9,8},{10,11... | collective-permute-start | bytes 442376 | tf_op jit(solution)/shard_map/ppermute | solution.py:511
